TPU v7x, 128 devices: a whole 4x4x4 slice. The times are simulated.
128 devices in a mesh: lat: 8 (over y, core), lon: 16 (over z, x).
Axes of the slice: x: 4, y: 4, z: 4, core: 2. Of those that a mesh axis runs over, the one named last changes fastest.
Arguments:
- ocean_forcing: bfloat16 [4, 1024, 8192], P(None, 'lat', 'lon'), may hold values from -3 to 3
- ice_velocity: float32 [2, 128, 131072], P(None, None, ('lat', 'lon')), may hold values from -3 to 3
- ice_stress: float32 [3, 128, 131072], P(None, None, ('lat', 'lon')), may hold values from -4 to 4
- cat_area: float32 [5, 128, 131072], P(None, None, ('lat', 'lon')), may hold values from 0.15 to 0.198
- cat_thick: float32 [5, 128, 131072], P(None, None, ('lat', 'lon')), may hold values from 0.5 to 3
- run_lengths: int32 [8, 16], replicated, may hold values from 1 to 8, 64 in all within a row
Outputs:
- velocity_out: float32 [2, 128, 131072], P(None, None, ('lat', 'lon'))
- stress_out: float32 [3, 128, 131072], P(None, None, ('lat', 'lon'))
- ocean_stress: bfloat16 [2, 1024, 8192], P(None, 'lat', 'lon')
Inputs may be any that keep to these rules, and one draw needn't show every extreme that they name: `run_lengths`: in every band the 16 run lengths sum to 64, and one of them is 8.
All inputs are finite; a program needn't handle non-finite values.
Results may differ from a plain program's by a relative error of at most 0.001.
Values may be sent and summed in bfloat16 or wider, within the bound.
No kernel may reach another device: no remote copies, remote signals or barrier semaphores. Data moves between devices by JAX's collectives and lax.ppermute only.
A program may use at most 128 MiB of HBM per device.

v0:
```python
import jax
import jax.numpy as jnp
from jax import lax
from jax.sharding import PartitionSpec as P

BS = 128
ITERS = 3


PSTAR = 2.0
CSTAR = 20.0
ECC_SQ = 4.0
DMIN_SQ = 0.01
KAPPA = 0.5
SPEED_SQ = 0.01


def passed_along(block, axis, distance):
    devices = range(lax.axis_size(axis))
    route = [(i - distance, i) for i in devices if i - distance in devices]
    return lax.ppermute(block, axis, route)


def ownership(run_lengths, nlat, nlon, slots, nbb):
    ends = jnp.cumsum(run_lengths, axis=1)
    starts = ends - run_lengths
    slot_range = jnp.arange(slots, dtype=jnp.int32)
    bands = jnp.arange(nlat, dtype=jnp.int32)
    position = starts[:, :, None] + slot_range[None, None, :]
    valid = slot_range[None, None, :] < run_lengths[:, :, None]
    column = jnp.where((bands % 2 == 0)[:, None, None], position, nbb - 1 - position)
    slot_col = jnp.where(valid, column, -1)
    columns = jnp.arange(nbb, dtype=jnp.int32)
    curve = jnp.where((bands % 2 == 0)[:, None], columns[None, :], nbb - 1 - columns[None, :])
    owner = jnp.sum((ends[:, None, :] <= curve[:, :, None]).astype(jnp.int32), axis=2)
    first = jnp.take_along_axis(starts, owner, axis=1)
    grid_slot = (bands[:, None] * nlon + owner) * slots + curve - first
    return (slot_col, grid_slot)


def pick_columns(carry, piece, wanted):
    width = piece.shape[2]
    inside = (wanted >= 0) & (wanted < width)
    taken = jnp.take(piece, jnp.clip(wanted, 0, width - 1), axis=2)
    return jnp.where(inside[None, None, :], taken, carry)


def update_stress(
    zonal, merid, zonal_east, merid_east, zonal_north, merid_north, stresses, strength
):
    first_inv, second_inv, shear_stress = stresses
    strain_xx = zonal_east - zonal
    strain_yy = merid_north - merid
    strain_xy = 0.5 * (zonal_north - zonal + merid_east - merid)
    divergence = strain_xx + strain_yy
    tension = strain_xx - strain_yy
    shearing = 2.0 * strain_xy
    deformation = jnp.sqrt(
        divergence * divergence + (tension * tension + shearing * shearing) / ECC_SQ + DMIN_SQ
    )
    viscous = strength / deformation
    first_inv = (first_inv + KAPPA * (viscous * divergence - strength)) / (1.0 + KAPPA)
    second_inv = (second_inv + KAPPA * viscous * tension / ECC_SQ) / (1.0 + KAPPA)
    shear_stress = (shear_stress + KAPPA * viscous * shearing / (2.0 * ECC_SQ)) / (1.0 + KAPPA)
    return (first_inv, second_inv, shear_stress)


def update_velocity(
    zonal, merid, stresses, west_stresses, south_stresses, mass, concentration, coriolis, forcing
):
    first_inv, second_inv, shear_stress = stresses
    normal_xx = 0.5 * (first_inv + second_inv)
    normal_yy = 0.5 * (first_inv - second_inv)
    west_xx = 0.5 * (west_stresses[0] + west_stresses[1])
    south_yy = 0.5 * (south_stresses[0] - south_stresses[1])
    force_x = normal_xx - west_xx + shear_stress - south_stresses[2]
    force_y = shear_stress - west_stresses[2] + normal_yy - south_yy
    cur_x, cur_y, wind_x, wind_y = (forcing[0], forcing[1], forcing[2], forcing[3])
    drag = concentration * jnp.sqrt((cur_x - zonal) ** 2 + (cur_y - merid) ** 2 + SPEED_SQ)
    diagonal = mass + drag
    turning = coriolis * mass
    rhs_x = mass * zonal + force_x + wind_x + drag * cur_x
    rhs_y = mass * merid + force_y + wind_y + drag * cur_y
    denominator = diagonal * diagonal + turning * turning
    return (
        (diagonal * rhs_x + turning * rhs_y) / denominator,
        (diagonal * rhs_y - turning * rhs_x) / denominator,
    )


def surface_stress(zonal, merid, concentration, forcing):
    cur_x, cur_y, wind_x, wind_y = (forcing[0], forcing[1], forcing[2], forcing[3])
    drag = concentration * jnp.sqrt((cur_x - zonal) ** 2 + (cur_y - merid) ** 2 + SPEED_SQ)
    return jnp.stack(
        [
            (1.0 - concentration) * wind_x + drag * (zonal - cur_x),
            (1.0 - concentration) * wind_y + drag * (merid - cur_y),
        ]
    )


def neighbour_edges(columns_out, rows_out, tables, layout, forward):
    slot_col, grid_slot = tables
    band_idx, lon_idx, nlat, nlon, slots, nbb = layout
    my_cols = jnp.maximum(slot_col[band_idx, lon_idx], 0)
    direction = 1 if forward else -1
    side_cols = (my_cols + direction) % nbb
    beside = jnp.take(grid_slot[band_idx], side_cols, axis=0)
    other_band = band_idx + direction
    clipped = jnp.clip(other_band, 0, nlat - 1)
    across = jnp.take(grid_slot[clipped], my_cols, axis=0)
    if forward:
        moved = passed_along(rows_out, "lat", -1)
    else:
        moved = passed_along(rows_out, "lat", 1)
    payload = jnp.stack([columns_out, moved], axis=1)
    if forward:
        gathered = lax.all_gather(payload, "lon", axis=0, tiled=True)
    else:
        gathered = lax.all_gather(payload, "lon", axis=0, tiled=True)
    col_edges = jnp.take(gathered[:, 0], beside - band_idx * nlon * slots, axis=0)
    row_edges = jnp.take(gathered[:, 1], across - clipped * nlon * slots, axis=0)
    return (col_edges, row_edges)


def body(ocean_forcing, ice_velocity, ice_stress, cat_area, cat_thick, run_lengths):
    nlat = lax.axis_size("lat")
    nlon = lax.axis_size("lon")
    band_idx = lax.axis_index("lat")
    lon_idx = lax.axis_index("lon")
    slots = ice_velocity.shape[2] // BS
    tile_width = ocean_forcing.shape[2]
    tile_blocks = tile_width // BS
    nbb = nlon * tile_blocks
    tables = ownership(run_lengths, nlat, nlon, slots, nbb)
    slot_col, grid_slot = tables
    layout = (band_idx, lon_idx, nlat, nlon, slots, nbb)
    mine = slot_col[band_idx, lon_idx]
    valid = mine >= 0
    my_cols = jnp.maximum(mine, 0)
    cell_range = jnp.arange(BS, dtype=jnp.int32)
    band_grid = grid_slot[band_idx]
    wanted = jnp.where(valid[:, None], my_cols[:, None] * BS + cell_range[None, :], -1).reshape(-1)
    initial = jnp.zeros((4, BS, slots * BS), jnp.bfloat16)
    forcing = pick_columns(
        initial, lax.all_gather(ocean_forcing, "lon", axis=2, tiled=True), wanted
    )
    forcing = forcing.astype(jnp.float32).reshape(4, BS, slots, BS)
    area = cat_area.reshape(cat_area.shape[0], BS, slots, BS)
    thick = cat_thick.reshape(cat_thick.shape[0], BS, slots, BS)
    concentration = jnp.sum(area, axis=0)
    mass = jnp.sum(area * thick, axis=0)
    strength = PSTAR * mass * jnp.exp(-CSTAR * (1.0 - concentration))
    rows = (band_idx * BS + cell_range).astype(jnp.float32)
    latitude = -78.0 + 168.0 * (rows + 0.5) / (BS * nlat)
    coriolis = jnp.sin(latitude * (jnp.pi / 180.0))[:, None, None]
    velocity = ice_velocity.reshape(2, BS, slots, BS)
    stress = ice_stress.reshape(3, BS, slots, BS)
    zonal, merid = (velocity[0], velocity[1])
    stresses = (stress[0], stress[1], stress[2])
    for subcycle in range(ITERS):
        speeds = jnp.stack([zonal, merid])
        west_cols = speeds[:, :, :, 0].transpose(2, 0, 1)
        south_rows = speeds[:, 0, :, :].transpose(1, 0, 2)
        col_edges, row_edges = neighbour_edges(west_cols, south_rows, tables, layout, True)
        east_side = jnp.concatenate(
            [speeds[..., 1:], col_edges.transpose(1, 2, 0)[..., None]], axis=3
        )
        north_side = jnp.concatenate([speeds[:, 1:], row_edges.transpose(1, 0, 2)[:, None]], axis=1)
        stresses = update_stress(
            zonal,
            merid,
            east_side[0],
            east_side[1],
            north_side[0],
            north_side[1],
            stresses,
            strength,
        )
        stacked = jnp.stack(stresses)
        east_cols = stacked[:, :, :, BS - 1].transpose(2, 0, 1)
        north_rows = stacked[:, BS - 1, :, :].transpose(1, 0, 2)
        col_edges, row_edges = neighbour_edges(east_cols, north_rows, tables, layout, False)
        west_side = jnp.concatenate(
            [col_edges.transpose(1, 2, 0)[..., None], stacked[..., :-1]], axis=3
        )
        south_side = jnp.concatenate(
            [row_edges.transpose(1, 0, 2)[:, None], stacked[:, :-1]], axis=1
        )
        zonal, merid = update_velocity(
            zonal,
            merid,
            stresses,
            (west_side[0], west_side[1], west_side[2]),
            (south_side[0], south_side[1], south_side[2]),
            mass,
            concentration,
            coriolis,
            forcing,
        )
    keep = valid[None, None, :, None]
    velocity_out = jnp.where(keep, jnp.stack([zonal, merid]), jnp.float32(0.0)).reshape(
        2, BS, slots * BS
    )
    stress_out = jnp.where(keep, jnp.stack(stresses), jnp.float32(0.0)).reshape(3, BS, slots * BS)
    handed = surface_stress(zonal, merid, concentration, forcing).astype(jnp.bfloat16)
    handed_flat = handed.reshape(2, BS, slots * BS)
    ocean_cols = lon_idx * tile_width + jnp.arange(tile_width, dtype=jnp.int32)
    band_slot = jnp.take(band_grid, ocean_cols // BS, axis=0) - band_idx * nlon * slots
    wanted_back = band_slot * BS + ocean_cols % BS
    empty = jnp.zeros((2, BS, tile_width), jnp.bfloat16)
    ocean_stress = pick_columns(
        empty, lax.all_gather(handed_flat, "lon", axis=2, tiled=True), wanted_back
    )
    return (velocity_out, stress_out, ocean_stress)


def solution(mesh):
    in_specs = (
        P(None, "lat", "lon"),
        P(None, None, ("lat", "lon")),
        P(None, None, ("lat", "lon")),
        P(None, None, ("lat", "lon")),
        P(None, None, ("lat", "lon")),
        P(),
    )
    out_specs = (
        P(None, None, ("lat", "lon")),
        P(None, None, ("lat", "lon")),
        P(None, "lat", "lon"),
    )
    return jax.shard_map(body, mesh=mesh, in_specs=in_specs, out_specs=out_specs, check_vma=False)
```

profile of v0, /device:TPU:8, one launch (start us, length us, event | category | flops | bytes accessed | tf_op | source)
XLA Modules:
  0.0 361.0 jit_solution(15358898396834507126)
XLA Ops:
  7.2 2.2 copy.252
  9.9 1.9 collective-permute-start
  14.0 2.6 gather_fusion.2
  16.8 2.0 compare_select_fusion.19
  21.7 2.9 slice_bitcast_fusion.1
  24.6 3.4 fusion.118
  28.1 1.0 slice.497
  29.8 2.1 copy.322
  31.9 1.2 copy.319
  35.1 26.6 %all_gather.25 = f32[128,2,2,128]{3,0,2,1:T(8,128)S(1)} all-gather(f32[8,2,2,128]{3,0,2,1:T(8,128)S(1)} %pad_maximum_fusion.19), channel_id=1, replica_groups=mesh['lat'=8,'lon'=16] {'lon'}, dimensions={0}, use_global_device_ids=true | all-gather | bytes 278528 | tf_op jit(solution)/shard_map/all_gather | solution.py:118
  62.6 1.3 copy.258
  64.6 2.5 fusion.70
  67.9 1.9 collective-permute-start.1
  70.0 1.4 slice.509
  71.3 1.6 slice.501
  72.9 1.9 copy.313
  74.8 24.6 %all_gather.26 = f32[128,2,3,128]{3,0,2,1:T(8,128)S(1)} all-gather(f32[8,2,3,128]{3,0,2,1:T(8,128)S(1)} %pad_maximum_fusion.16), channel_id=1, replica_groups=mesh['lat'=8,'lon'=16] {'lon'}, dimensions={0}, use_global_device_ids=true | all-gather | bytes 417792 | tf_op jit(solution)/shard_map/all_gather | solution.py:120
  100.4 1.7 copy.264
  102.8 6.9 %gather_fusion = bf16[1024,4,128]{2,1,0:T(4,128)(2,1)S(1)} fusion(bf16[4,128,8192]{1,0,2:T(4,128)(2,1)} %all-gather.3.cloned.1.call-done, s32[1024]{0:T(1024)S(1)} %broadcast_clamp_fusion), kind=kCustom, calls=%fused_computation.16 | custom fusion | bytes 2101248 | tf_op jit(solution)/shard_map/jit(_take)/gather | solution.py:44
  109.7 4.8 %convert_bitcast_fusion = f32[4,128,1024]{1,0,2:T(4,128)S(1)} fusion(bf16[1024,4,128]{2,1,0:T(4,128)(2,1)S(1)} %gather_fusion, pred[1024]{0:T(1024)(128)(4,1)S(1)} %get-tuple-element.94, pred[1024]{0:T(1024)(128)(4,1)S(1)} %get-tuple-element.93), kind=kLoop, calls=%fused_computation.26 | loop fusion | flops 1572864 | bytes 3147776 | tf_op jit(solution)/shard_map/convert_element_type | solution.py:148
  114.5 2.3 fusion.132
  117.1 1.0 copy.303
  118.1 1.3 copy.298
  119.4 1.0 copy.304
  120.4 4.0 %add_divide_fusion.2 = (f32[1,128,8,128]{3,2,1,0:T(8,128)S(1)}, f32[1,128,8,128]{3,2,1,0:T(8,128)S(1)}, f32[1,128,8,128]{3,2,1,0:T(8,128)S(1)}, f32[1,128,8,128]{3,2,1,0:T(8,128)S(1)}) fusion(f32[128]{0:T(128)S(1)} %multiply_sine_fusion, f32[1,128,8,128]{3,2,1,0:T(8,128)S(1)} %copy.298, f32[1,128,8,128]{3,2,1,0:T(8,128)} %copy.304, ...), kind=kLoop, calls=%fused_computation.218 | loop fusion | flops 6029312 | bytes 11010560 | tf_op jit(solution)/shard_map/div | solution.py:86
  124.6 1.0 fusion.3
  125.6 1.9 collective-permute-start.2
  127.6 1.3 fusion.2
  128.9 1.6 copy.314
  130.5 21.4 %all_gather.27 = f32[128,2,2,128]{3,0,2,1:T(8,128)S(1)} all-gather(f32[8,2,2,128]{3,0,2,1:T(8,128)S(1)} %pad_maximum_fusion.20), channel_id=1, replica_groups=mesh['lat'=8,'lon'=16] {'lon'}, dimensions={0}, use_global_device_ids=true | all-gather | bytes 278528 | tf_op jit(solution)/shard_map/all_gather | solution.py:118
  152.6 1.0 fusion.5
  154.4 1.3 copy.272
  155.8 2.7 add_multiply_fusion.5
  159.0 1.9 collective-permute-start.3
  161.1 1.3 slice.536
  162.7 1.6 slice.528
  164.3 1.9 copy.315
  166.2 24.0 %all_gather.28 = f32[128,2,3,128]{3,0,2,1:T(8,128)S(1)} all-gather(f32[8,2,3,128]{3,0,2,1:T(8,128)S(1)} %pad_maximum_fusion.17), channel_id=1, replica_groups=mesh['lat'=8,'lon'=16] {'lon'}, dimensions={0}, use_global_device_ids=true | all-gather | bytes 417792 | tf_op jit(solution)/shard_map/all_gather | solution.py:120
  191.8 1.7 copy.278
  193.5 4.0 %add_divide_fusion.1 = (f32[1,128,8,128]{3,2,1,0:T(8,128)S(1)}, f32[1,128,8,128]{3,2,1,0:T(8,128)S(1)}, f32[1,128,8,128]{3,2,1,0:T(8,128)S(1)}, f32[1,128,8,128]{3,2,1,0:T(8,128)S(1)}) fusion(f32[128]{0:T(128)S(1)} %multiply_sine_fusion, f32[1,128,8,128]{3,2,1,0:T(8,128)S(1)} %copy.298, f32[1,128,8,128]{3,2,1,0:T(8,128)} %copy.304, ...), kind=kLoop, calls=%fused_computation.211 | loop fusion | flops 6029312 | bytes 11010560 | tf_op jit(solution)/shard_map/div | solution.py:86
  197.8 2.1 collective-permute-start.4
  200.0 1.3 fusion
  201.7 21.4 %all_gather.29 = f32[128,2,2,128]{3,0,2,1:T(8,128)S(1)} all-gather(f32[8,2,2,128]{3,0,2,1:T(8,128)S(1)} %pad_maximum_fusion.21), channel_id=1, replica_groups=mesh['lat'=8,'lon'=16] {'lon'}, dimensions={0}, use_global_device_ids=true | all-gather | bytes 278528 | tf_op jit(solution)/shard_map/all_gather | solution.py:118
  223.8 1.0 fusion.4
  225.6 1.3 copy.284
  227.0 2.6 add_multiply_fusion.2
  230.1 1.9 collective-permute-start.5
  232.1 1.3 slice.561
  233.4 1.6 slice.553
  235.0 1.9 copy.317
  236.9 24.5 %all_gather.30 = f32[128,2,3,128]{3,0,2,1:T(8,128)S(1)} all-gather(f32[8,2,3,128]{3,0,2,1:T(8,128)S(1)} %pad_maximum_fusion.18), channel_id=1, replica_groups=mesh['lat'=8,'lon'=16] {'lon'}, dimensions={0}, use_global_device_ids=true | all-gather | bytes 417792 | tf_op jit(solution)/shard_map/all_gather | solution.py:120
  262.2 1.5 gather_fusion.18
  264.7 1.5 gather_fusion.17
  266.3 1.7 copy.290
  268.0 3.2 fusion.50
  272.4 1.1 add_convert_fusion.1
  275.5 1.4 copy.295
  278.8 4.4 %compare_select_fusion.6 = s32[512,1]{0,1:T(1,128)S(1)} fusion(s32[]{:T(128)} %bitcast.144, s32[]{:T(128)} %bitcast.145, s32[]{:T(128)} %bitcast.146, s32[]{:T(128)} %bitcast.147, s32[]{:T(128)} %bitcast.148, s32[]{:T(128)} %bitcast.150, s32[]{:T(128)} %bitcast.149, s32[]{:T(128)S(6)} %mul.1276), kind=kLoop, calls=%fused_computation.336 | loop fusion | flops 15872 | bytes 2080 | tf_op jit(solution)/shard_map/jit(_take)/gather | solution.py:209
  285.3 35.8 %compare_and_fusion.6 = (pred[512]{0:T(512)(128)(4,1)S(1)}, s32[512]{0:T(512)S(1)}, s32[512]{0:T(512)S(1)}) fusion(s32[]{:T(128)S(6)} %mul.1204, s32[]{:T(128)S(6)} %mul.1276, pred[512]{0:T(512)(128)(4,1)S(1)} %get-tuple-element.166, pred[512]{0:T(512)(128)(4,1)S(1)} %get-tuple-element.167, pred[512]{0:T(512)(128)(4,1)S(1)} %get-tuple-element.168, ...), kind=kLoop, calls=%fused_computation.405 | loop fusion | flops 46080 | bytes 36076 | tf_op jit(solution)/shard_map/and | solution.py:43
  321.6 1.3 maximum_select_fusion
  323.3 1.1 maximum_select_fusion.1
  324.3 21.8 %all-gather.5.cloned.1.call-done = bf16[2,128,16384]{1,0,2:T(2,128)(2,1)} async-done(((bf16[2,128,1024]{1,0,2:T(2,128)(2,1)}), bf16[2,128,16384]{1,0,2:T(2,128)(2,1)}) %all-gather.5.cloned.1.call-update) | async-done | bytes 8388624 | tf_op jit(solution)/shard_map/all_gather | solution.py:213
  346.2 4.7 %gather_fusion.1 = bf16[512,2,128]{2,1,0:T(2,128)(2,1)S(1)} fusion(bf16[2,128,16384]{1,0,2:T(2,128)(2,1)} %all-gather.5.cloned.1.call-done, s32[1024]{0:T(1024)S(1)} %pad_clamp_fusion), kind=kCustom, calls=%fused_computation.17 | custom fusion | bytes 526336 | tf_op jit(solution)/shard_map/jit(_take)/gather | solution.py:44
  350.9 2.3 fusion.89
  (270 shorter events, 30.2 us)
Async XLA Ops:
  7.2 2.3 copy-start.50
  7.2 95.6 %all-gather.3.cloned.1.call-start = ((), (), s32[]{:S(2)}) async-start(), calls=%async_computation | async-start | bytes 8912896 | tf_op jit(solution)/shard_map/all_gather | solution.py:146
  9.4 336.8 %all-gather.5.cloned.1.call-start = ((), (), s32[]{:S(2)}) async-start(), calls=%async_computation.1 | async-start | bytes 8912896 | tf_op jit(solution)/shard_map/all_gather | solution.py:213
  9.7 54.9 %copy-start.36 = (f32[16,8,8,128]{3,2,1,0:T(8,128)}, f32[16,8,8,128]{3,2,1,0:T(8,128)S(1)}, u32[]{:S(2)}) copy-start(f32[16,8,8,128]{3,2,1,0:T(8,128)S(1)} %copy.320) | copy-start | bytes 1572868
  9.7 2.2 copy-start.51
  9.8 54.8 %copy-start.37 = (f32[16,8,8,128]{3,2,1,0:T(8,128)}, f32[16,8,8,128]{3,2,1,0:T(8,128)S(1)}, u32[]{:S(2)}) copy-start(f32[16,8,8,128]{3,2,1,0:T(8,128)S(1)} %copy.321) | copy-start | bytes 1572868
  9.9 25.2 %collective-permute-start = (f32[8,2,128]{2,0,1:T(8,128)S(1)}, f32[8,2,128]{2,0,1:T(8,128)S(1)}, u32[]{:S(2)}, u32[]{:S(2)}) collective-permute-start(f32[8,2,128]{2,0,1:T(8,128)S(1)} %slice_bitcast_fusion.17), channel_id=1, source_target_pairs={{16,0},{32,16},{48,32},{64,48},{80,64},{96,80},{112,96},{17,1},{33... | collective-permute-start | bytes 24584 | tf_op jit(solution)/shard_map/ppermute | solution.py:21
  21.7 2.9 copy-start.44
  29.8 3.3 copy-start.45
  29.8 3.4 copy-start.47
  31.9 2.2 copy-start.46
  33.1 160.3 %copy-start = (f32[16,8,8,128]{3,2,1,0:T(8,128)}, f32[16,8,8,128]{3,2,1,0:T(8,128)S(1)}, u32[]{:S(2)}) copy-start(f32[16,8,8,128]{3,2,1,0:T(8,128)S(1)} %copy.319) | copy-start | bytes 1572868
  64.6 2.5 copy-start.48
  64.6 2.5 copy-start.49
  67.1 0.8 copy-start.12
  67.1 2.7 copy-start.26
  67.9 2.0 copy-start.28
  67.9 2.1 copy-start.30
  67.9 6.9 %collective-permute-start.1 = (f32[8,3,128]{2,0,1:T(8,128)S(1)}, f32[8,3,128]{2,0,1:T(8,128)S(1)}, u32[]{:S(2)}, u32[]{:S(2)}) collective-permute-start(f32[8,3,128]{2,0,1:T(8,128)S(1)} %maximum_bitcast_fusion.2), channel_id=1, source_target_pairs={{0,16},{16,32},{32,48},{48,64},{64,80},{80,96},{96,112},{1,17},{17... | collective-permute-start | bytes 36872 | tf_op jit(solution)/shard_map/ppermute | solution.py:21
  69.9 3.0 copy-start.2
  117.0 3.3 copy-start.15
  117.0 3.3 copy-start.27
  119.3 74.1 %copy-start.4 = (f32[1,128,8,128]{3,2,1,0:T(8,128)}, f32[1,128,8,128]{3,2,1,0:T(8,128)S(1)}, u32[]{:S(2)}) copy-start(f32[1,128,8,128]{3,2,1,0:T(8,128)S(1)} %copy.298) | copy-start | bytes 1572868
  125.6 4.8 %collective-permute-start.2 = (f32[8,2,128]{2,0,1:T(8,128)S(1)}, f32[8,2,128]{2,0,1:T(8,128)S(1)}, u32[]{:S(2)}, u32[]{:S(2)}) collective-permute-start(f32[8,2,128]{2,0,1:T(8,128)S(1)} %fusion.98), channel_id=1, source_target_pairs={{16,0},{32,16},{48,32},{64,48},{80,64},{96,80},{112,96},{17,1},{33... | collective-permute-start | bytes 24584 | tf_op jit(solution)/shard_map/ppermute | solution.py:21
  152.6 3.1 copy-start.13
  155.8 2.8 copy-start.29
  155.8 2.8 copy-start.31
  155.8 2.8 copy-start.39
  158.5 2.4 copy-start.32
  158.9 2.1 copy-start.22
  159.0 2.1 copy-start.24
  159.0 7.2 %collective-permute-start.3 = (f32[8,3,128]{2,0,1:T(8,128)S(1)}, f32[8,3,128]{2,0,1:T(8,128)S(1)}, u32[]{:S(2)}, u32[]{:S(2)}) collective-permute-start(f32[8,3,128]{2,0,1:T(8,128)S(1)} %maximum_bitcast_fusion.1), channel_id=1, source_target_pairs={{0,16},{16,32},{32,48},{48,64},{64,80},{80,96},{96,112},{1,17},{17... | collective-permute-start | bytes 36872 | tf_op jit(solution)/shard_map/ppermute | solution.py:21
  161.0 1.6 copy-start.3
  197.8 3.8 %collective-permute-start.4 = (f32[8,2,128]{2,0,1:T(8,128)S(1)}, f32[8,2,128]{2,0,1:T(8,128)S(1)}, u32[]{:S(2)}, u32[]{:S(2)}) collective-permute-start(f32[8,2,128]{2,0,1:T(8,128)S(1)} %fusion.99), channel_id=1, source_target_pairs={{16,0},{32,16},{48,32},{64,48},{80,64},{96,80},{112,96},{17,1},{33... | collective-permute-start | bytes 24584 | tf_op jit(solution)/shard_map/ppermute | solution.py:21
  223.8 3.1 copy-start.14
  223.8 3.2 copy-start.33
  227.0 2.6 copy-start.23
  227.0 2.6 copy-start.25
  227.0 2.6 copy-start.38
  229.6 2.4 copy-start.17
  230.0 2.1 copy-start.6
  230.0 2.1 copy-start.9
  230.1 6.8 %collective-permute-start.5 = (f32[8,3,128]{2,0,1:T(8,128)S(1)}, f32[8,3,128]{2,0,1:T(8,128)S(1)}, u32[]{:S(2)}, u32[]{:S(2)}) collective-permute-start(f32[8,3,128]{2,0,1:T(8,128)S(1)} %maximum_bitcast_fusion), channel_id=1, source_target_pairs={{0,16},{16,32},{32,48},{48,64},{64,80},{80,96},{96,112},{1,17},{17... | collective-permute-start | bytes 36872 | tf_op jit(solution)/shard_map/ppermute | solution.py:21
  267.9 3.3 copy-start.1
  267.9 3.3 copy-start.5
  267.9 3.3 copy-start.7
  267.9 3.3 copy-start.10
  267.9 3.3 copy-start.16
  267.9 3.4 copy-start.18
  268.0 3.9 %copy-start.20 = (f32[3,128,8,1]{3,2,1,0:T(8,128)S(1)}, f32[3,128,8,1]{3,2,1,0:T(8,128)}, u32[]{:S(2)}) copy-start(f32[3,128,8,1]{3,2,1,0:T(8,128)} %copy.290) | copy-start | bytes 36868
  268.0 4.4 %copy-start.21 = (f32[3,127,8,128]{3,2,1,0:T(8,128)S(1)}, f32[3,127,8,128]{3,2,1,0:T(8,128)}, u32[]{:S(2)}) copy-start(f32[3,127,8,128]{3,2,1,0:T(8,128)} %slice.561) | copy-start | bytes 4681732
  268.0 4.4 %copy-start.35 = (f32[1,128,8,128]{3,2,1,0:T(8,128)S(1)}, f32[1,128,8,128]{3,2,1,0:T(8,128)}, u32[]{:S(2)}) copy-start(f32[1,128,8,128]{3,2,1,0:T(8,128)} %copy.303) | copy-start | bytes 1572868
  272.4 2.1 copy-start.34
  273.6 0.8 copy-start.40
  273.6 1.0 copy-start.42
  275.4 45.8 %copy-start.11 = (f32[1,128,8,128]{3,2,1,0:T(8,128)S(1)}, f32[1,128,8,128]{3,2,1,0:T(8,128)}, u32[]{:S(2)}) copy-start(f32[1,128,8,128]{3,2,1,0:T(8,128)} %copy-done.9) | copy-start | bytes 1572868
  275.5 45.9 %copy-start.8 = (f32[1,128,8,128]{3,2,1,0:T(8,128)S(1)}, f32[1,128,8,128]{3,2,1,0:T(8,128)}, u32[]{:S(2)}) copy-start(f32[1,128,8,128]{3,2,1,0:T(8,128)} %copy-done.6) | copy-start | bytes 1572868
  276.9 44.6 %copy-start.19 = (f32[1,128,8,128]{3,2,1,0:T(8,128)S(1)}, f32[1,128,8,128]{3,2,1,0:T(8,128)}, u32[]{:S(2)}) copy-start(f32[1,128,8,128]{3,2,1,0:T(8,128)} %copy-done.17) | copy-start | bytes 1572868
  321.5 1.3 copy-start.43
  321.5 1.7 copy-start.41
Sparse Core Ops, SparseCore 0:
  10.1 75.2 all-gather.2
  277.0 69.1 all-gather.4
where the time goes:
time: 363 us; the launch traced here: 361 us
  blocking collectives  142 us (39%)
  other arithmetic  86.1 us (24%)
  local copies, waits for them, and re-layouts  83.5 us (23%)
  waiting for transfers between devices  21.9 us (6%)
  between operations  15.3 us (4%)
  starting transfers between devices  11.8 us (3%)
    all_gather x6, blocking collectives, neighbour_edges(): gathered = lax.all_gather(payload, 'lon', axis=0, tiled=True)  142 us
    and x1, other arithmetic, pick_columns(): inside = (wanted >= 0) & (wanted < width)  35.8 us
    unnamed x121, local copies, waits for them, and re-layouts  22.3 us
    all_gather x1, waiting for transfers between devices, body(): lax.all_gather(handed_flat, 'lon', axis=2, tiled=True)  21.8 us
    ppermute x6, starting transfers between devices, passed_along(): return lax.ppermute(block, axis, route)  11.7 us
    gather x2, local copies, waits for them, and re-layouts, pick_columns(): taken = jnp.take(piece, jnp.clip(wanted, 0, width - 1), axis=2)  11.7 us
    broadcast_in_dim x6, local copies, waits for them, and re-layouts, body(): col_edges.transpose(1, 2, 0)[..., None]  9.04 us
    div x2, other arithmetic, update_velocity(): (diagonal * rhs_x + turning * rhs_y) / denominator  7.94 us
  transfers between devices with their start and end apart: 8, of which 1 were waited for; matrix products, arithmetic and copies ran while one was open for 27% of the time, Pallas kernels for 0%

commit v1 on v0

v1 whole, which is shorter than its diff:
```python
import functools

import jax
import jax.numpy as jnp
from jax import lax
from jax.experimental import pallas as pl
from jax.experimental.pallas import tpu as pltpu
from jax.sharding import PartitionSpec as P

BS = 128
ITERS = 3
NLAT = 8
NLON = 16
SLOTS = 8
NBB = 64
TILE = 4
DEEP = 3
PSTAR = 2.0
CSTAR = 20.0
DMIN_SQ = 0.01
SPEED_SQ = 0.01
ICE = 7
U, V, S1, S2, S12, AREA, MASS, STR, UO, VO, TX, TY = range(12)
STRIP = (SLOTS + 1) * BS
TOP = 8
ROWS = BS + 2 * TOP
SEND_ROWS = 32
M1_ROWS = TILE * 32 + SLOTS * 8
M2_ROWS = (SLOTS + 1) * 32 + 80
M3_ROWS = SLOTS * 16
M4_ROWS = TILE * 16
F32 = jnp.float32
BF16 = jnp.bfloat16


def lanes_of(shape):
    return lax.broadcasted_iota(jnp.int32, shape, len(shape) - 1)


def ice_fields(vel, stress, area, thick):
    conc = area[0] + area[1] + area[2] + area[3] + area[4]
    mass = area[0] * thick[0]
    for n in range(1, 5):
        mass = mass + area[n] * thick[n]
    return [vel[0], vel[1], stress[0], stress[1], stress[2], conc, mass]


def strength_of(conc, mass):
    return (PSTAR / 3.0) * mass * jnp.exp(-CSTAR * (1.0 - conc))


def edges_kernel(lens, place, *refs):
    ice = [refs[4 * i : 4 * i + 4] for i in range(4)]
    f_low, f_high, south, north, prev, nxt = refs[16:]
    odd = lax.rem(place[0], 2) == 1
    for out, which, force, row0, frow0 in (
        (south, 0, f_low, 0, 0),
        (north, 1, f_high, 5, 14),
    ):
        arrays = [ice[i][which] for i in range(4)]
        fields = ice_fields(*[[a[n] for n in range(a.shape[0])] for a in arrays])
        out[...] = jnp.zeros(out.shape, F32)
        for f in range(ICE):
            out[3 * f : 3 * f + 3, :] = fields[f][row0 : row0 + 3, :]
        for f in range(4):
            rows = force[f].astype(F32)
            out[21 + f : 22 + f, 0:512] = rows[frow0 : frow0 + 1, :]
            out[21 + f : 22 + f, 512:1024] = rows[frow0 + 1 : frow0 + 2, :]
    lane = lanes_of((BS, BS))
    for out, which, col_even, col_odd in ((prev, 2, 0, 125), (nxt, 3, 125, 0)):
        arrays = [ice[i][which] for i in range(4)]
        fields = ice_fields(*[[a[n] for n in range(a.shape[0])] for a in arrays])
        packed = jnp.zeros((BS, BS), F32)
        for f in range(ICE):
            shift = jnp.where(odd, (3 * f - col_odd) % BS, (3 * f - col_even) % BS)
            moved = pltpu.roll(fields[f], shift, 1)
            packed = jnp.where((lane >= 3 * f) & (lane < 3 * f + 3), moved, packed)
        out[...] = packed


def make_edges(lens, place, vel, stress, area, thick, forcing):
    width = SLOTS * BS

    def specs(n):
        return [
            pl.BlockSpec((n, 8, width), lambda i, lens, place: (0, 0, 0)),
            pl.BlockSpec((n, 8, width), lambda i, lens, place: (0, BS // 8 - 1, 0)),
            pl.BlockSpec((n, BS, BS), lambda i, lens, place: (0, 0, 0)),
            pl.BlockSpec(
                (n, BS, BS),
                lambda i, lens, place: (0, 0, lens[place[0] * NLON + place[1]] - 1),
            ),
        ]

    in_specs = specs(2) + specs(3) + specs(5) + specs(5)
    in_specs += [
        pl.BlockSpec((4, 16, 512), lambda i, lens, place: (0, 0, 0)),
        pl.BlockSpec((4, 16, 512), lambda i, lens, place: (0, BS // 16 - 1, 0)),
    ]
    whole = lambda i, lens, place: (0, 0)
    return pl.pallas_call(
        edges_kernel,
        grid_spec=pltpu.PrefetchScalarGridSpec(
            num_scalar_prefetch=2,
            grid=(1,),
            in_specs=in_specs,
            out_specs=[
                pl.BlockSpec((SEND_ROWS, width), whole),
                pl.BlockSpec((SEND_ROWS, width), whole),
                pl.BlockSpec((BS, BS), whole),
                pl.BlockSpec((BS, BS), whole),
            ],
        ),
        out_shape=[
            jax.ShapeDtypeStruct((SEND_ROWS, width), F32),
            jax.ShapeDtypeStruct((SEND_ROWS, width), F32),
            jax.ShapeDtypeStruct((BS, BS), F32),
            jax.ShapeDtypeStruct((BS, BS), F32),
        ],
        compiler_params=pltpu.CompilerParams(vmem_limit_bytes=32 * 2**20),
        name="edges",
    )(lens, place, *([vel] * 4), *([stress] * 4), *([area] * 4), *([thick] * 4), forcing, forcing)


def spread_kernel(forcing, north, south, out, hold):
    def rows16(pair, carry):
        base = pl.multiple_of(pair * 16, 16)
        for cb in range(TILE):
            parts = [
                forcing[f, pl.ds(base, 16), cb * BS : (cb + 1) * BS].astype(F32) for f in range(4)
            ]
            low = jnp.concatenate([p[0:8] for p in parts], axis=0)
            high = jnp.concatenate([p[8:16] for p in parts], axis=0)
            out[2 * pair, cb * 32 : (cb + 1) * 32, :] = low.astype(BF16)
            out[2 * pair + 1, cb * 32 : (cb + 1) * 32, :] = high.astype(BF16)
        return carry

    lax.fori_loop(0, BS // 16, rows16, 0)
    for j in range(NLON):
        hold[...] = jnp.zeros(hold.shape, F32)
        source = north if j < 8 else south
        f = j % 8
        if f < ICE:
            rows = source[3 * f : 3 * f + 3, :]
            high = rows.astype(BF16).astype(F32)
            low = rows - high
            for s in range(SLOTS):
                hold[8 * s : 8 * s + 3, :] = high[:, s * BS : (s + 1) * BS]
                hold[8 * s + 3 : 8 * s + 6, :] = low[:, s * BS : (s + 1) * BS]
        field, h = j // 4, j % 4
        source = south if h < 2 else north
        for cb in range(TILE):
            at = (h % 2) * 512 + cb * BS
            hold[8 * cb + 6 : 8 * cb + 7, :] = source[21 + field : 22 + field, at : at + BS]
        out[j, TILE * 32 :, :] = hold[...].astype(BF16)


def spread(forcing, north, south):
    return pl.pallas_call(
        spread_kernel,
        out_shape=jax.ShapeDtypeStruct((NLON, M1_ROWS, BS), BF16),
        in_specs=[pl.BlockSpec(memory_space=pltpu.VMEM)] * 3,
        out_specs=pl.BlockSpec(memory_space=pltpu.VMEM),
        scratch_shapes=[pltpu.VMEM((SLOTS * 8, BS), F32)],
        compiler_params=pltpu.CompilerParams(vmem_limit_bytes=32 * 2**20),
        name="spread",
    )(forcing, north, south)


def deal_kernel(lens, place, got, out, groups, hold, table):
    band, lon = place[0], place[1]
    odd = lax.rem(band, 2) == 1
    other = jnp.where(lon < 8, jnp.minimum(band + 1, NLAT - 1), jnp.maximum(band - 1, 0))
    other_odd = lax.rem(other, 2) == 1

    def fill(l, start):
        groups[pl.ds(pl.multiple_of(l * SLOTS, SLOTS), SLOTS)] = (
            got[l, TILE * 32 :, :].astype(F32).reshape(SLOTS, 8, BS)
        )
        count = lens[other * NLON + l]

        def slot(s, carry):
            at = start + s
            table[jnp.where(other_odd, NBB - 1 - at, at)] = l * SLOTS + s
            return carry

        lax.fori_loop(0, count, slot, 0)
        return start + count

    lax.fori_loop(0, NLON, fill, 0)
    lane32 = lanes_of((32, BS)) < 64
    lane8 = lanes_of((8, BS)) < 64
    row6 = lax.broadcasted_iota(jnp.int32, (8, BS), 0) == 6
    hold[72:80, :] = jnp.zeros((8, BS), F32)

    def block(c):
        tile, cb = c // TILE, lax.rem(c, TILE)
        rows = got[tile, pl.ds(pl.multiple_of(cb * 32, 32), 32), :].astype(F32)
        group = jnp.where(row6, groups[tile * SLOTS + cb], groups[table[c]])
        return rows, group

    def owner(k, start):
        count = lens[band * NLON + k]
        last = start + count - 1
        east = jnp.where(odd, NBB - 1 - start, last) + 1
        west = jnp.where(odd, NBB - 1 - last, start) - 1
        east, west = lax.rem(east, NBB), lax.rem(west + NBB, NBB)
        for e in range(SLOTS + 1):
            mine = e < count
            at = start + e
            column = jnp.where(odd, NBB - 1 - at, at)
            rows_a, group_a = block(jnp.where(mine, column, east))
            rows_b, group_b = block(jnp.where(mine, column, west))
            out[k, e * 32 : (e + 1) * 32, :] = jnp.where(lane32, rows_a, rows_b).astype(BF16)
            hold[e * 8 : (e + 1) * 8, :] = jnp.where(lane8, group_a, group_b)
        out[k, (SLOTS + 1) * 32 :, :] = hold[...].astype(BF16)
        return start + count

    lax.fori_loop(0, NLON, owner, 0)


def deal(lens, place, got):
    return pl.pallas_call(
        deal_kernel,
        out_shape=jax.ShapeDtypeStruct((NLON, M2_ROWS, BS), BF16),
        in_specs=[pl.BlockSpec(memory_space=pltpu.SMEM)] * 2
        + [pl.BlockSpec(memory_space=pltpu.VMEM)],
        out_specs=pl.BlockSpec(memory_space=pltpu.VMEM),
        scratch_shapes=[
            pltpu.VMEM((NLON * SLOTS, 8, BS), F32),
            pltpu.VMEM((80, BS), F32),
            pltpu.SMEM((NBB,), jnp.int32),
        ],
        compiler_params=pltpu.CompilerParams(vmem_limit_bytes=32 * 2**20),
        name="deal",
    )(lens, place, got)


def dynamics_kernel(
    lens, place, vel, stress, area, thick, got, from_prev, from_next, coriolis,
    vel_out, stress_out, handed, st,
):
    s = pl.program_id(0)
    band, lon = place[0], place[1]
    odd = lax.rem(band, 2) == 1
    count = lens[band * NLON + lon]
    own = pl.ds(TOP, BS)

    def lanes_at(slot):
        return pl.ds(pl.multiple_of(jnp.where(odd, SLOTS - 1 - slot, slot) * BS, BS), BS)

    edge_lanes = pl.ds(SLOTS * BS, BS)

    @pl.when(s == 0)
    def _():
        lane = lanes_of((BS, BS)) < 64
        east = jnp.where(odd, from_prev[...], from_next[...])
        west = jnp.where(odd, from_next[...], from_prev[...])
        edge = []
        for f in range(ICE):
            moved = jnp.where(
                lane,
                pltpu.roll(east, (BS - 3 * f) % BS, 1),
                pltpu.roll(west, 125 - 3 * f, 1),
            )
            st[f, own, edge_lanes] = moved
            edge.append(moved)
        st[STR, own, edge_lanes] = strength_of(edge[AREA], edge[MASS])

        def forcing_rows(j, carry):
            at = pl.ds(pl.multiple_of(TOP + j * 8, 8), 8)
            for e in range(SLOTS + 1):
                rows = got[j, e * 32 : (e + 1) * 32, :].astype(F32)
                lanes = lanes_at(e) if e < SLOTS else edge_lanes
                for f in range(4):
                    st[UO + f, at, lanes] = rows[f * 8 : (f + 1) * 8, :]
            return carry

        lax.fori_loop(0, NLON, forcing_rows, 0)
        for j in range(NLON):
            group = got[j, (SLOTS + 1) * 32 :, :].astype(F32)
            f = j % 8
            row0 = TOP + BS if j < 8 else TOP - DEEP
            force_row = (TOP - 2, TOP - 1, TOP + BS, TOP + BS + 1)[j % 4]
            for e in range(SLOTS + 1):
                lanes = lanes_at(e) if e < SLOTS else edge_lanes
                if f < ICE:
                    st[f, row0 : row0 + DEEP, lanes] = (
                        group[8 * e : 8 * e + 3, :] + group[8 * e + 3 : 8 * e + 6, :]
                    )
                st[UO + j // 4, force_row : force_row + 1, lanes] = group[8 * e + 6 : 8 * e + 7, :]
        for row0 in (0, TOP + BS):
            rows = pl.ds(row0, 8)
            st[STR, rows, :] = strength_of(st[AREA, rows, :], st[MASS, rows, :])

    @pl.when(s < count)
    def _():
        fields = ice_fields(
            [vel[0], vel[1]],
            [stress[0], stress[1], stress[2]],
            [area[n] for n in range(5)],
            [thick[n] for n in range(5)],
        )
        lanes = lanes_at(s)
        for f in range(ICE):
            st[f, own, lanes] = fields[f]
        st[STR, own, lanes] = strength_of(fields[AREA], fields[MASS])

    @pl.when(s >= count)
    def _():
        lanes = lanes_at(s)
        for f in range(STR + 1):
            st[f, own, lanes] = st[f, own, edge_lanes]

    @pl.when(s == SLOTS - 1)
    def _():
        cells = (8, STRIP)

        row = lax.broadcasted_iota(jnp.int32, cells, 0)

        def load(f, g):
            return st[f, pl.ds(pl.multiple_of(g * 8, 8), 8), :]

        def north_of(x, above):
            return pltpu.roll(jnp.where(row == 0, above, x), 7, 0)

        def south_of(x, below):
            return pltpu.roll(jnp.where(row == 7, below, x), 1, 0)

        def stress_rows(g):
            u, v = load(U, g), load(V, g)
            exx = pltpu.roll(u, STRIP - 1, 1) - u
            eyy = north_of(v, load(V, g + 1)) - v
            shr = north_of(u, load(U, g + 1)) - u + (pltpu.roll(v, STRIP - 1, 1) - v)
            div = exx + eyy
            ten = exx - eyy
            square = div * div + 0.25 * (ten * ten + shr * shr) + DMIN_SQ
            third = load(STR, g)
            visc = third * lax.rsqrt(square)
            rows = pl.ds(pl.multiple_of(g * 8, 8), 8)
            st[S1, rows, :] = (2.0 / 3.0) * load(S1, g) + (visc * div - third)
            st[S2, rows, :] = (2.0 / 3.0) * load(S2, g) + 0.25 * visc * ten
            st[S12, rows, :] = (2.0 / 3.0) * load(S12, g) + 0.125 * visc * shr

        def velocity_rows(g, beyond=None):
            below = max(g - 1, 0) if isinstance(g, int) else g - 1
            s1, s2, s12 = load(S1, g), load(S2, g), load(S12, g)
            sxx = 0.5 * (s1 + s2)
            syy = 0.5 * (s1 - s2)
            syy_s = south_of(syy, 0.5 * (load(S1, below) - load(S2, below)))
            fx = sxx - pltpu.roll(sxx, 1, 1) + s12 - south_of(s12, load(S12, below))
            fy = s12 - pltpu.roll(s12, 1, 1) + syy - syy_s
            u, v, uo, vo, m = load(U, g), load(V, g), load(UO, g), load(VO, g), load(MASS, g)
            du, dv = uo - u, vo - v
            square = du * du + dv * dv + SPEED_SQ
            drag = load(AREA, g) * (square * lax.rsqrt(square))
            d = m + drag
            turn = jnp.broadcast_to(
                coriolis[pl.ds(pl.multiple_of(g * 8, 8), 8), :], (8, BS)
            )
            q = jnp.concatenate([turn] * (SLOTS + 1), axis=1) * m
            ru = m * u + fx + load(TX, g) + drag * uo
            rv = m * v + fy + load(TY, g) + drag * vo
            inv = 1.0 / (d * d + q * q)
            new_u = (d * ru + q * rv) * inv
            new_v = (d * rv - q * ru) * inv
            if beyond is not None:
                new_u = jnp.where(beyond, 0.0, new_u)
                new_v = jnp.where(beyond, 0.0, new_v)
            rows = pl.ds(pl.multiple_of(g * 8, 8), 8)
            st[U, rows, :] = new_u
            st[V, rows, :] = new_v

        groups = BS // 8
        first = jnp.broadcast_to(band == 0, cells)
        final = jnp.broadcast_to(band == NLAT - 1, cells)
        for it in range(ITERS):
            last = it == ITERS - 1

            def stress_step(g, carry):
                stress_rows(g)
                return carry

            def velocity_step(g, carry):
                velocity_rows(g)
                return carry

            lax.fori_loop(0, groups + (1 if last else 2), stress_step, 0)
            if not last:
                velocity_rows(0, first)
                velocity_rows(groups + 1, final)
            lax.fori_loop(1, groups + 1, velocity_step, 0)

        def finish(j, carry):
            rows = pl.ds(pl.multiple_of(TOP + j * 8, 8), 8)
            out_rows = pl.ds(pl.multiple_of(j * 8, 8), 8)
            for e in range(SLOTS):
                lanes = lanes_at(e)
                out_lanes = slice(e * BS, (e + 1) * BS)
                mine = jnp.broadcast_to(e < count, (8, BS))
                u, v = st[U, rows, lanes], st[V, rows, lanes]
                vel_out[0, out_rows, out_lanes] = jnp.where(mine, u, 0.0)
                vel_out[1, out_rows, out_lanes] = jnp.where(mine, v, 0.0)
                for n in range(3):
                    stress_out[n, out_rows, out_lanes] = jnp.where(
                        mine, st[S1 + n, rows, lanes], 0.0
                    )
                conc = st[AREA, rows, lanes]
                du, dv = u - st[UO, rows, lanes], v - st[VO, rows, lanes]
                square = du * du + dv * dv + SPEED_SQ
                drag = conc * (square * lax.rsqrt(square))
                x = (1.0 - conc) * st[TX, rows, lanes] + drag * du
                y = (1.0 - conc) * st[TY, rows, lanes] + drag * dv
                handed[j, e * 16 : (e + 1) * 16, :] = jnp.concatenate([x, y], axis=0).astype(BF16)
            return carry

        lax.fori_loop(0, groups, finish, 0)


def dynamics(lens, place, vel, stress, area, thick, got, from_prev, from_next, coriolis):
    def slot(n):
        return pl.BlockSpec((n, BS, BS), lambda i, lens, place: (0, 0, i))

    def whole(*shape):
        return pl.BlockSpec(shape, lambda i, lens, place: (0,) * len(shape))

    width = SLOTS * BS
    return pl.pallas_call(
        dynamics_kernel,
        grid_spec=pltpu.PrefetchScalarGridSpec(
            num_scalar_prefetch=2,
            grid=(SLOTS,),
            in_specs=[
                slot(2), slot(3), slot(5), slot(5),
                whole(NLON, M2_ROWS, BS), whole(BS, BS), whole(BS, BS), whole(ROWS, BS),
            ],
            out_specs=[whole(2, BS, width), whole(3, BS, width), whole(NLON, M3_ROWS, BS)],
            scratch_shapes=[pltpu.VMEM((12, ROWS + 8, STRIP), F32)],
        ),
        out_shape=[
            jax.ShapeDtypeStruct((2, BS, width), F32),
            jax.ShapeDtypeStruct((3, BS, width), F32),
            jax.ShapeDtypeStruct((NLON, M3_ROWS, BS), BF16),
        ],
        compiler_params=pltpu.CompilerParams(vmem_limit_bytes=48 * 2**20),
        name="dynamics",
    )(lens, place, vel, stress, area, thick, got, from_prev, from_next, coriolis)


def sort_kernel(lens, place, got, out):
    band = place[0]
    odd = lax.rem(band, 2) == 1

    def owner(k, start):
        count = lens[band * NLON + k]

        def slot(s, carry):
            at = start + s
            out[jnp.where(odd, NBB - 1 - at, at)] = got[k * SLOTS + s]
            return carry

        lax.fori_loop(0, count, slot, 0)
        return start + count

    lax.fori_loop(0, NLON, owner, 0)


def sort_back(lens, place, got):
    return pl.pallas_call(
        sort_kernel,
        out_shape=jax.ShapeDtypeStruct((NBB, 16, BS), BF16),
        in_specs=[pl.BlockSpec(memory_space=pltpu.SMEM)] * 2
        + [pl.BlockSpec(memory_space=pltpu.VMEM)],
        out_specs=pl.BlockSpec(memory_space=pltpu.VMEM),
        name="sort_back",
    )(lens, place, got)


def settle_kernel(got, out):
    def rows16(pair, carry):
        rows = pl.ds(pl.multiple_of(pair * 16, 16), 16)
        for cb in range(TILE):
            a = got[2 * pair, cb * 16 : (cb + 1) * 16, :].astype(F32)
            b = got[2 * pair + 1, cb * 16 : (cb + 1) * 16, :].astype(F32)
            lanes = slice(cb * BS, (cb + 1) * BS)
            out[0, rows, lanes] = jnp.concatenate([a[0:8], b[0:8]], axis=0).astype(BF16)
            out[1, rows, lanes] = jnp.concatenate([a[8:16], b[8:16]], axis=0).astype(BF16)
        return carry

    lax.fori_loop(0, BS // 16, rows16, 0)


def settle(got):
    return pl.pallas_call(
        settle_kernel,
        out_shape=jax.ShapeDtypeStruct((2, BS, TILE * BS), BF16),
        in_specs=[pl.BlockSpec(memory_space=pltpu.VMEM)],
        out_specs=pl.BlockSpec(memory_space=pltpu.VMEM),
        name="settle",
    )(got)


def to_all(block):
    return lax.all_to_all(block, "lon", 0, 0, tiled=True)


def body(ocean_forcing, ice_velocity, ice_stress, cat_area, cat_thick, run_lengths):
    band_idx = lax.axis_index("lat")
    lon_idx = lax.axis_index("lon")
    lens = run_lengths.reshape(-1)
    place = jnp.stack([band_idx, lon_idx]).astype(jnp.int32)
    ice = (ice_velocity, ice_stress, cat_area, cat_thick)
    to_south, to_north, to_prev, to_next = make_edges(lens, place, *ice, ocean_forcing)
    north = lax.ppermute(to_south, "lat", [(b, b - 1) for b in range(1, NLAT)])
    south = lax.ppermute(to_north, "lat", [(b, b + 1) for b in range(NLAT - 1)])
    from_prev = lax.ppermute(to_next, "lon", [(k, (k + 1) % NLON) for k in range(NLON)])
    from_next = lax.ppermute(to_prev, "lon", [(k, (k - 1) % NLON) for k in range(NLON)])
    rows = (band_idx * BS + jnp.arange(-TOP, BS + TOP, dtype=jnp.int32)).astype(F32)
    latitude = -78.0 + 168.0 * (rows + 0.5) / (BS * NLAT)
    coriolis = jnp.broadcast_to(jnp.sin(latitude * (jnp.pi / 180.0))[:, None], (ROWS, BS))
    dealt = to_all(deal(lens, place, to_all(spread(ocean_forcing, north, south))))
    velocity_out, stress_out, handed = dynamics(
        lens, place, *ice, dealt, from_prev, from_next, coriolis
    )
    handed = to_all(handed).reshape(NLON * SLOTS, 16, BS)
    back = sort_back(lens, place, handed).reshape(NLON, M4_ROWS, BS)
    return (velocity_out, stress_out, settle(to_all(back)))


def solution(mesh):
    slots = P(None, None, ("lat", "lon"))
    grid = P(None, "lat", "lon")
    return jax.shard_map(
        body,
        mesh=mesh,
        in_specs=(grid, slots, slots, slots, slots, P()),
        out_specs=(slots, slots, grid),
        check_vma=False,
    )
```

time: 363 us -> 130 us (0.36)
  the two profiles are of different devices: /device:TPU:8 before, /device:TPU:0 now
where the time goes in v1:
time: 130 us
  blocking collectives  50.8 us (39%)
  Pallas kernels  30.4 us (23%)
  waiting for transfers between devices  23.9 us (18%)
  starting transfers between devices  14.4 us (11%)
  local copies, waits for them, and re-layouts  9.13 us (7%)
    all_to_all x3, blocking collectives, to_all(): return lax.all_to_all(block, 'lon', 0, 0, tiled=True)  50.8 us
    pallas_call x1, Pallas kernels, dynamics(): pl.pallas_call(dynamics_kernel, grid_spec=pltpu.PrefetchScalarGridSpec(nu...  21.2 us
    ppermute x1, waiting for transfers between devices, body(): lax.ppermute(to_next, 'lon', [(k, (k + 1) % NLON) for k in range(NLON)])  17.9 us
    unnamed x20, local copies, waits for them, and re-layouts  8.29 us
    all_to_all x1, starting transfers between devices, to_all(): return lax.all_to_all(block, 'lon', 0, 0, tiled=True)  4.68 us
    all_to_all x1, waiting for transfers between devices, to_all(): return lax.all_to_all(block, 'lon', 0, 0, tiled=True)  4.56 us
    pallas_call x1, Pallas kernels, deal(): pl.pallas_call(deal_kernel, out_shape=jax.ShapeDtypeStruct((NLON, M2_ROWS...  3.8 us
    ppermute x1, starting transfers between devices, body(): lax.ppermute(to_prev, 'lon', [(k, (k - 1) % NLON) for k in range(NLON)])  3.66 us
  transfers between devices with their start and end apart: 5, of which 4 were waited for; matrix products, arithmetic and copies ran while one was open for 0% of the time, Pallas kernels for 0%

profile of v1, /device:TPU:0, one launch (start us, length us, event | category | flops | bytes accessed | tf_op | source)
XLA Modules:
  0.0 129.5 jit_solution(9577862338239269144)
XLA Ops:
  0.6 0.8 reshape.26.lens
  1.4 0.0 copy-start.8
  1.4 0.1 pad_add_fusion.place
  1.5 0.0 copy-start
  1.5 1.7 %copy-done = f32[5,128,1024]{2,1,0:T(8,128)S(1)} copy-done((f32[5,128,1024]{2,1,0:T(8,128)S(1)}, f32[5,128,1024]{2,1,0:T(8,128)}, u32[]{:S(2)}) %copy-start) | copy-done | bytes 2621464
  3.2 0.0 copy-start.1
  3.2 1.7 %copy-done.1 = f32[5,128,1024]{2,1,0:T(8,128)S(1)} copy-done((f32[5,128,1024]{2,1,0:T(8,128)S(1)}, f32[5,128,1024]{2,1,0:T(8,128)}, u32[]{:S(2)}) %copy-start.1) | copy-done | bytes 2621464
  5.0 0.0 copy-start.2
  5.0 1.4 %copy-done.2 = f32[3,128,1024]{2,1,0:T(8,128)S(1)} copy-done((f32[3,128,1024]{2,1,0:T(8,128)S(1)}, f32[3,128,1024]{2,1,0:T(8,128)}, u32[]{:S(2)}) %copy-start.2) | copy-done | bytes 1572888
  6.4 0.0 copy-start.4
  6.4 1.2 copy-done.4
  7.6 0.0 copy-start.7
  7.6 1.0 copy-done.7
  8.6 0.0 copy-start.9
  8.6 1.0 edges.1
  9.7 1.3 collective-permute-start
  11.0 3.0 %collective-permute-start.1 = (f32[32,1024]{1,0:T(8,128)S(1)}, f32[32,1024]{1,0:T(8,128)S(1)}, u32[]{:S(2)}, u32[]{:S(2)}) collective-permute-start(f32[32,1024]{1,0:T(8,128)S(1)} %get-tuple-element.11), channel_id=1, source_target_pairs={{0,16},{16,32},{32,48},{48,64},{64,80},{80,96},{96,112},{1,17},{17... | collective-permute-start | bytes 393224 | tf_op jit(solution)/shard_map/ppermute | solution.py:515
  14.0 0.0 collective-permute-done.north
  14.0 1.0 collective-permute-done.1.south
  15.0 0.3 spread.1
  15.3 22.6 %all_to_all.20.got = bf16[16,192,128]{2,1,0:T(8,128)(2,1)S(1)} all-to-all(bf16[16,192,128]{2,1,0:T(8,128)(2,1)S(1)} %spread.1), channel_id=1, replica_groups=mesh['lat'=8,'lon'=16] {'lon'}, dimensions={0} | all-to-all | bytes 1572864 | tf_op jit(solution)/shard_map/all_to_all | solution.py:504
  37.9 3.8 %deal.1 = bf16[16,368,128]{2,1,0:T(8,128)(2,1)S(1)} custom-call(s32[128]{0:T(128)S(1)} %reshape.26.lens, s32[2]{0:T(128)S(1)} %pad_add_fusion.place, bf16[16,192,128]{2,1,0:T(8,128)(2,1)S(1)} %all_to_all.20.got), custom_call_target="tpu_custom_call" | custom-call | tf_op jit(solution)/shard_map/deal/pallas_call | solution.py:223
  41.7 0.0 copy-start.6
  41.8 1.1 copy-done.6
  42.9 0.0 copy-start.3
  42.9 0.0 copy-start.5
  42.9 4.7 %all-to-all-start.1 = ((bf16[16,368,128]{2,1,0:T(8,128)(2,1)}), bf16[16,368,128]{2,1,0:T(8,128)(2,1)}, u32[]{:S(2)}, u32[]{:S(2)}) async-start(bf16[16,368,128]{2,1,0:T(8,128)(2,1)} %copy-done.6), calls=%async_computation.1 | async-start | bytes 3014656 | tf_op jit(solution)/shard_map/all_to_all | solution.py:504
  47.6 1.8 %collective-permute-start.2 = (f32[128,128]{1,0:T(8,128)S(1)}, f32[128,128]{1,0:T(8,128)S(1)}, u32[]{:S(2)}, u32[]{:S(2)}) collective-permute-start(f32[128,128]{1,0:T(8,128)S(1)} %get-tuple-element.12), channel_id=1, source_target_pairs={{0,1},{1,2},{2,3},{3,4},{4,5},{5,6},{6,7},{7,8},{8,9},{9,10},{10,1... | collective-permute-start | bytes 196616 | tf_op jit(solution)/shard_map/ppermute | solution.py:516
  49.3 3.7 %collective-permute-start.3 = (f32[128,128]{1,0:T(8,128)S(1)}, f32[128,128]{1,0:T(8,128)S(1)}, u32[]{:S(2)}, u32[]{:S(2)}) collective-permute-start(f32[128,128]{1,0:T(8,128)S(1)} %get-tuple-element.13), channel_id=1, source_target_pairs={{0,15},{1,0},{2,1},{3,2},{4,3},{5,4},{6,5},{7,6},{8,7},{9,8},{10,9... | collective-permute-start | bytes 196616 | tf_op jit(solution)/shard_map/ppermute | solution.py:517
  53.0 17.9 %collective-permute-done.2.from_prev = f32[128,128]{1,0:T(8,128)S(1)} collective-permute-done((f32[128,128]{1,0:T(8,128)S(1)}, f32[128,128]{1,0:T(8,128)S(1)}, u32[]{:S(2)}, u32[]{:S(2)}) %collective-permute-start.2) | collective-permute-done | bytes 65568 | tf_op jit(solution)/shard_map/ppermute | solution.py:516
  71.0 0.4 collective-permute-done.3.from_next
  71.4 4.6 %all-to-all-done.1.got = bf16[16,368,128]{2,1,0:T(8,128)(2,1)} async-done(((bf16[16,368,128]{2,1,0:T(8,128)(2,1)}), bf16[16,368,128]{2,1,0:T(8,128)(2,1)}, u32[]{:S(2)}, u32[]{:S(2)}) %all-to-all-start.1) | async-done | bytes 1507360 | tf_op jit(solution)/shard_map/all_to_all | solution.py:504
  75.9 0.1 broadcast_in_dim.2.coriolis
  76.0 0.0 copy-done.8
  76.0 0.0 copy-done.9
  76.0 0.0 copy-done.3
  76.0 0.0 copy-done.5
  76.1 21.2 %dynamics.1 = (f32[2,128,1024]{2,1,0:T(8,128)}, f32[3,128,1024]{2,1,0:T(8,128)}, bf16[16,128,128]{2,1,0:T(8,128)(2,1)S(1)}) custom-call(s32[128]{0:T(128)S(1)} %reshape.26.lens, s32[2]{0:T(128)S(1)} %pad_add_fusion.place, f32[2,128,1024]{2,1,0:T(8,128)S(1)} %copy-done.5, f32[3,128,1024]{2,1,0:T(8,128)S(1)} %copy-done.3, f32[5,128,1024]{2,1,0:T(8,128)} %area.1, ...), custom_call_target="tpu_custom_call" | custom-call | tf_op jit(solution)/shard_map/dynamics/pallas_call | solution.py:428
  97.2 15.3 %all_to_all.21 = bf16[16,128,128]{2,1,0:T(8,128)(2,1)} all-to-all(bf16[16,128,128]{2,1,0:T(8,128)(2,1)S(1)} %get-tuple-element.16), channel_id=1, replica_groups=mesh['lat'=8,'lon'=16] {'lon'}, dimensions={0} | all-to-all | bytes 1048576 | tf_op jit(solution)/shard_map/all_to_all | solution.py:504
  112.5 2.4 %sort_back.1 = bf16[64,16,128]{2,1,0:T(8,128)(2,1)} custom-call(s32[128]{0:T(128)} %copy-done.8, s32[2]{0:T(128)} %copy-done.9, bf16[128,16,128]{2,1,0:T(8,128)(2,1)} %bitcast.4), custom_call_target="tpu_custom_call" | custom-call | tf_op jit(solution)/shard_map/sort_back/pallas_call | solution.py:469
  114.9 12.9 %all_to_all.22.got = bf16[16,64,128]{2,1,0:T(8,128)(2,1)} all-to-all(bf16[16,64,128]{2,1,0:T(8,128)(2,1)} %bitcast.5), channel_id=1, replica_groups=mesh['lat'=8,'lon'=16] {'lon'}, dimensions={0} | all-to-all | bytes 524288 | tf_op jit(solution)/shard_map/all_to_all | solution.py:504
  127.8 1.7 %settle.1 = bf16[2,128,512]{2,1,0:T(8,128)(2,1)} custom-call(bf16[16,64,128]{2,1,0:T(8,128)(2,1)} %all_to_all.22.got), custom_call_target="tpu_custom_call" | custom-call | tf_op jit(solution)/shard_map/settle/pallas_call | solution.py:494
  (1 shorter events, 0.0 us)
Async XLA Ops:
  1.4 74.6 %copy-start.8 = (s32[128]{0:T(128)}, s32[128]{0:T(128)S(1)}, u32[]{:S(2)}) copy-start(s32[128]{0:T(128)S(1)} %reshape.26.lens) | copy-start | bytes 1540
  1.5 1.7 %copy-start = (f32[5,128,1024]{2,1,0:T(8,128)S(1)}, f32[5,128,1024]{2,1,0:T(8,128)}, u32[]{:S(2)}) copy-start(f32[5,128,1024]{2,1,0:T(8,128)} %area.1) | copy-start | bytes 7864324
  3.2 1.7 %copy-start.1 = (f32[5,128,1024]{2,1,0:T(8,128)S(1)}, f32[5,128,1024]{2,1,0:T(8,128)}, u32[]{:S(2)}) copy-start(f32[5,128,1024]{2,1,0:T(8,128)} %thick.1) | copy-start | bytes 7864324
  5.0 1.4 %copy-start.2 = (f32[3,128,1024]{2,1,0:T(8,128)S(1)}, f32[3,128,1024]{2,1,0:T(8,128)}, u32[]{:S(2)}) copy-start(f32[3,128,1024]{2,1,0:T(8,128)} %stress.1) | copy-start | bytes 4718596
  6.4 1.2 copy-start.4
  7.6 1.0 copy-start.7
  8.6 67.4 %copy-start.9 = (s32[2]{0:T(128)}, s32[2]{0:T(128)S(1)}, u32[]{:S(2)}) copy-start(s32[2]{0:T(128)S(1)} %pad_add_fusion.place) | copy-start | bytes 28
  9.7 4.3 %collective-permute-start = (f32[32,1024]{1,0:T(8,128)S(1)}, f32[32,1024]{1,0:T(8,128)S(1)}, u32[]{:S(2)}, u32[]{:S(2)}) collective-permute-start(f32[32,1024]{1,0:T(8,128)S(1)} %get-tuple-element.10), channel_id=1, source_target_pairs={{16,0},{32,16},{48,32},{64,48},{80,64},{96,80},{112,96},{17,1},{33... | collective-permute-start | bytes 393224 | tf_op jit(solution)/shard_map/ppermute | solution.py:514
  11.0 4.0 %collective-permute-start.1 = (f32[32,1024]{1,0:T(8,128)S(1)}, f32[32,1024]{1,0:T(8,128)S(1)}, u32[]{:S(2)}, u32[]{:S(2)}) collective-permute-start(f32[32,1024]{1,0:T(8,128)S(1)} %get-tuple-element.11), channel_id=1, source_target_pairs={{0,16},{16,32},{32,48},{48,64},{64,80},{80,96},{96,112},{1,17},{17... | collective-permute-start | bytes 393224 | tf_op jit(solution)/shard_map/ppermute | solution.py:515
  41.7 1.1 copy-start.6
  42.9 33.2 %copy-start.3 = (f32[3,128,1024]{2,1,0:T(8,128)S(1)}, f32[3,128,1024]{2,1,0:T(8,128)}, u32[]{:S(2)}) copy-start(f32[3,128,1024]{2,1,0:T(8,128)} %stress.1) | copy-start | bytes 4718596
  42.9 33.2 %copy-start.5 = (f32[2,128,1024]{2,1,0:T(8,128)S(1)}, f32[2,128,1024]{2,1,0:T(8,128)}, u32[]{:S(2)}) copy-start(f32[2,128,1024]{2,1,0:T(8,128)} %vel.1) | copy-start | bytes 3145732
  42.9 33.1 %all-to-all-start.1 = ((bf16[16,368,128]{2,1,0:T(8,128)(2,1)}), bf16[16,368,128]{2,1,0:T(8,128)(2,1)}, u32[]{:S(2)}, u32[]{:S(2)}) async-start(bf16[16,368,128]{2,1,0:T(8,128)(2,1)} %copy-done.6), calls=%async_computation.1 | async-start | bytes 3014656 | tf_op jit(solution)/shard_map/all_to_all | solution.py:504
  47.6 23.4 %collective-permute-start.2 = (f32[128,128]{1,0:T(8,128)S(1)}, f32[128,128]{1,0:T(8,128)S(1)}, u32[]{:S(2)}, u32[]{:S(2)}) collective-permute-start(f32[128,128]{1,0:T(8,128)S(1)} %get-tuple-element.12), channel_id=1, source_target_pairs={{0,1},{1,2},{2,3},{3,4},{4,5},{5,6},{6,7},{7,8},{8,9},{9,10},{10,1... | collective-permute-start | bytes 196616 | tf_op jit(solution)/shard_map/ppermute | solution.py:516
  49.3 22.1 %collective-permute-start.3 = (f32[128,128]{1,0:T(8,128)S(1)}, f32[128,128]{1,0:T(8,128)S(1)}, u32[]{:S(2)}, u32[]{:S(2)}) collective-permute-start(f32[128,128]{1,0:T(8,128)S(1)} %get-tuple-element.13), channel_id=1, source_target_pairs={{0,15},{1,0},{2,1},{3,2},{4,3},{5,4},{6,5},{7,6},{8,7},{9,8},{10,9... | collective-permute-start | bytes 196616 | tf_op jit(solution)/shard_map/ppermute | solution.py:517

commit v2 on v1

v2 whole, which is shorter than its diff:
```python
import functools

import jax
import jax.numpy as jnp
from jax import lax
from jax.experimental import pallas as pl
from jax.experimental.pallas import tpu as pltpu
from jax.sharding import PartitionSpec as P

BS = 128
ITERS = 3
NLAT = 8
NLON = 16
SLOTS = 8
NBB = 64
TILE = 4
DEEP = 3
PSTAR = 2.0
CSTAR = 20.0
DMIN_SQ = 0.01
SPEED_SQ = 0.01
ICE = 7
U, V, SXX, SYY, S12, AREA, MASS, STR, UO, VO, TX, TY, TURN, S2_OUT = range(14)
EDGE_LANES = 3 * ICE
STRIP = (SLOTS + 1) * BS
WIDE = 3 * BS
TOP = 8
ROWS = BS + 2 * TOP
SEND_ROWS = 32
M1_ROWS = TILE * 32 + SLOTS * 8
M2_ROWS = (SLOTS + 1) * 32 + 80
M3_ROWS = SLOTS * 16
M4_ROWS = TILE * 16
F32 = jnp.float32
BF16 = jnp.bfloat16


def lanes_of(shape):
    return lax.broadcasted_iota(jnp.int32, shape, len(shape) - 1)


def ice_fields(vel, stress, area, thick):
    conc = area[0] + area[1] + area[2] + area[3] + area[4]
    mass = area[0] * thick[0]
    for n in range(1, 5):
        mass = mass + area[n] * thick[n]
    sxx, syy = 0.5 * (stress[0] + stress[1]), 0.5 * (stress[0] - stress[1])
    return [vel[0], vel[1], sxx, syy, stress[2], conc, mass]


def strength_of(conc, mass):
    return (PSTAR / 6.0) * mass * jnp.exp(-CSTAR * (1.0 - conc))


def edges_kernel(lens, place, *refs):
    ice = [refs[4 * i : 4 * i + 4] for i in range(4)]
    f_low, f_high, south, north, packed_out = refs[16:]
    odd = lax.rem(place[0], 2) == 1
    for out, which, force, row0, frow0 in (
        (south, 0, f_low, 0, 0),
        (north, 1, f_high, 5, 14),
    ):
        arrays = [ice[i][which] for i in range(4)]
        fields = ice_fields(*[[a[n] for n in range(a.shape[0])] for a in arrays])
        out[...] = jnp.zeros(out.shape, F32)
        for f in range(ICE):
            out[3 * f : 3 * f + 3, :] = fields[f][row0 : row0 + 3, :]
        for f in range(4):
            rows = force[f].astype(F32)
            out[21 + f : 22 + f, 0:512] = rows[frow0 : frow0 + 1, :]
            out[21 + f : 22 + f, 512:1024] = rows[frow0 + 1 : frow0 + 2, :]
    lane = lanes_of((BS, BS))
    packed = jnp.zeros((BS, BS), F32)
    for side, which, col_even, col_odd in ((0, 2, 0, 125), (1, 3, 125, 0)):
        arrays = [ice[i][which] for i in range(4)]
        fields = ice_fields(*[[a[n] for n in range(a.shape[0])] for a in arrays])
        for f in range(ICE):
            at = 2 * side * EDGE_LANES + 3 * f
            high = fields[f].astype(BF16).astype(F32)
            for part, there in ((high, at), (fields[f] - high, at + EDGE_LANES)):
                shift = jnp.where(odd, (there - col_odd) % BS, (there - col_even) % BS)
                moved = pltpu.roll(part, shift, 1)
                packed = jnp.where((lane >= there) & (lane < there + 3), moved, packed)
    packed_out[...] = packed


def make_edges(lens, place, vel, stress, area, thick, forcing):
    width = SLOTS * BS

    def specs(n):
        return [
            pl.BlockSpec((n, 8, width), lambda i, lens, place: (0, 0, 0)),
            pl.BlockSpec((n, 8, width), lambda i, lens, place: (0, BS // 8 - 1, 0)),
            pl.BlockSpec((n, BS, BS), lambda i, lens, place: (0, 0, 0)),
            pl.BlockSpec(
                (n, BS, BS),
                lambda i, lens, place: (0, 0, lens[place[0], place[1]] - 1),
            ),
        ]

    in_specs = specs(2) + specs(3) + specs(5) + specs(5)
    in_specs += [
        pl.BlockSpec((4, 16, 512), lambda i, lens, place: (0, 0, 0)),
        pl.BlockSpec((4, 16, 512), lambda i, lens, place: (0, BS // 16 - 1, 0)),
    ]
    whole = lambda i, lens, place: (0, 0)
    return pl.pallas_call(
        edges_kernel,
        grid_spec=pltpu.PrefetchScalarGridSpec(
            num_scalar_prefetch=2,
            grid=(1,),
            in_specs=in_specs,
            out_specs=[
                pl.BlockSpec((SEND_ROWS, width), whole),
                pl.BlockSpec((SEND_ROWS, width), whole),
                pl.BlockSpec((BS, BS), whole),
            ],
        ),
        out_shape=[
            jax.ShapeDtypeStruct((SEND_ROWS, width), F32),
            jax.ShapeDtypeStruct((SEND_ROWS, width), F32),
            jax.ShapeDtypeStruct((BS, BS), F32),
        ],
        compiler_params=pltpu.CompilerParams(vmem_limit_bytes=60 * 2**20),
        name="edges",
    )(lens, place, *([vel] * 4), *([stress] * 4), *([area] * 4), *([thick] * 4), forcing, forcing)


def spread_kernel(forcing, north, south, edges, out, hold):
    def rows16(pair, carry):
        base = pl.multiple_of(pair * 16, 16)
        for cb in range(TILE):
            parts = [
                forcing[f, pl.ds(base, 16), cb * BS : (cb + 1) * BS].astype(F32) for f in range(4)
            ]
            low = jnp.concatenate([p[0:8] for p in parts], axis=0)
            high = jnp.concatenate([p[8:16] for p in parts], axis=0)
            out[2 * pair, cb * 32 : (cb + 1) * 32, :] = low.astype(BF16)
            out[2 * pair + 1, cb * 32 : (cb + 1) * 32, :] = high.astype(BF16)
        return carry

    lax.fori_loop(0, BS // 16, rows16, 0)
    for j in range(NLON):
        hold[...] = jnp.zeros(hold.shape, F32)
        source = north if j < 8 else south
        f = j % 8
        if f < ICE:
            rows = source[3 * f : 3 * f + 3, :]
            high = rows.astype(BF16).astype(F32)
            low = rows - high
            for s in range(SLOTS):
                hold[8 * s : 8 * s + 3, :] = high[:, s * BS : (s + 1) * BS]
                hold[8 * s + 3 : 8 * s + 6, :] = low[:, s * BS : (s + 1) * BS]
        field, h = j // 4, j % 4
        source = south if h < 2 else north
        for cb in range(TILE):
            at = (h % 2) * 512 + cb * BS
            hold[8 * cb + 6 : 8 * cb + 7, :] = source[21 + field : 22 + field, at : at + BS]
        for s in range(SLOTS):
            hold[8 * s + 7 : 8 * s + 8, :] = edges[8 * j + s : 8 * j + s + 1, :]
        out[j, TILE * 32 :, :] = hold[...].astype(BF16)


def spread(forcing, north, south, edges):
    return pl.pallas_call(
        spread_kernel,
        out_shape=jax.ShapeDtypeStruct((NLON, M1_ROWS, BS), BF16),
        in_specs=[pl.BlockSpec(memory_space=pltpu.VMEM)] * 4,
        out_specs=pl.BlockSpec(memory_space=pltpu.VMEM),
        scratch_shapes=[pltpu.VMEM((SLOTS * 8, BS), F32)],
        compiler_params=pltpu.CompilerParams(vmem_limit_bytes=32 * 2**20),
        name="spread",
    )(forcing, north, south, edges)


def deal_kernel(lens, place, got, out, groups, hold, table):
    band, lon = place[0], place[1]
    odd = lax.rem(band, 2) == 1
    other = jnp.where(lon < 8, jnp.minimum(band + 1, NLAT - 1), jnp.maximum(band - 1, 0))
    other_odd = lax.rem(other, 2) == 1

    def fill(l, start):
        groups[pl.ds(pl.multiple_of(l * SLOTS, SLOTS), SLOTS)] = (
            got[l, TILE * 32 :, :].astype(F32).reshape(SLOTS, 8, BS)
        )
        count = lens[other, l]

        def slot(s, carry):
            at = start + s
            table[jnp.where(other_odd, NBB - 1 - at, at)] = l * SLOTS + s
            return carry

        lax.fori_loop(0, count, slot, 0)
        return start + count

    lax.fori_loop(0, NLON, fill, 0)
    lane32 = lanes_of((32, BS)) < 64
    lane8 = lanes_of((8, BS)) < 64
    row6 = lax.broadcasted_iota(jnp.int32, (8, BS), 0) == 6
    from_next = lanes_of((8, BS)) < 2 * EDGE_LANES

    def edges(k):
        at = pl.multiple_of(lax.rem(k, NLON) * SLOTS, SLOTS)
        return groups[pl.ds(at, SLOTS), 7, :]

    def block(c):
        tile, cb = c // TILE, lax.rem(c, TILE)
        rows = got[tile, pl.ds(pl.multiple_of(cb * 32, 32), 32), :].astype(F32)
        group = jnp.where(row6, groups[tile * SLOTS + cb], groups[table[c]])
        return rows, group

    def owner(k, start):
        count = lens[band, k]
        last = start + count - 1
        east = jnp.where(odd, NBB - 1 - start, last) + 1
        west = jnp.where(odd, NBB - 1 - last, start) - 1
        east, west = lax.rem(east, NBB), lax.rem(west + NBB, NBB)
        for e in range(SLOTS + 1):
            mine = e < count
            at = start + e
            column = jnp.where(odd, NBB - 1 - at, at)
            rows_a, group_a = block(jnp.where(mine, column, east))
            rows_b, group_b = block(jnp.where(mine, column, west))
            out[k, e * 32 : (e + 1) * 32, :] = jnp.where(lane32, rows_a, rows_b).astype(BF16)
            hold[e * 8 : (e + 1) * 8, :] = jnp.where(lane8, group_a, group_b)
        hold[72:80, :] = jnp.where(from_next, edges(k + 1), edges(k + NLON - 1))
        out[k, (SLOTS + 1) * 32 :, :] = hold[...].astype(BF16)
        return start + count

    lax.fori_loop(0, NLON, owner, 0)


def deal(lens, place, got):
    return pl.pallas_call(
        deal_kernel,
        out_shape=jax.ShapeDtypeStruct((NLON, M2_ROWS, BS), BF16),
        in_specs=[pl.BlockSpec(memory_space=pltpu.SMEM)] * 2
        + [pl.BlockSpec(memory_space=pltpu.VMEM)],
        out_specs=pl.BlockSpec(memory_space=pltpu.VMEM),
        scratch_shapes=[
            pltpu.VMEM((NLON * SLOTS, 8, BS), F32),
            pltpu.VMEM((80, BS), F32),
            pltpu.SMEM((NBB,), jnp.int32),
        ],
        compiler_params=pltpu.CompilerParams(vmem_limit_bytes=32 * 2**20),
        name="deal",
    )(lens, place, got)


def dynamics_kernel(
    lens, place, vel, stress, area, thick, got, coriolis,
    vel_out, stress_out, handed, st, edge, empty, sems,
):
    band, lon = place[0], place[1]
    odd = lax.rem(band, 2) == 1
    count = lens[band, lon]
    groups = BS // 8

    def rows_at(g):
        return pl.ds(g * 8 if isinstance(g, int) else pl.multiple_of(g * 8, 8), 8)

    def slot_lanes(slot):
        return pl.ds(pl.multiple_of(jnp.where(odd, SLOTS - 1 - slot, slot) * BS, BS), BS)

    edge_lanes = pl.ds(SLOTS * BS, BS)
    empty[...] = jnp.zeros(empty.shape, F32)

    def arrived(j, carry):
        for e in range(SLOTS + 1):
            rows = got[j, e * 32 : (e + 1) * 32, :].astype(F32)
            lanes = slot_lanes(e) if e < SLOTS else edge_lanes
            for f in range(4):
                st[UO + f, rows_at(j + 1), lanes] = rows[f * 8 : (f + 1) * 8, :]
        edge[rows_at(j), :] = got[j, M2_ROWS - 16 :, :].astype(F32)[8:16, :]
        return carry

    lax.fori_loop(0, NLON, arrived, 0)
    for j in range(NLON):
        group = got[j, (SLOTS + 1) * 32 :, :].astype(F32)
        f = j % 8
        row0 = TOP + BS if j < 8 else TOP - DEEP
        force_row = (TOP - 2, TOP - 1, TOP + BS, TOP + BS + 1)[j % 4]
        for e in range(SLOTS + 1):
            lanes = slot_lanes(e) if e < SLOTS else edge_lanes
            if f < ICE:
                st[f, row0 : row0 + DEEP, lanes] = (
                    group[8 * e : 8 * e + 3, :] + group[8 * e + 3 : 8 * e + 6, :]
                )
            st[UO + j // 4, force_row : force_row + 1, lanes] = group[8 * e + 6 : 8 * e + 7, :]

    def derived(conc, mass, g, lanes):
        turn = coriolis[rows_at(g), :]
        if conc.shape[1] > BS:
            turn = jnp.concatenate([turn] * (conc.shape[1] // BS), axis=1)
        st[STR, rows_at(g), lanes] = strength_of(conc, mass)
        st[TURN, rows_at(g), lanes] = turn * mass

    for g in (0, groups + 1):
        derived(st[AREA, rows_at(g), :], st[MASS, rows_at(g), :], g, slice(0, STRIP))

    def own_rows(j, carry):
        packed = edge[rows_at(j), :]
        packed = packed + pltpu.roll(packed, BS - EDGE_LANES, 1)
        at_zero = pltpu.roll(packed, BS - 2 * EDGE_LANES, 1)
        east = jnp.where(odd, at_zero, packed)
        west = jnp.where(odd, packed, at_zero)
        near = lanes_of((8, BS)) < 64
        beside = [
            jnp.where(
                near,
                pltpu.roll(east, (BS - 3 * f) % BS, 1),
                pltpu.roll(west, 125 - 3 * f, 1),
            )
            for f in range(ICE)
        ]
        rows = rows_at(j)
        for e in range(SLOTS + 1):
            if e == SLOTS:
                fields, lanes = beside, edge_lanes
            else:
                lanes = slot_lanes(e)
                at = slice(e * BS, (e + 1) * BS)
                fields = ice_fields(
                    [vel[n, rows, at] for n in range(2)],
                    [stress[n, rows, at] for n in range(3)],
                    [area[n, rows, at] for n in range(5)],
                    [thick[n, rows, at] for n in range(5)],
                )
                mine = jnp.broadcast_to(e < count, (8, BS))
                fields = [jnp.where(mine, fields[f], beside[f]) for f in range(ICE)]
            for f in range(ICE):
                st[f, rows_at(j + 1), lanes] = fields[f]
            derived(fields[AREA], fields[MASS], j + 1, lanes)
        return carry

    lax.fori_loop(0, groups, own_rows, 0)

    cells = (8, WIDE)
    row = lax.broadcasted_iota(jnp.int32, cells, 0)

    def load(f, g, c, width=WIDE):
        return st[f, rows_at(g), c : c + width]

    def north_of(f, x, g, c):
        return pltpu.roll(jnp.where(row == 0, load(f, g + 1, c), x), 7, 0)

    def south_of(f, x, g, c):
        return pltpu.roll(jnp.where(row == 7, load(f, max(g - 1, 0) if isinstance(g, int) else g - 1, c), x), 1, 0)

    def east_of(f, x, g, c):
        if WIDE == STRIP:
            return pltpu.roll(x, STRIP - 1, 1)
        more = load(f, g, (c + WIDE) % STRIP, BS)
        return pltpu.roll(jnp.concatenate([x, more], axis=1), WIDE + BS - 1, 1)[:, :WIDE]

    def west_of(f, x, g, c):
        if WIDE == STRIP:
            return pltpu.roll(x, 1, 1)
        more = load(f, g, (c - BS) % STRIP, BS)
        return pltpu.roll(jnp.concatenate([more, x], axis=1), 1, 1)[:, BS:]

    def stress_rows(g, last):
        for c in range(0, STRIP, WIDE):
            u, v = load(U, g, c), load(V, g, c)
            exx = east_of(U, u, g, c) - u
            eyy = north_of(V, v, g, c) - v
            shr = (north_of(U, u, g, c) - u) + (east_of(V, v, g, c) - v)
            div = exx + eyy
            ten = exx - eyy
            square = div * div + 0.25 * (ten * ten + shr * shr) + DMIN_SQ
            sixth = load(STR, g, c)
            half = sixth * lax.rsqrt(square)
            eighth = 0.25 * half
            both = half * div - sixth
            apart = eighth * ten
            sxx = (2.0 / 3.0) * load(SXX, g, c) + (both + apart)
            syy = (2.0 / 3.0) * load(SYY, g, c) + (both - apart)
            at = slice(c, c + WIDE)
            st[SXX, rows_at(g), at] = sxx
            st[SYY, rows_at(g), at] = syy
            st[S12, rows_at(g), at] = (2.0 / 3.0) * load(S12, g, c) + eighth * shr
            if last:
                st[STR, rows_at(g), at] = sxx + syy
                st[S2_OUT, rows_at(g), at] = sxx - syy

    def velocity_rows(g, beyond=None, last=False):
        for c in range(0, STRIP, WIDE):
            sxx, syy, s12 = load(SXX, g, c), load(SYY, g, c), load(S12, g, c)
            fx = sxx - west_of(SXX, sxx, g, c) + s12 - south_of(S12, s12, g, c)
            fy = s12 - west_of(S12, s12, g, c) + syy - south_of(SYY, syy, g, c)
            u, v, uo, vo = [load(f, g, c) for f in (U, V, UO, VO)]
            m, conc, tx, ty = [load(f, g, c) for f in (MASS, AREA, TX, TY)]
            du, dv = uo - u, vo - v
            square = du * du + dv * dv + SPEED_SQ
            drag = conc * (square * lax.rsqrt(square))
            d = m + drag
            q = load(TURN, g, c)
            ru = m * u + fx + tx + drag * uo
            rv = m * v + fy + ty + drag * vo
            inv = 1.0 / (d * d + q * q)
            u = (d * ru + q * rv) * inv
            v = (d * rv - q * ru) * inv
            if beyond is not None:
                mask = jnp.broadcast_to(beyond, cells)
                u = jnp.where(mask, 0.0, u)
                v = jnp.where(mask, 0.0, v)
            at = slice(c, c + WIDE)
            st[U, rows_at(g), at] = u
            st[V, rows_at(g), at] = v
            if last:
                du, dv = u - uo, v - vo
                square = du * du + dv * dv + SPEED_SQ
                drag = conc * (square * lax.rsqrt(square))
                x = (1.0 - conc) * tx + drag * du
                y = (1.0 - conc) * ty + drag * dv
                for i in range(WIDE // BS):
                    p = c // BS + i
                    if p < SLOTS:
                        slot = jnp.where(odd, SLOTS - 1 - p, p)
                        pair = [x[:, i * BS : (i + 1) * BS], y[:, i * BS : (i + 1) * BS]]
                        handed[g - 1, pl.ds(pl.multiple_of(slot * 16, 16), 16), :] = (
                            jnp.concatenate(pair, axis=0).astype(BF16)
                        )

    def copies(fields, out, row0, rows, sem0):
        made = []
        for n, f in enumerate(fields):
            for e in range(SLOTS):
                to = out.at[n, pl.ds(row0, rows), pl.ds(e * BS, BS)]
                sem = sems.at[sem0 + n * SLOTS + e]
                block = st.at[f, pl.ds(TOP + row0, rows), slot_lanes(e)]
                made.append((e, pltpu.make_async_copy(block, to, sem),
                             pltpu.make_async_copy(empty.at[pl.ds(0, rows), :], to, sem)))
        return made

    def start(made):
        for e, full, none in made:
            @pl.when(e < count)
            def _():
                full.start()

            @pl.when(e >= count)
            def _():
                none.start()

    pending = []
    for it in range(ITERS):
        last = it == ITERS - 1

        def stress_step(g, carry):
            stress_rows(g, last)
            return carry

        lax.fori_loop(0, groups + (1 if last else 2), stress_step, 0)
        if last:
            made = copies((STR, S2_OUT, S12), stress_out, 0, BS, 0)
            start(made)
            pending += made
        else:
            velocity_rows(0, band == 0)
            velocity_rows(groups + 1, band == NLAT - 1)

        def velocity_step(g, carry):
            velocity_rows(g, None, last)
            return carry

        if last:
            for h in range(2):
                lax.fori_loop(1 + h * groups // 2, 1 + (h + 1) * groups // 2, velocity_step, 0)
                made = copies((U, V), vel_out, h * BS // 2, BS // 2, 24 + 16 * h)
                start(made)
                pending += made
        else:
            lax.fori_loop(1, groups + 1, velocity_step, 0)
    for _, full, _ in pending:
        full.wait()


def dynamics(lens, place, vel, stress, area, thick, got, coriolis):
    width = SLOTS * BS
    vmem = pl.BlockSpec(memory_space=pltpu.VMEM)
    smem = pl.BlockSpec(memory_space=pltpu.SMEM)
    return pl.pallas_call(
        dynamics_kernel,
        in_specs=[smem, smem] + [vmem] * 6,
        out_specs=[pl.BlockSpec(memory_space=pl.ANY)] * 2 + [vmem],
        scratch_shapes=[
            pltpu.VMEM((14, ROWS + 8, STRIP), F32),
            pltpu.VMEM((BS, BS), F32),
            pltpu.VMEM((BS, BS), F32),
            pltpu.SemaphoreType.DMA((24 + 32,)),
        ],
        out_shape=[
            jax.ShapeDtypeStruct((2, BS, width), F32),
            jax.ShapeDtypeStruct((3, BS, width), F32),
            jax.ShapeDtypeStruct((NLON, M3_ROWS, BS), BF16),
        ],
        compiler_params=pltpu.CompilerParams(vmem_limit_bytes=32 * 2**20),
        name="dynamics",
    )(lens, place, vel, stress, area, thick, got, coriolis)


def sort_kernel(lens, place, got, out):
    band = place[0]
    odd = lax.rem(band, 2) == 1

    def owner(k, start):
        count = lens[band, k]

        def slot(s, carry):
            at = start + s
            out[jnp.where(odd, NBB - 1 - at, at)] = got[k * SLOTS + s]
            return carry

        lax.fori_loop(0, count, slot, 0)
        return start + count

    lax.fori_loop(0, NLON, owner, 0)


def sort_back(lens, place, got):
    return pl.pallas_call(
        sort_kernel,
        out_shape=jax.ShapeDtypeStruct((NBB, 16, BS), BF16),
        in_specs=[pl.BlockSpec(memory_space=pltpu.SMEM)] * 2
        + [pl.BlockSpec(memory_space=pltpu.VMEM)],
        out_specs=pl.BlockSpec(memory_space=pltpu.VMEM),
        name="sort_back",
    )(lens, place, got)


def settle_kernel(got, out):
    def rows16(pair, carry):
        rows = pl.ds(pl.multiple_of(pair * 16, 16), 16)
        for cb in range(TILE):
            a = got[2 * pair, cb * 16 : (cb + 1) * 16, :].astype(F32)
            b = got[2 * pair + 1, cb * 16 : (cb + 1) * 16, :].astype(F32)
            lanes = slice(cb * BS, (cb + 1) * BS)
            out[0, rows, lanes] = jnp.concatenate([a[0:8], b[0:8]], axis=0).astype(BF16)
            out[1, rows, lanes] = jnp.concatenate([a[8:16], b[8:16]], axis=0).astype(BF16)
        return carry

    lax.fori_loop(0, BS // 16, rows16, 0)


def settle(got):
    return pl.pallas_call(
        settle_kernel,
        out_shape=jax.ShapeDtypeStruct((2, BS, TILE * BS), BF16),
        in_specs=[pl.BlockSpec(memory_space=pltpu.VMEM)],
        out_specs=pl.BlockSpec(memory_space=pltpu.VMEM),
        name="settle",
    )(got)


def to_all(block):
    return lax.all_to_all(block, "lon", 0, 0, tiled=True)


def body(ocean_forcing, ice_velocity, ice_stress, cat_area, cat_thick, run_lengths):
    band_idx = lax.axis_index("lat")
    lon_idx = lax.axis_index("lon")
    lens = run_lengths
    place = jnp.stack([band_idx, lon_idx]).astype(jnp.int32)
    ice = (ice_velocity, ice_stress, cat_area, cat_thick)
    rows = (band_idx * BS + jnp.arange(-TOP, BS + TOP, dtype=jnp.int32)).astype(F32)
    latitude = -78.0 + 168.0 * (rows + 0.5) / (BS * NLAT)
    coriolis = jnp.broadcast_to(jnp.sin(latitude * (jnp.pi / 180.0))[:, None], (ROWS, BS))
    to_south, to_north, edges = make_edges(lens, place, *ice, ocean_forcing)
    north = lax.ppermute(to_south, "lat", [(b, b - 1) for b in range(1, NLAT)])
    south = lax.ppermute(to_north, "lat", [(b, b + 1) for b in range(NLAT - 1)])
    north, south, coriolis = lax.optimization_barrier((north, south, coriolis))
    message = spread(ocean_forcing, north, south, edges)
    dealt = to_all(deal(lens, place, to_all(message)))
    velocity_out, stress_out, handed = dynamics(lens, place, *ice, dealt, coriolis)
    handed = to_all(handed).reshape(NLON * SLOTS, 16, BS)
    back = sort_back(lens, place, handed).reshape(NLON, M4_ROWS, BS)
    return (velocity_out, stress_out, settle(to_all(back)))


def solution(mesh):
    slots = P(None, None, ("lat", "lon"))
    grid = P(None, "lat", "lon")
    return jax.shard_map(
        body,
        mesh=mesh,
        in_specs=(grid, slots, slots, slots, slots, P()),
        out_specs=(slots, slots, grid),
        check_vma=False,
    )
```

time: 130 us -> 118 us (0.908)
  the two profiles are of different devices: /device:TPU:0 before, /device:TPU:8 now
where the time goes in v2:
time: 118 us; the launch traced here: 116 us
  blocking collectives  71.9 us (61%)
  Pallas kernels  33.4 us (28%)
  starting transfers between devices  4.31 us (4%)
  waiting for transfers between devices  4.03 us (3%)
    all_to_all x4, blocking collectives, to_all(): return lax.all_to_all(block, 'lon', 0, 0, tiled=True)  71.9 us
    pallas_call x1, Pallas kernels, dynamics(): pl.pallas_call(dynamics_kernel, in_specs=[smem, smem] + [vmem] * 6, out_s...  20.5 us
    pallas_call x1, Pallas kernels, deal(): pl.pallas_call(deal_kernel, out_shape=jax.ShapeDtypeStruct((NLON, M2_ROWS...  4.43 us
    pallas_call x1, Pallas kernels, make_edges(): pl.pallas_call(edges_kernel, grid_spec=pltpu.PrefetchScalarGridSpec(num_s...  3.96 us
    ppermute x1, waiting for transfers between devices, body(): south = lax.ppermute(to_north, 'lat', [(b, b + 1) for b in range(NLAT - 1)])  3.68 us
    ppermute x1, starting transfers between devices, body(): south = lax.ppermute(to_north, 'lat', [(b, b + 1) for b in range(NLAT - 1)])  2.41 us
    pallas_call x1, Pallas kernels, sort_back(): pl.pallas_call(sort_kernel, out_shape=jax.ShapeDtypeStruct((NBB, 16, BS),...  2.41 us
  transfers between devices with their start and end apart: 2, of which 2 were waited for; matrix products, arithmetic and copies ran while one was open for 0% of the time, Pallas kernels for 0%

profile of v2, /device:TPU:8, one launch (start us, length us, event | category | flops | bytes accessed | tf_op | source)
XLA Modules:
  0.0 115.9 jit_solution(10014302278410686685)
XLA Ops:
  0.6 0.6 pad_add_fusion.place
  1.3 0.0 copy-start.4
  1.3 4.0 %edges.1 = (f32[32,1024]{1,0:T(8,128)}, f32[32,1024]{1,0:T(8,128)}, f32[128,128]{1,0:T(8,128)}) custom-call(s32[8,16]{1,0:T(8,128)} %lens.7, s32[2]{0:T(128)} %pad_add_fusion.place, f32[2,128,1024]{2,1,0:T(8,128)} %vel.1, f32[2,128,1024]{2,1,0:T(8,128)} %vel.1, f32[2,128,1024]{2,1,0:T(8,128)} %vel.1, f32[2,128,1024]{2,1,0:T(8,128)} %vel.1, ...), custom_call_target="tpu_custom_call" | custom-call | tf_op jit(solution)/shard_map/edges/pallas_call | solution.py:107
  5.2 1.9 %collective-permute-start = (f32[32,1024]{1,0:T(8,128)}, f32[32,1024]{1,0:T(8,128)S(1)}, u32[]{:S(2)}, u32[]{:S(2)}) collective-permute-start(f32[32,1024]{1,0:T(8,128)} %get-tuple-element.12), channel_id=1, source_target_pairs={{16,0},{32,16},{48,32},{64,48},{80,64},{96,80},{112,96},{17,1},{33... | collective-permute-start | bytes 393224 | tf_op jit(solution)/shard_map/ppermute | solution.py:570
  7.1 2.4 %collective-permute-start.1 = (f32[32,1024]{1,0:T(8,128)}, f32[32,1024]{1,0:T(8,128)S(1)}, u32[]{:S(2)}, u32[]{:S(2)}) collective-permute-start(f32[32,1024]{1,0:T(8,128)} %get-tuple-element.13), channel_id=1, source_target_pairs={{0,16},{16,32},{32,48},{48,64},{64,80},{80,96},{96,112},{1,17},{17... | collective-permute-start | bytes 393224 | tf_op jit(solution)/shard_map/ppermute | solution.py:571
  9.6 0.3 collective-permute-done.north
  9.9 3.7 %collective-permute-done.1.south = f32[32,1024]{1,0:T(8,128)S(1)} collective-permute-done((f32[32,1024]{1,0:T(8,128)}, f32[32,1024]{1,0:T(8,128)S(1)}, u32[]{:S(2)}, u32[]{:S(2)}) %collective-permute-start.1) | collective-permute-done | bytes 131104 | tf_op jit(solution)/shard_map/ppermute | solution.py:571
  13.6 0.1 broadcast_in_dim.2.coriolis
  13.7 0.0 copy-done.4
  13.7 0.0 copy-start.6
  13.7 0.8 copy-done.6
  14.6 0.0 copy-start.5
  14.6 0.0 copy-start.7
  14.6 0.0 copy-start.3
  14.6 0.4 spread.1
  14.9 0.0 copy-start.2
  14.9 21.7 %all_to_all.20.got = bf16[16,192,128]{2,1,0:T(8,128)(2,1)S(1)} all-to-all(bf16[16,192,128]{2,1,0:T(8,128)(2,1)S(1)} %spread.1), channel_id=1, replica_groups=mesh['lat'=8,'lon'=16] {'lon'}, dimensions={0} | all-to-all | bytes 1572864 | tf_op jit(solution)/shard_map/all_to_all | solution.py:557
  36.6 0.0 copy-done.5
  36.6 0.0 copy-done.7
  36.6 0.0 copy-start.1
  36.6 4.4 %deal.1 = bf16[16,368,128]{2,1,0:T(8,128)(2,1)S(1)} custom-call(s32[8,16]{1,0:T(8,128)S(1)} %copy-done.5, s32[2]{0:T(128)S(1)} %copy-done.7, bf16[16,192,128]{2,1,0:T(8,128)(2,1)S(1)} %all_to_all.20.got), custom_call_target="tpu_custom_call" | custom-call | tf_op jit(solution)/shard_map/deal/pallas_call | solution.py:234
  41.0 0.0 copy-start
  41.1 23.9 %all_to_all.21.got = bf16[16,368,128]{2,1,0:T(8,128)(2,1)S(1)} all-to-all(bf16[16,368,128]{2,1,0:T(8,128)(2,1)S(1)} %deal.1), channel_id=1, replica_groups=mesh['lat'=8,'lon'=16] {'lon'}, dimensions={0} | all-to-all | bytes 3014656 | tf_op jit(solution)/shard_map/all_to_all | solution.py:557
  65.0 0.0 copy-done.3
  65.0 0.0 copy-done.2
  65.0 0.0 copy-done.1
  65.0 0.0 copy-done
  65.0 20.5 %dynamics.1 = (f32[2,128,1024]{2,1,0:T(8,128)}, f32[3,128,1024]{2,1,0:T(8,128)}, bf16[16,128,128]{2,1,0:T(8,128)(2,1)S(1)}) custom-call(s32[8,16]{1,0:T(8,128)S(1)} %copy-done.5, s32[2]{0:T(128)S(1)} %copy-done.7, f32[2,128,1024]{2,1,0:T(8,128)S(1)} %copy-done.3, f32[3,128,1024]{2,1,0:T(8,128)S(1)} %copy-done.2, f32[5,128,1024]{2,1,0:T(8,128)S(1)} %copy-done, ...), custom_call_target="tpu_custom_call" | custom-call | tf_op jit(solution)/shard_map/dynamics/pallas_call | solution.py:483
  85.5 13.4 %all_to_all.22 = bf16[16,128,128]{2,1,0:T(8,128)(2,1)} all-to-all(bf16[16,128,128]{2,1,0:T(8,128)(2,1)S(1)} %get-tuple-element.20), channel_id=1, replica_groups=mesh['lat'=8,'lon'=16] {'lon'}, dimensions={0} | all-to-all | bytes 1048576 | tf_op jit(solution)/shard_map/all_to_all | solution.py:557
  98.9 2.4 %sort_back.1 = bf16[64,16,128]{2,1,0:T(8,128)(2,1)} custom-call(s32[8,16]{1,0:T(8,128)} %lens.7, s32[2]{0:T(128)} %pad_add_fusion.place, bf16[128,16,128]{2,1,0:T(8,128)(2,1)} %bitcast.4), custom_call_target="tpu_custom_call" | custom-call | tf_op jit(solution)/shard_map/sort_back/pallas_call | solution.py:522
  101.3 12.9 %all_to_all.23.got = bf16[16,64,128]{2,1,0:T(8,128)(2,1)} all-to-all(bf16[16,64,128]{2,1,0:T(8,128)(2,1)} %bitcast.5), channel_id=1, replica_groups=mesh['lat'=8,'lon'=16] {'lon'}, dimensions={0} | all-to-all | bytes 524288 | tf_op jit(solution)/shard_map/all_to_all | solution.py:557
  114.2 1.7 %settle.1 = bf16[2,128,512]{2,1,0:T(8,128)(2,1)} custom-call(bf16[16,64,128]{2,1,0:T(8,128)(2,1)} %all_to_all.23.got), custom_call_target="tpu_custom_call" | custom-call | tf_op jit(solution)/shard_map/settle/pallas_call | solution.py:547
  (1 shorter events, 0.0 us)
Async XLA Ops:
  1.3 12.5 %copy-start.4 = (bf16[4,128,512]{2,1,0:T(8,128)(2,1)S(1)}, bf16[4,128,512]{2,1,0:T(8,128)(2,1)}, u32[]{:S(2)}) copy-start(bf16[4,128,512]{2,1,0:T(8,128)(2,1)} %forcing.1) | copy-start | bytes 1572868
  5.2 4.7 %collective-permute-start = (f32[32,1024]{1,0:T(8,128)}, f32[32,1024]{1,0:T(8,128)S(1)}, u32[]{:S(2)}, u32[]{:S(2)}) collective-permute-start(f32[32,1024]{1,0:T(8,128)} %get-tuple-element.12), channel_id=1, source_target_pairs={{16,0},{32,16},{48,32},{64,48},{80,64},{96,80},{112,96},{17,1},{33... | collective-permute-start | bytes 393224 | tf_op jit(solution)/shard_map/ppermute | solution.py:570
  7.1 6.5 %collective-permute-start.1 = (f32[32,1024]{1,0:T(8,128)}, f32[32,1024]{1,0:T(8,128)S(1)}, u32[]{:S(2)}, u32[]{:S(2)}) collective-permute-start(f32[32,1024]{1,0:T(8,128)} %get-tuple-element.13), channel_id=1, source_target_pairs={{0,16},{16,32},{32,48},{48,64},{64,80},{80,96},{96,112},{1,17},{17... | collective-permute-start | bytes 393224 | tf_op jit(solution)/shard_map/ppermute | solution.py:571
  13.7 0.8 copy-start.6
  14.6 22.0 %copy-start.5 = (s32[8,16]{1,0:T(8,128)S(1)}, s32[8,16]{1,0:T(8,128)}, u32[]{:S(2)}) copy-start(s32[8,16]{1,0:T(8,128)} %lens.7) | copy-start | bytes 1540
  14.6 22.0 %copy-start.7 = (s32[2]{0:T(128)S(1)}, s32[2]{0:T(128)}, u32[]{:S(2)}) copy-start(s32[2]{0:T(128)} %pad_add_fusion.place) | copy-start | bytes 28
  14.6 50.4 %copy-start.3 = (f32[2,128,1024]{2,1,0:T(8,128)S(1)}, f32[2,128,1024]{2,1,0:T(8,128)}, u32[]{:S(2)}) copy-start(f32[2,128,1024]{2,1,0:T(8,128)} %vel.1) | copy-start | bytes 3145732
  14.9 50.1 %copy-start.2 = (f32[3,128,1024]{2,1,0:T(8,128)S(1)}, f32[3,128,1024]{2,1,0:T(8,128)}, u32[]{:S(2)}) copy-start(f32[3,128,1024]{2,1,0:T(8,128)} %stress.1) | copy-start | bytes 4718596
  36.6 28.4 %copy-start.1 = (f32[5,128,1024]{2,1,0:T(8,128)S(1)}, f32[5,128,1024]{2,1,0:T(8,128)}, u32[]{:S(2)}) copy-start(f32[5,128,1024]{2,1,0:T(8,128)} %thick.1) | copy-start | bytes 7864324
  41.0 24.0 %copy-start = (f32[5,128,1024]{2,1,0:T(8,128)S(1)}, f32[5,128,1024]{2,1,0:T(8,128)}, u32[]{:S(2)}) copy-start(f32[5,128,1024]{2,1,0:T(8,128)} %area.1) | copy-start | bytes 7864324

commit v3 on v2

--- a/solution.py
+++ b/solution.py
@@ -20,9 +20,11 @@
 DMIN_SQ = 0.01
 SPEED_SQ = 0.01
 ICE = 7
-U, V, SXX, SYY, S12, AREA, MASS, STR, UO, VO, TX, TY, TURN, S2_OUT = range(14)
+U, V, SXX, SYY, S12, AREA, MASS, STR, UO, VO, TX, TY, TURN, S1_OUT, S2_OUT, U_NEW, V_NEW = range(17)
+RENEWED = (U, V, SXX, SYY, S12)
 EDGE_LANES = 3 * ICE
 STRIP = (SLOTS + 1) * BS
+UNROLL = 4
 WIDE = 3 * BS
 TOP = 8
 ROWS = BS + 2 * TOP
@@ -52,10 +54,10 @@
     return (PSTAR / 6.0) * mass * jnp.exp(-CSTAR * (1.0 - conc))
 
 
-def edges_kernel(lens, place, *refs):
+def edges_kernel(lens, band, lon, *refs):
     ice = [refs[4 * i : 4 * i + 4] for i in range(4)]
     f_low, f_high, south, north, packed_out = refs[16:]
-    odd = lax.rem(place[0], 2) == 1
+    odd = lax.rem(band[0], 2) == 1
     for out, which, force, row0, frow0 in (
         (south, 0, f_low, 0, 0),
         (north, 1, f_high, 5, 14),
@@ -84,30 +86,30 @@
     packed_out[...] = packed
 
 
-def make_edges(lens, place, vel, stress, area, thick, forcing):
+def make_edges(lens, band, lon, vel, stress, area, thick, forcing):
     width = SLOTS * BS
 
     def specs(n):
         return [
-            pl.BlockSpec((n, 8, width), lambda i, lens, place: (0, 0, 0)),
-            pl.BlockSpec((n, 8, width), lambda i, lens, place: (0, BS // 8 - 1, 0)),
-            pl.BlockSpec((n, BS, BS), lambda i, lens, place: (0, 0, 0)),
+            pl.BlockSpec((n, 8, width), lambda i, lens, band, lon: (0, 0, 0)),
+            pl.BlockSpec((n, 8, width), lambda i, lens, band, lon: (0, BS // 8 - 1, 0)),
+            pl.BlockSpec((n, BS, BS), lambda i, lens, band, lon: (0, 0, 0)),
             pl.BlockSpec(
                 (n, BS, BS),
-                lambda i, lens, place: (0, 0, lens[place[0], place[1]] - 1),
+                lambda i, lens, band, lon: (0, 0, lens[band[0], lon[0]] - 1),
             ),
         ]
 
     in_specs = specs(2) + specs(3) + specs(5) + specs(5)
     in_specs += [
-        pl.BlockSpec((4, 16, 512), lambda i, lens, place: (0, 0, 0)),
-        pl.BlockSpec((4, 16, 512), lambda i, lens, place: (0, BS // 16 - 1, 0)),
+        pl.BlockSpec((4, 16, 512), lambda i, lens, band, lon: (0, 0, 0)),
+        pl.BlockSpec((4, 16, 512), lambda i, lens, band, lon: (0, BS // 16 - 1, 0)),
     ]
-    whole = lambda i, lens, place: (0, 0)
+    whole = lambda i, lens, band, lon: (0, 0)
     return pl.pallas_call(
         edges_kernel,
         grid_spec=pltpu.PrefetchScalarGridSpec(
-            num_scalar_prefetch=2,
+            num_scalar_prefetch=3,
             grid=(1,),
             in_specs=in_specs,
             out_specs=[
@@ -123,7 +125,7 @@
         ],
         compiler_params=pltpu.CompilerParams(vmem_limit_bytes=60 * 2**20),
         name="edges",
-    )(lens, place, *([vel] * 4), *([stress] * 4), *([area] * 4), *([thick] * 4), forcing, forcing)
+    )(lens, band, lon, *([vel] * 4), *([stress] * 4), *([area] * 4), *([thick] * 4), forcing, forcing)
 
 
 def spread_kernel(forcing, north, south, edges, out, hold):
@@ -173,8 +175,15 @@
     )(forcing, north, south, edges)
 
 
-def deal_kernel(lens, place, got, out, groups, hold, table):
-    band, lon = place[0], place[1]
+def note_slots(table, k, count, start, odd):
+    for s in range(SLOTS):
+        at = start + s
+        column = jnp.where(odd, NBB - 1 - at, at)
+        table[jnp.where(s < count, column, NBB)] = k * SLOTS + s
+
+
+def deal_kernel(lens, band, lon, got, out, groups, hold, table):
+    band, lon = band[0], lon[0]
     odd = lax.rem(band, 2) == 1
     other = jnp.where(lon < 8, jnp.minimum(band + 1, NLAT - 1), jnp.maximum(band - 1, 0))
     other_odd = lax.rem(other, 2) == 1
@@ -183,17 +192,10 @@
         groups[pl.ds(pl.multiple_of(l * SLOTS, SLOTS), SLOTS)] = (
             got[l, TILE * 32 :, :].astype(F32).reshape(SLOTS, 8, BS)
         )
-        count = lens[other, l]
-
-        def slot(s, carry):
-            at = start + s
-            table[jnp.where(other_odd, NBB - 1 - at, at)] = l * SLOTS + s
-            return carry
-
-        lax.fori_loop(0, count, slot, 0)
-        return start + count
-
-    lax.fori_loop(0, NLON, fill, 0)
+        note_slots(table, l, lens[other, l], start, other_odd)
+        return start + lens[other, l]
+
+    lax.fori_loop(0, NLON, fill, 0, unroll=UNROLL)
     lane32 = lanes_of((32, BS)) < 64
     lane8 = lanes_of((8, BS)) < 64
     row6 = lax.broadcasted_iota(jnp.int32, (8, BS), 0) == 6
@@ -227,31 +229,32 @@
         out[k, (SLOTS + 1) * 32 :, :] = hold[...].astype(BF16)
         return start + count
 
-    lax.fori_loop(0, NLON, owner, 0)
-
-
-def deal(lens, place, got):
+    lax.fori_loop(0, NLON, owner, 0, unroll=2)
+
+
+def deal(lens, band, lon, got):
     return pl.pallas_call(
         deal_kernel,
         out_shape=jax.ShapeDtypeStruct((NLON, M2_ROWS, BS), BF16),
-        in_specs=[pl.BlockSpec(memory_space=pltpu.SMEM)] * 2
+        in_specs=[pl.BlockSpec(memory_space=pltpu.SMEM)] * 3
         + [pl.BlockSpec(memory_space=pltpu.VMEM)],
         out_specs=pl.BlockSpec(memory_space=pltpu.VMEM),
         scratch_shapes=[
             pltpu.VMEM((NLON * SLOTS, 8, BS), F32),
             pltpu.VMEM((80, BS), F32),
-            pltpu.SMEM((NBB,), jnp.int32),
+            pltpu.SMEM((NBB + 1,), jnp.int32),
         ],
         compiler_params=pltpu.CompilerParams(vmem_limit_bytes=32 * 2**20),
         name="deal",
-    )(lens, place, got)
+    )(lens, band, lon, got)
 
 
 def dynamics_kernel(
-    lens, place, vel, stress, area, thick, got, coriolis,
-    vel_out, stress_out, handed, st, edge, empty, sems,
+    lens, band, lon, vel, stress, area, thick, got, coriolis,
+    vel_out, stress_out, handed, *scratch,
 ):
-    band, lon = place[0], place[1]
+    fields_at, (edge, empty, sems) = list(scratch[:-3]), scratch[-3:]
+    band, lon = band[0], lon[0]
     odd = lax.rem(band, 2) == 1
     count = lens[band, lon]
     groups = BS // 8
@@ -270,33 +273,35 @@
             rows = got[j, e * 32 : (e + 1) * 32, :].astype(F32)
             lanes = slot_lanes(e) if e < SLOTS else edge_lanes
             for f in range(4):
-                st[UO + f, rows_at(j + 1), lanes] = rows[f * 8 : (f + 1) * 8, :]
+                fields_at[UO + f][rows_at(j + 1), lanes] = rows[f * 8 : (f + 1) * 8, :]
         edge[rows_at(j), :] = got[j, M2_ROWS - 16 :, :].astype(F32)[8:16, :]
         return carry
 
     lax.fori_loop(0, NLON, arrived, 0)
     for j in range(NLON):
-        group = got[j, (SLOTS + 1) * 32 :, :].astype(F32)
+        group = got[j, (SLOTS + 1) * 32 :, :].astype(F32)[0 : 8 * (SLOTS + 1), :]
+        group = group.reshape(SLOTS + 1, 8, BS)
+        whole = group + pltpu.roll(group, 5, 1)
+        if j >= 8:
+            whole = pltpu.roll(whole, 5, 1)
         f = j % 8
-        row0 = TOP + BS if j < 8 else TOP - DEEP
+        g = groups + 1 if j < 8 else 0
         force_row = (TOP - 2, TOP - 1, TOP + BS, TOP + BS + 1)[j % 4]
         for e in range(SLOTS + 1):
             lanes = slot_lanes(e) if e < SLOTS else edge_lanes
             if f < ICE:
-                st[f, row0 : row0 + DEEP, lanes] = (
-                    group[8 * e : 8 * e + 3, :] + group[8 * e + 3 : 8 * e + 6, :]
-                )
-            st[UO + j // 4, force_row : force_row + 1, lanes] = group[8 * e + 6 : 8 * e + 7, :]
+                fields_at[f][rows_at(g), lanes] = whole[e]
+            fields_at[UO + j // 4][force_row : force_row + 1, lanes] = group[e, 6:7, :]
 
     def derived(conc, mass, g, lanes):
         turn = coriolis[rows_at(g), :]
         if conc.shape[1] > BS:
             turn = jnp.concatenate([turn] * (conc.shape[1] // BS), axis=1)
-        st[STR, rows_at(g), lanes] = strength_of(conc, mass)
-        st[TURN, rows_at(g), lanes] = turn * mass
+        fields_at[STR][rows_at(g), lanes] = strength_of(conc, mass)
+        fields_at[TURN][rows_at(g), lanes] = turn * mass
 
     for g in (0, groups + 1):
-        derived(st[AREA, rows_at(g), :], st[MASS, rows_at(g), :], g, slice(0, STRIP))
+        derived(fields_at[AREA][rows_at(g), :], fields_at[MASS][rows_at(g), :], g, slice(0, STRIP))
 
     def own_rows(j, carry):
         packed = edge[rows_at(j), :]
@@ -329,17 +334,17 @@
                 mine = jnp.broadcast_to(e < count, (8, BS))
                 fields = [jnp.where(mine, fields[f], beside[f]) for f in range(ICE)]
             for f in range(ICE):
-                st[f, rows_at(j + 1), lanes] = fields[f]
+                fields_at[f][rows_at(j + 1), lanes] = fields[f]
             derived(fields[AREA], fields[MASS], j + 1, lanes)
         return carry
 
-    lax.fori_loop(0, groups, own_rows, 0)
+    lax.fori_loop(0, groups, own_rows, 0, unroll=UNROLL)
 
     cells = (8, WIDE)
     row = lax.broadcasted_iota(jnp.int32, cells, 0)
 
     def load(f, g, c, width=WIDE):
-        return st[f, rows_at(g), c : c + width]
+        return fields_at[f][rows_at(g), c : c + width]
 
     def north_of(f, x, g, c):
         return pltpu.roll(jnp.where(row == 0, load(f, g + 1, c), x), 7, 0)
@@ -359,7 +364,7 @@
         more = load(f, g, (c - BS) % STRIP, BS)
         return pltpu.roll(jnp.concatenate([more, x], axis=1), 1, 1)[:, BS:]
 
-    def stress_rows(g, last):
+    def stress_rows(g, new, last):
         for c in range(0, STRIP, WIDE):
             u, v = load(U, g, c), load(V, g, c)
             exx = east_of(U, u, g, c) - u
@@ -376,14 +381,14 @@
             sxx = (2.0 / 3.0) * load(SXX, g, c) + (both + apart)
             syy = (2.0 / 3.0) * load(SYY, g, c) + (both - apart)
             at = slice(c, c + WIDE)
-            st[SXX, rows_at(g), at] = sxx
-            st[SYY, rows_at(g), at] = syy
-            st[S12, rows_at(g), at] = (2.0 / 3.0) * load(S12, g, c) + eighth * shr
+            new[SXX][rows_at(g), at] = sxx
+            new[SYY][rows_at(g), at] = syy
+            new[S12][rows_at(g), at] = (2.0 / 3.0) * load(S12, g, c) + eighth * shr
             if last:
-                st[STR, rows_at(g), at] = sxx + syy
-                st[S2_OUT, rows_at(g), at] = sxx - syy
-
-    def velocity_rows(g, beyond=None, last=False):
+                new[S1_OUT][rows_at(g), at] = sxx + syy
+                new[S2_OUT][rows_at(g), at] = sxx - syy
+
+    def velocity_rows(g, new, beyond=None, last=False):
         for c in range(0, STRIP, WIDE):
             sxx, syy, s12 = load(SXX, g, c), load(SYY, g, c), load(S12, g, c)
             fx = sxx - west_of(SXX, sxx, g, c) + s12 - south_of(S12, s12, g, c)
@@ -405,8 +410,8 @@
                 u = jnp.where(mask, 0.0, u)
                 v = jnp.where(mask, 0.0, v)
             at = slice(c, c + WIDE)
-            st[U, rows_at(g), at] = u
-            st[V, rows_at(g), at] = v
+            new[U][rows_at(g), at] = u
+            new[V][rows_at(g), at] = v
             if last:
                 du, dv = u - uo, v - vo
                 square = du * du + dv * dv + SPEED_SQ
@@ -428,7 +433,7 @@
             for e in range(SLOTS):
                 to = out.at[n, pl.ds(row0, rows), pl.ds(e * BS, BS)]
                 sem = sems.at[sem0 + n * SLOTS + e]
-                block = st.at[f, pl.ds(TOP + row0, rows), slot_lanes(e)]
+                block = fields_at[f].at[pl.ds(TOP + row0, rows), slot_lanes(e)]
                 made.append((e, pltpu.make_async_copy(block, to, sem),
                              pltpu.make_async_copy(empty.at[pl.ds(0, rows), :], to, sem)))
         return made
@@ -446,46 +451,55 @@
     pending = []
     for it in range(ITERS):
         last = it == ITERS - 1
+        new = {f: fields_at[n] for f, n in zip(RENEWED, range(S2_OUT + 1, S2_OUT + 6))}
+        new[S1_OUT], new[S2_OUT] = fields_at[S1_OUT], fields_at[S2_OUT]
 
         def stress_step(g, carry):
-            stress_rows(g, last)
+            stress_rows(g, new, last)
             return carry
 
-        lax.fori_loop(0, groups + (1 if last else 2), stress_step, 0)
+        lax.fori_loop(0, groups + (1 if last else 2), stress_step, 0, unroll=UNROLL)
+        for f in (SXX, SYY, S12):
+            n = S2_OUT + 1 + RENEWED.index(f)
+            fields_at[f], fields_at[n] = fields_at[n], fields_at[f]
         if last:
-            made = copies((STR, S2_OUT, S12), stress_out, 0, BS, 0)
+            made = copies((S1_OUT, S2_OUT, S12), stress_out, 0, BS, 0)
             start(made)
             pending += made
         else:
-            velocity_rows(0, band == 0)
-            velocity_rows(groups + 1, band == NLAT - 1)
+            velocity_rows(0, new, band == 0)
+            velocity_rows(groups + 1, new, band == NLAT - 1)
 
         def velocity_step(g, carry):
-            velocity_rows(g, None, last)
+            velocity_rows(g, new, None, last)
             return carry
 
         if last:
             for h in range(2):
-                lax.fori_loop(1 + h * groups // 2, 1 + (h + 1) * groups // 2, velocity_step, 0)
-                made = copies((U, V), vel_out, h * BS // 2, BS // 2, 24 + 16 * h)
+                half = groups // 2
+                lax.fori_loop(1 + h * half, 1 + (h + 1) * half, velocity_step, 0, unroll=UNROLL)
+                made = copies((U_NEW, V_NEW), vel_out, h * BS // 2, BS // 2, 24 + 16 * h)
                 start(made)
                 pending += made
         else:
-            lax.fori_loop(1, groups + 1, velocity_step, 0)
+            lax.fori_loop(1, groups + 1, velocity_step, 0, unroll=UNROLL)
+            for f in (U, V):
+                n = S2_OUT + 1 + RENEWED.index(f)
+                fields_at[f], fields_at[n] = fields_at[n], fields_at[f]
     for _, full, _ in pending:
         full.wait()
 
 
-def dynamics(lens, place, vel, stress, area, thick, got, coriolis):
+def dynamics(lens, band, lon, vel, stress, area, thick, got, coriolis):
     width = SLOTS * BS
     vmem = pl.BlockSpec(memory_space=pltpu.VMEM)
     smem = pl.BlockSpec(memory_space=pltpu.SMEM)
     return pl.pallas_call(
         dynamics_kernel,
-        in_specs=[smem, smem] + [vmem] * 6,
+        in_specs=[smem] * 3 + [vmem] * 6,
         out_specs=[pl.BlockSpec(memory_space=pl.ANY)] * 2 + [vmem],
         scratch_shapes=[
-            pltpu.VMEM((14, ROWS + 8, STRIP), F32),
+            *[pltpu.VMEM((ROWS + 8, STRIP), F32) for _ in range(S2_OUT + 6)],
             pltpu.VMEM((BS, BS), F32),
             pltpu.VMEM((BS, BS), F32),
             pltpu.SemaphoreType.DMA((24 + 32,)),
@@ -497,36 +511,36 @@
         ],
         compiler_params=pltpu.CompilerParams(vmem_limit_bytes=32 * 2**20),
         name="dynamics",
-    )(lens, place, vel, stress, area, thick, got, coriolis)
-
-
-def sort_kernel(lens, place, got, out):
-    band = place[0]
-    odd = lax.rem(band, 2) == 1
+    )(lens, band, lon, vel, stress, area, thick, got, coriolis)
+
+
+def sort_kernel(lens, band, got, out, table):
+    odd = lax.rem(band[0], 2) == 1
 
     def owner(k, start):
-        count = lens[band, k]
-
-        def slot(s, carry):
-            at = start + s
-            out[jnp.where(odd, NBB - 1 - at, at)] = got[k * SLOTS + s]
-            return carry
-
-        lax.fori_loop(0, count, slot, 0)
-        return start + count
-
-    lax.fori_loop(0, NLON, owner, 0)
-
-
-def sort_back(lens, place, got):
+        note_slots(table, k, lens[band[0], k], start, odd)
+        return start + lens[band[0], k]
+
+    lax.fori_loop(0, NLON, owner, 0, unroll=UNROLL)
+
+    def block(c, carry):
+        out[c] = got[table[c]]
+        return carry
+
+    lax.fori_loop(0, NBB, block, 0, unroll=8)
+
+
+def sort_back(lens, band, got):
     return pl.pallas_call(
         sort_kernel,
         out_shape=jax.ShapeDtypeStruct((NBB, 16, BS), BF16),
         in_specs=[pl.BlockSpec(memory_space=pltpu.SMEM)] * 2
         + [pl.BlockSpec(memory_space=pltpu.VMEM)],
         out_specs=pl.BlockSpec(memory_space=pltpu.VMEM),
+        scratch_shapes=[pltpu.SMEM((NBB + 1,), jnp.int32)],
+        compiler_params=pltpu.CompilerParams(vmem_limit_bytes=16 * 2**20),
         name="sort_back",
-    )(lens, place, got)
+    )(lens, band, got)
 
 
 def settle_kernel(got, out):
@@ -540,7 +554,7 @@
             out[1, rows, lanes] = jnp.concatenate([a[8:16], b[8:16]], axis=0).astype(BF16)
         return carry
 
-    lax.fori_loop(0, BS // 16, rows16, 0)
+    lax.fori_loop(0, BS // 16, rows16, 0, unroll=UNROLL)
 
 
 def settle(got):
@@ -549,6 +563,7 @@
         out_shape=jax.ShapeDtypeStruct((2, BS, TILE * BS), BF16),
         in_specs=[pl.BlockSpec(memory_space=pltpu.VMEM)],
         out_specs=pl.BlockSpec(memory_space=pltpu.VMEM),
+        compiler_params=pltpu.CompilerParams(vmem_limit_bytes=16 * 2**20),
         name="settle",
     )(got)
 
@@ -561,20 +576,20 @@
     band_idx = lax.axis_index("lat")
     lon_idx = lax.axis_index("lon")
     lens = run_lengths
-    place = jnp.stack([band_idx, lon_idx]).astype(jnp.int32)
+    place = (jnp.reshape(band_idx, (1,)), jnp.reshape(lon_idx, (1,)))
     ice = (ice_velocity, ice_stress, cat_area, cat_thick)
     rows = (band_idx * BS + jnp.arange(-TOP, BS + TOP, dtype=jnp.int32)).astype(F32)
     latitude = -78.0 + 168.0 * (rows + 0.5) / (BS * NLAT)
     coriolis = jnp.broadcast_to(jnp.sin(latitude * (jnp.pi / 180.0))[:, None], (ROWS, BS))
-    to_south, to_north, edges = make_edges(lens, place, *ice, ocean_forcing)
+    to_south, to_north, edges = make_edges(lens, *place, *ice, ocean_forcing)
     north = lax.ppermute(to_south, "lat", [(b, b - 1) for b in range(1, NLAT)])
     south = lax.ppermute(to_north, "lat", [(b, b + 1) for b in range(NLAT - 1)])
     north, south, coriolis = lax.optimization_barrier((north, south, coriolis))
     message = spread(ocean_forcing, north, south, edges)
-    dealt = to_all(deal(lens, place, to_all(message)))
-    velocity_out, stress_out, handed = dynamics(lens, place, *ice, dealt, coriolis)
+    dealt = to_all(deal(lens, *place, to_all(message)))
+    velocity_out, stress_out, handed = dynamics(lens, *place, *ice, dealt, coriolis)
     handed = to_all(handed).reshape(NLON * SLOTS, 16, BS)
-    back = sort_back(lens, place, handed).reshape(NLON, M4_ROWS, BS)
+    back = sort_back(lens, place[0], handed).reshape(NLON, M4_ROWS, BS)
     return (velocity_out, stress_out, settle(to_all(back)))
 
 

time: 118 us -> 104 us (0.88)
  Pallas kernels: 33.4 us -> 22.2 us
  blocking collectives: 71.9 us -> 70.2 us
    pallas_call x1, Pallas kernels: 20.5 us -> 11.9 us  [dynamics(): pl.pallas_call(dynamics_kernel, in_specs=[smem] * 3 + [vmem] * 6, out_spe...]
    all_to_all x4, blocking collectives: 71.9 us -> 70.2 us  [to_all(): return lax.all_to_all(block, 'lon', 0, 0, tiled=True)]
    pallas_call x1, Pallas kernels: 2.41 us -> 1.03 us  [sort_back(): pl.pallas_call(sort_kernel, out_shape=jax.ShapeDtypeStruct((NBB, 16, BS),...]
where the time goes in v3:
time: 104 us; the launch traced here: 102 us
  blocking collectives  70.2 us (68%)
  Pallas kernels  22.2 us (21%)
  starting transfers between devices  4.31 us (4%)
  waiting for transfers between devices  4.03 us (4%)
    all_to_all x4, blocking collectives, to_all(): return lax.all_to_all(block, 'lon', 0, 0, tiled=True)  70.2 us
    pallas_call x1, Pallas kernels, dynamics(): pl.pallas_call(dynamics_kernel, in_specs=[smem] * 3 + [vmem] * 6, out_spe...  11.9 us
    pallas_call x1, Pallas kernels, deal(): pl.pallas_call(deal_kernel, out_shape=jax.ShapeDtypeStruct((NLON, M2_ROWS...  4.13 us
    pallas_call x1, Pallas kernels, make_edges(): pl.pallas_call(edges_kernel, grid_spec=pltpu.PrefetchScalarGridSpec(num_s...  4 us
    ppermute x1, waiting for transfers between devices, body(): south = lax.ppermute(to_north, 'lat', [(b, b + 1) for b in range(NLAT - 1)])  3.68 us
    ppermute x1, starting transfers between devices, body(): south = lax.ppermute(to_north, 'lat', [(b, b + 1) for b in range(NLAT - 1)])  2.41 us
  transfers between devices with their start and end apart: 2, of which 2 were waited for; matrix products, arithmetic and copies ran while one was open for 0% of the time, Pallas kernels for 0%

profile of v3, /device:TPU:8, one launch (start us, length us, event | category | flops | bytes accessed | tf_op | source)
XLA Modules:
  0.0 102.5 jit_solution(1593532252130634828)
XLA Ops:
  0.6 0.0 copy-start.4
  0.6 4.0 %edges.1 = (f32[32,1024]{1,0:T(8,128)}, f32[32,1024]{1,0:T(8,128)}, f32[128,128]{1,0:T(8,128)}) custom-call(s32[8,16]{1,0:T(8,128)} %lens.7, s32[1]{0:T(128)} %bitcast.band, s32[1]{0:T(128)} %bitcast.1.lon, f32[2,128,1024]{2,1,0:T(8,128)} %vel.1, f32[2,128,1024]{2,1,0:T(8,128)} %vel.1, f32[2,128,1024]{2,1,0:T(8,128)} %vel.1, f32[2,128,1024]{2,1,0:T(8,128)} %vel.1, ...), custom_call_target="tpu_custom_call" | custom-call | tf_op jit(solution)/shard_map/edges/pallas_call | solution.py:109
  4.6 1.9 %collective-permute-start = (f32[32,1024]{1,0:T(8,128)}, f32[32,1024]{1,0:T(8,128)S(1)}, u32[]{:S(2)}, u32[]{:S(2)}) collective-permute-start(f32[32,1024]{1,0:T(8,128)} %get-tuple-element.12), channel_id=1, source_target_pairs={{16,0},{32,16},{48,32},{64,48},{80,64},{96,80},{112,96},{17,1},{33... | collective-permute-start | bytes 393224 | tf_op jit(solution)/shard_map/ppermute | solution.py:585
  6.6 2.4 %collective-permute-start.1 = (f32[32,1024]{1,0:T(8,128)}, f32[32,1024]{1,0:T(8,128)S(1)}, u32[]{:S(2)}, u32[]{:S(2)}) collective-permute-start(f32[32,1024]{1,0:T(8,128)} %get-tuple-element.13), channel_id=1, source_target_pairs={{0,16},{16,32},{32,48},{48,64},{64,80},{80,96},{96,112},{1,17},{17... | collective-permute-start | bytes 393224 | tf_op jit(solution)/shard_map/ppermute | solution.py:586
  9.0 0.3 collective-permute-done.north
  9.4 3.7 %collective-permute-done.1.south = f32[32,1024]{1,0:T(8,128)S(1)} collective-permute-done((f32[32,1024]{1,0:T(8,128)}, f32[32,1024]{1,0:T(8,128)S(1)}, u32[]{:S(2)}, u32[]{:S(2)}) %collective-permute-start.1) | collective-permute-done | bytes 131104 | tf_op jit(solution)/shard_map/ppermute | solution.py:586
  13.1 0.1 broadcast_in_dim.2.coriolis
  13.1 0.0 copy-done.4
  13.1 0.0 copy-start.6
  13.2 0.8 copy-done.6
  14.0 0.0 copy-start.5
  14.0 0.0 copy-start.3
  14.0 0.4 spread.1
  14.3 0.0 copy-start.2
  14.4 21.7 %all_to_all.20.got = bf16[16,192,128]{2,1,0:T(8,128)(2,1)S(1)} all-to-all(bf16[16,192,128]{2,1,0:T(8,128)(2,1)S(1)} %spread.1), channel_id=1, replica_groups=mesh['lat'=8,'lon'=16] {'lon'}, dimensions={0} | all-to-all | bytes 1572864 | tf_op jit(solution)/shard_map/all_to_all | solution.py:572
  36.0 0.0 copy-done.5
  36.0 0.0 copy-start.1
  36.0 4.1 %deal.1 = bf16[16,368,128]{2,1,0:T(8,128)(2,1)S(1)} custom-call(s32[8,16]{1,0:T(8,128)S(1)} %copy-done.5, s32[1]{0:T(128)} %bitcast.band, s32[1]{0:T(128)} %bitcast.1.lon, bf16[16,192,128]{2,1,0:T(8,128)(2,1)S(1)} %all_to_all.20.got), custom_call_target="tpu_custom_call" | custom-call | tf_op jit(solution)/shard_map/deal/pallas_call | solution.py:236
  40.2 0.0 copy-start
  40.2 23.9 %all_to_all.21.got = bf16[16,368,128]{2,1,0:T(8,128)(2,1)S(1)} all-to-all(bf16[16,368,128]{2,1,0:T(8,128)(2,1)S(1)} %deal.1), channel_id=1, replica_groups=mesh['lat'=8,'lon'=16] {'lon'}, dimensions={0} | all-to-all | bytes 3014656 | tf_op jit(solution)/shard_map/all_to_all | solution.py:572
  64.1 0.0 copy-done.3
  64.1 0.0 copy-done.2
  64.1 0.0 copy-done.1
  64.1 0.0 copy-done
  64.1 11.9 %dynamics.1 = (f32[2,128,1024]{2,1,0:T(8,128)}, f32[3,128,1024]{2,1,0:T(8,128)}, bf16[16,128,128]{2,1,0:T(8,128)(2,1)S(1)}) custom-call(s32[8,16]{1,0:T(8,128)S(1)} %copy-done.5, s32[1]{0:T(128)} %bitcast.band, s32[1]{0:T(128)} %bitcast.1.lon, f32[2,128,1024]{2,1,0:T(8,128)S(1)} %copy-done.3, f32[3,128,1024]{2,1,0:T(8,128)S(1)} %copy-done.2, ...), custom_call_target="tpu_custom_call" | custom-call | tf_op jit(solution)/shard_map/dynamics/pallas_call | solution.py:497
  76.1 12.9 %all_to_all.22 = bf16[16,128,128]{2,1,0:T(8,128)(2,1)S(1)} all-to-all(bf16[16,128,128]{2,1,0:T(8,128)(2,1)S(1)} %get-tuple-element.20), channel_id=1, replica_groups=mesh['lat'=8,'lon'=16] {'lon'}, dimensions={0} | all-to-all | bytes 1048576 | tf_op jit(solution)/shard_map/all_to_all | solution.py:572
  89.0 1.0 %sort_back.1 = bf16[64,16,128]{2,1,0:T(8,128)(2,1)S(1)} custom-call(s32[8,16]{1,0:T(8,128)S(1)} %copy-done.5, s32[1]{0:T(128)} %bitcast.band, bf16[128,16,128]{2,1,0:T(8,128)(2,1)S(1)} %bitcast.4), custom_call_target="tpu_custom_call" | custom-call | tf_op jit(solution)/shard_map/sort_back/pallas_call | solution.py:534
  90.1 11.6 %all_to_all.23.got = bf16[16,64,128]{2,1,0:T(8,128)(2,1)S(1)} all-to-all(bf16[16,64,128]{2,1,0:T(8,128)(2,1)S(1)} %bitcast.5), channel_id=1, replica_groups=mesh['lat'=8,'lon'=16] {'lon'}, dimensions={0} | all-to-all | bytes 524288 | tf_op jit(solution)/shard_map/all_to_all | solution.py:572
  101.7 0.8 settle.1
  (1 shorter events, 0.0 us)
Async XLA Ops:
  0.6 12.5 %copy-start.4 = (bf16[4,128,512]{2,1,0:T(8,128)(2,1)S(1)}, bf16[4,128,512]{2,1,0:T(8,128)(2,1)}, u32[]{:S(2)}) copy-start(bf16[4,128,512]{2,1,0:T(8,128)(2,1)} %forcing.1) | copy-start | bytes 1572868
  4.6 4.7 %collective-permute-start = (f32[32,1024]{1,0:T(8,128)}, f32[32,1024]{1,0:T(8,128)S(1)}, u32[]{:S(2)}, u32[]{:S(2)}) collective-permute-start(f32[32,1024]{1,0:T(8,128)} %get-tuple-element.12), channel_id=1, source_target_pairs={{16,0},{32,16},{48,32},{64,48},{80,64},{96,80},{112,96},{17,1},{33... | collective-permute-start | bytes 393224 | tf_op jit(solution)/shard_map/ppermute | solution.py:585
  6.6 6.5 %collective-permute-start.1 = (f32[32,1024]{1,0:T(8,128)}, f32[32,1024]{1,0:T(8,128)S(1)}, u32[]{:S(2)}, u32[]{:S(2)}) collective-permute-start(f32[32,1024]{1,0:T(8,128)} %get-tuple-element.13), channel_id=1, source_target_pairs={{0,16},{16,32},{32,48},{48,64},{64,80},{80,96},{96,112},{1,17},{17... | collective-permute-start | bytes 393224 | tf_op jit(solution)/shard_map/ppermute | solution.py:586
  13.1 0.8 copy-start.6
  14.0 22.0 %copy-start.5 = (s32[8,16]{1,0:T(8,128)S(1)}, s32[8,16]{1,0:T(8,128)}, u32[]{:S(2)}) copy-start(s32[8,16]{1,0:T(8,128)} %lens.7) | copy-start | bytes 1540
  14.0 50.1 %copy-start.3 = (f32[2,128,1024]{2,1,0:T(8,128)S(1)}, f32[2,128,1024]{2,1,0:T(8,128)}, u32[]{:S(2)}) copy-start(f32[2,128,1024]{2,1,0:T(8,128)} %vel.1) | copy-start | bytes 3145732
  14.3 49.8 %copy-start.2 = (f32[3,128,1024]{2,1,0:T(8,128)S(1)}, f32[3,128,1024]{2,1,0:T(8,128)}, u32[]{:S(2)}) copy-start(f32[3,128,1024]{2,1,0:T(8,128)} %stress.1) | copy-start | bytes 4718596
  36.0 28.1 %copy-start.1 = (f32[5,128,1024]{2,1,0:T(8,128)S(1)}, f32[5,128,1024]{2,1,0:T(8,128)}, u32[]{:S(2)}) copy-start(f32[5,128,1024]{2,1,0:T(8,128)} %thick.1) | copy-start | bytes 7864324
  40.2 24.0 %copy-start = (f32[5,128,1024]{2,1,0:T(8,128)S(1)}, f32[5,128,1024]{2,1,0:T(8,128)}, u32[]{:S(2)}) copy-start(f32[5,128,1024]{2,1,0:T(8,128)} %area.1) | copy-start | bytes 7864324

commit v4 on v3

--- a/solution.py
+++ b/solution.py
@@ -23,14 +23,19 @@
 U, V, SXX, SYY, S12, AREA, MASS, STR, UO, VO, TX, TY, TURN, S1_OUT, S2_OUT, U_NEW, V_NEW = range(17)
 RENEWED = (U, V, SXX, SYY, S12)
 EDGE_LANES = 3 * ICE
+EAST_AT = 4 * EDGE_LANES
+WEST_AT = EAST_AT + 12
 STRIP = (SLOTS + 1) * BS
 UNROLL = 4
+UNROLL_OWN = 8
+UNROLL_STRESS = 9
+UNROLL_VELOCITY = 8
 WIDE = 3 * BS
 TOP = 8
 ROWS = BS + 2 * TOP
 SEND_ROWS = 32
 M1_ROWS = TILE * 32 + SLOTS * 8
-M2_ROWS = (SLOTS + 1) * 32 + 80
+M2_ROWS = SLOTS * 32 + (SLOTS + 1) * 8 + 8
 M3_ROWS = SLOTS * 16
 M4_ROWS = TILE * 16
 F32 = jnp.float32
@@ -54,10 +59,9 @@
     return (PSTAR / 6.0) * mass * jnp.exp(-CSTAR * (1.0 - conc))
 
 
-def edges_kernel(lens, band, lon, *refs):
-    ice = [refs[4 * i : 4 * i + 4] for i in range(4)]
-    f_low, f_high, south, north, packed_out = refs[16:]
-    odd = lax.rem(band[0], 2) == 1
+def rows_kernel(*refs):
+    ice = [refs[2 * i : 2 * i + 2] for i in range(4)]
+    f_low, f_high, south, north = refs[8:]
     for out, which, force, row0, frow0 in (
         (south, 0, f_low, 0, 0),
         (north, 1, f_high, 5, 14),
@@ -71,64 +75,85 @@
             rows = force[f].astype(F32)
             out[21 + f : 22 + f, 0:512] = rows[frow0 : frow0 + 1, :]
             out[21 + f : 22 + f, 512:1024] = rows[frow0 + 1 : frow0 + 2, :]
-    lane = lanes_of((BS, BS))
-    packed = jnp.zeros((BS, BS), F32)
-    for side, which, col_even, col_odd in ((0, 2, 0, 125), (1, 3, 125, 0)):
-        arrays = [ice[i][which] for i in range(4)]
-        fields = ice_fields(*[[a[n] for n in range(a.shape[0])] for a in arrays])
-        for f in range(ICE):
-            at = 2 * side * EDGE_LANES + 3 * f
-            high = fields[f].astype(BF16).astype(F32)
-            for part, there in ((high, at), (fields[f] - high, at + EDGE_LANES)):
-                shift = jnp.where(odd, (there - col_odd) % BS, (there - col_even) % BS)
-                moved = pltpu.roll(part, shift, 1)
-                packed = jnp.where((lane >= there) & (lane < there + 3), moved, packed)
-    packed_out[...] = packed
-
-
-def make_edges(lens, band, lon, vel, stress, area, thick, forcing):
+
+
+def edge_rows(vel, stress, area, thick, forcing):
     width = SLOTS * BS
 
     def specs(n):
         return [
-            pl.BlockSpec((n, 8, width), lambda i, lens, band, lon: (0, 0, 0)),
-            pl.BlockSpec((n, 8, width), lambda i, lens, band, lon: (0, BS // 8 - 1, 0)),
-            pl.BlockSpec((n, BS, BS), lambda i, lens, band, lon: (0, 0, 0)),
-            pl.BlockSpec(
-                (n, BS, BS),
-                lambda i, lens, band, lon: (0, 0, lens[band[0], lon[0]] - 1),
-            ),
+            pl.BlockSpec((n, 8, width), lambda i: (0, 0, 0)),
+            pl.BlockSpec((n, 8, width), lambda i: (0, BS // 8 - 1, 0)),
         ]
 
     in_specs = specs(2) + specs(3) + specs(5) + specs(5)
     in_specs += [
-        pl.BlockSpec((4, 16, 512), lambda i, lens, band, lon: (0, 0, 0)),
-        pl.BlockSpec((4, 16, 512), lambda i, lens, band, lon: (0, BS // 16 - 1, 0)),
+        pl.BlockSpec((4, 16, 512), lambda i: (0, 0, 0)),
+        pl.BlockSpec((4, 16, 512), lambda i: (0, BS // 16 - 1, 0)),
     ]
-    whole = lambda i, lens, band, lon: (0, 0)
     return pl.pallas_call(
-        edges_kernel,
-        grid_spec=pltpu.PrefetchScalarGridSpec(
-            num_scalar_prefetch=3,
-            grid=(1,),
-            in_specs=in_specs,
-            out_specs=[
-                pl.BlockSpec((SEND_ROWS, width), whole),
-                pl.BlockSpec((SEND_ROWS, width), whole),
-                pl.BlockSpec((BS, BS), whole),
-            ],
-        ),
-        out_shape=[
-            jax.ShapeDtypeStruct((SEND_ROWS, width), F32),
-            jax.ShapeDtypeStruct((SEND_ROWS, width), F32),
-            jax.ShapeDtypeStruct((BS, BS), F32),
-        ],
+        rows_kernel,
+        grid=(1,),
+        in_specs=in_specs,
+        out_specs=[pl.BlockSpec((SEND_ROWS, width), lambda i: (0, 0))] * 2,
+        out_shape=[jax.ShapeDtypeStruct((SEND_ROWS, width), F32)] * 2,
         compiler_params=pltpu.CompilerParams(vmem_limit_bytes=60 * 2**20),
-        name="edges",
-    )(lens, band, lon, *([vel] * 4), *([stress] * 4), *([area] * 4), *([thick] * 4), forcing, forcing)
-
-
-def spread_kernel(forcing, north, south, edges, out, hold):
+        name="edge_rows",
+    )(*([vel] * 2), *([stress] * 2), *([area] * 2), *([thick] * 2), forcing, forcing)
+
+
+def columns_kernel(lens, band, lon, vel, stress, area, thick, packed_out, blocks, sems):
+    odd = lax.rem(band[0], 2) == 1
+    last = pl.multiple_of((lens[band[0], lon[0]] - 1) * BS, BS)
+    made = []
+    for side, at in ((0, 0), (1, last)):
+        n = 0
+        for ref in (vel, stress, area, thick):
+            for m in range(ref.shape[0]):
+                made.append(
+                    pltpu.make_async_copy(
+                        ref.at[m, :, pl.ds(at, BS)], blocks.at[side, n], sems.at[side, n]
+                    )
+                )
+                n += 1
+    for copy in made:
+        copy.start()
+    lane = lanes_of((BS, BS))
+    total = jnp.zeros((BS, BS), F32)
+    for side in range(2):
+        for copy in made[15 * side : 15 * side + 15]:
+            copy.wait()
+        held = [blocks[side, n] for n in range(15)]
+        fields = ice_fields(held[0:2], held[2:5], held[5:10], held[10:15])
+        first_columns = jnp.broadcast_to(odd if side else jnp.logical_not(odd), (BS, BS))
+        packed = jnp.zeros((BS, BS), F32)
+        for f in range(ICE):
+            at_zero = jnp.where(first_columns, fields[f], pltpu.roll(fields[f], 3, 1))
+            moved = pltpu.roll(at_zero, 3 * f, 1) if f else at_zero
+            packed = jnp.where((lane >= 3 * f) & (lane < 3 * f + 3), moved, packed)
+        high = packed.astype(BF16).astype(F32)
+        both = high + pltpu.roll(packed - high, EDGE_LANES, 1)
+        total = total + (pltpu.roll(both, 2 * EDGE_LANES, 1) if side else both)
+    packed_out[...] = total
+
+
+def edge_columns(lens, band, lon, vel, stress, area, thick):
+    return pl.pallas_call(
+        columns_kernel,
+        in_specs=[pl.BlockSpec(memory_space=pltpu.SMEM)] * 3
+        + [pl.BlockSpec(memory_space=pl.ANY)] * 4,
+        out_specs=pl.BlockSpec(memory_space=pltpu.VMEM),
+        out_shape=jax.ShapeDtypeStruct((BS, BS), F32),
+        scratch_shapes=[pltpu.VMEM((2, 15, BS, BS), F32), pltpu.SemaphoreType.DMA((2, 15))],
+        compiler_params=pltpu.CompilerParams(vmem_limit_bytes=60 * 2**20),
+        name="edge_columns",
+    )(lens, band, lon, vel, stress, area, thick)
+
+
+def spread_kernel(forcing, north, south, edges_in, out, hold, edges, sem):
+    fetch = pltpu.make_async_copy(edges_in, edges, sem)
+    fetch.start()
+
     def rows16(pair, carry):
         base = pl.multiple_of(pair * 16, 16)
         for cb in range(TILE):
@@ -141,7 +166,8 @@
             out[2 * pair + 1, cb * 32 : (cb + 1) * 32, :] = high.astype(BF16)
         return carry
 
-    lax.fori_loop(0, BS // 16, rows16, 0)
+    lax.fori_loop(0, BS // 16, rows16, 0, unroll=2)
+    fetch.wait()
     for j in range(NLON):
         hold[...] = jnp.zeros(hold.shape, F32)
         source = north if j < 8 else south
@@ -167,9 +193,14 @@
     return pl.pallas_call(
         spread_kernel,
         out_shape=jax.ShapeDtypeStruct((NLON, M1_ROWS, BS), BF16),
-        in_specs=[pl.BlockSpec(memory_space=pltpu.VMEM)] * 4,
+        in_specs=[pl.BlockSpec(memory_space=pltpu.VMEM)] * 3
+        + [pl.BlockSpec(memory_space=pl.ANY)],
         out_specs=pl.BlockSpec(memory_space=pltpu.VMEM),
-        scratch_shapes=[pltpu.VMEM((SLOTS * 8, BS), F32)],
+        scratch_shapes=[
+            pltpu.VMEM((SLOTS * 8, BS), F32),
+            pltpu.VMEM((BS, BS), F32),
+            pltpu.SemaphoreType.DMA,
+        ],
         compiler_params=pltpu.CompilerParams(vmem_limit_bytes=32 * 2**20),
         name="spread",
     )(forcing, north, south, edges)
@@ -182,7 +213,7 @@
         table[jnp.where(s < count, column, NBB)] = k * SLOTS + s
 
 
-def deal_kernel(lens, band, lon, got, out, groups, hold, table):
+def deal_kernel(lens, band, lon, got, out, groups, halos, table):
     band, lon = band[0], lon[0]
     odd = lax.rem(band, 2) == 1
     other = jnp.where(lon < 8, jnp.minimum(band + 1, NLAT - 1), jnp.maximum(band - 1, 0))
@@ -196,20 +227,27 @@
         return start + lens[other, l]
 
     lax.fori_loop(0, NLON, fill, 0, unroll=UNROLL)
-    lane32 = lanes_of((32, BS)) < 64
-    lane8 = lanes_of((8, BS)) < 64
     row6 = lax.broadcasted_iota(jnp.int32, (8, BS), 0) == 6
-    from_next = lanes_of((8, BS)) < 2 * EDGE_LANES
+
+    def halo(c, carry):
+        own = (c // TILE) * SLOTS + lax.rem(c, TILE)
+        halos[c] = jnp.where(row6, groups[own], groups[table[c]])
+        return carry
+
+    lax.fori_loop(0, NBB, halo, 0, unroll=8)
+    lane = lanes_of((8, BS))
+
+    def column_at(p):
+        p = jnp.minimum(p, NBB - 1)
+        return jnp.where(odd, NBB - 1 - p, p)
+
+    def forcing(c):
+        at = pl.multiple_of(lax.rem(c, TILE) * 32, 32)
+        return got[c // TILE, pl.ds(at, 32), :]
 
     def edges(k):
         at = pl.multiple_of(lax.rem(k, NLON) * SLOTS, SLOTS)
         return groups[pl.ds(at, SLOTS), 7, :]
-
-    def block(c):
-        tile, cb = c // TILE, lax.rem(c, TILE)
-        rows = got[tile, pl.ds(pl.multiple_of(cb * 32, 32), 32), :].astype(F32)
-        group = jnp.where(row6, groups[tile * SLOTS + cb], groups[table[c]])
-        return rows, group
 
     def owner(k, start):
         count = lens[band, k]
@@ -217,19 +255,24 @@
         east = jnp.where(odd, NBB - 1 - start, last) + 1
         west = jnp.where(odd, NBB - 1 - last, start) - 1
         east, west = lax.rem(east, NBB), lax.rem(west + NBB, NBB)
-        for e in range(SLOTS + 1):
-            mine = e < count
-            at = start + e
-            column = jnp.where(odd, NBB - 1 - at, at)
-            rows_a, group_a = block(jnp.where(mine, column, east))
-            rows_b, group_b = block(jnp.where(mine, column, west))
-            out[k, e * 32 : (e + 1) * 32, :] = jnp.where(lane32, rows_a, rows_b).astype(BF16)
-            hold[e * 8 : (e + 1) * 8, :] = jnp.where(lane8, group_a, group_b)
-        hold[72:80, :] = jnp.where(from_next, edges(k + 1), edges(k + NLON - 1))
-        out[k, (SLOTS + 1) * 32 :, :] = hold[...].astype(BF16)
+        parts = []
+        for e in range(SLOTS):
+            c = column_at(start + e)
+            out[k, e * 32 : (e + 1) * 32, :] = forcing(c)
+            parts.append(halos[c])
+        parts.append(jnp.where(lane < 64, halos[east], halos[west]))
+        side = jnp.where(lane < 2 * EDGE_LANES, edges(k + 1), edges(k + NLON - 1))
+        by_east, by_west = forcing(east).astype(F32), forcing(west).astype(F32)
+        for f in range(4):
+            for rows, at, col in ((by_east, EAST_AT, 0), (by_west, WEST_AT, 125)):
+                there = at + 3 * f
+                moved = pltpu.roll(rows[8 * f : 8 * f + 8, :], (there - col) % BS, 1)
+                side = jnp.where((lane >= there) & (lane < there + 3), moved, side)
+        parts.append(side)
+        out[k, SLOTS * 32 :, :] = jnp.concatenate(parts, axis=0).astype(BF16)
         return start + count
 
-    lax.fori_loop(0, NLON, owner, 0, unroll=2)
+    lax.fori_loop(0, NLON, owner, 0, unroll=4)
 
 
 def deal(lens, band, lon, got):
@@ -241,7 +284,7 @@
         out_specs=pl.BlockSpec(memory_space=pltpu.VMEM),
         scratch_shapes=[
             pltpu.VMEM((NLON * SLOTS, 8, BS), F32),
-            pltpu.VMEM((80, BS), F32),
+            pltpu.VMEM((NBB, 8, BS), F32),
             pltpu.SMEM((NBB + 1,), jnp.int32),
         ],
         compiler_params=pltpu.CompilerParams(vmem_limit_bytes=32 * 2**20),
@@ -253,7 +296,7 @@
     lens, band, lon, vel, stress, area, thick, got, coriolis,
     vel_out, stress_out, handed, *scratch,
 ):
-    fields_at, (edge, empty, sems) = list(scratch[:-3]), scratch[-3:]
+    fields_at, (empty, sems) = list(scratch[:-2]), scratch[-2:]
     band, lon = band[0], lon[0]
     odd = lax.rem(band, 2) == 1
     count = lens[band, lon]
@@ -268,18 +311,8 @@
     edge_lanes = pl.ds(SLOTS * BS, BS)
     empty[...] = jnp.zeros(empty.shape, F32)
 
-    def arrived(j, carry):
-        for e in range(SLOTS + 1):
-            rows = got[j, e * 32 : (e + 1) * 32, :].astype(F32)
-            lanes = slot_lanes(e) if e < SLOTS else edge_lanes
-            for f in range(4):
-                fields_at[UO + f][rows_at(j + 1), lanes] = rows[f * 8 : (f + 1) * 8, :]
-        edge[rows_at(j), :] = got[j, M2_ROWS - 16 :, :].astype(F32)[8:16, :]
-        return carry
-
-    lax.fori_loop(0, NLON, arrived, 0)
     for j in range(NLON):
-        group = got[j, (SLOTS + 1) * 32 :, :].astype(F32)[0 : 8 * (SLOTS + 1), :]
+        group = got[j, SLOTS * 32 : SLOTS * 32 + 8 * (SLOTS + 1), :].astype(F32)
         group = group.reshape(SLOTS + 1, 8, BS)
         whole = group + pltpu.roll(group, 5, 1)
         if j >= 8:
@@ -289,9 +322,11 @@
         force_row = (TOP - 2, TOP - 1, TOP + BS, TOP + BS + 1)[j % 4]
         for e in range(SLOTS + 1):
             lanes = slot_lanes(e) if e < SLOTS else edge_lanes
+            mine = jnp.broadcast_to(e < count, (8, BS))
             if f < ICE:
-                fields_at[f][rows_at(g), lanes] = whole[e]
-            fields_at[UO + j // 4][force_row : force_row + 1, lanes] = group[e, 6:7, :]
+                fields_at[f][rows_at(g), lanes] = jnp.where(mine, whole[e], whole[SLOTS])
+            rows = jnp.where(mine, group[e], group[SLOTS])
+            fields_at[UO + j // 4][force_row : force_row + 1, lanes] = rows[6:7, :]
 
     def derived(conc, mass, g, lanes):
         turn = coriolis[rows_at(g), :]
@@ -304,20 +339,22 @@
         derived(fields_at[AREA][rows_at(g), :], fields_at[MASS][rows_at(g), :], g, slice(0, STRIP))
 
     def own_rows(j, carry):
-        packed = edge[rows_at(j), :]
+        packed = got[j, M2_ROWS - 16 :, :].astype(F32)[8:16, :]
+        near = lanes_of((8, BS)) < 64
+
+        def joined(east, east_lane, west, west_lane):
+            return jnp.where(
+                near,
+                pltpu.roll(east, (BS - east_lane) % BS, 1),
+                pltpu.roll(west, (125 - west_lane) % BS, 1),
+            )
+
+        forced = [joined(packed, EAST_AT + 3 * f, packed, WEST_AT + 3 * f) for f in range(4)]
         packed = packed + pltpu.roll(packed, BS - EDGE_LANES, 1)
         at_zero = pltpu.roll(packed, BS - 2 * EDGE_LANES, 1)
         east = jnp.where(odd, at_zero, packed)
         west = jnp.where(odd, packed, at_zero)
-        near = lanes_of((8, BS)) < 64
-        beside = [
-            jnp.where(
-                near,
-                pltpu.roll(east, (BS - 3 * f) % BS, 1),
-                pltpu.roll(west, 125 - 3 * f, 1),
-            )
-            for f in range(ICE)
-        ]
+        beside = [joined(east, 3 * f, west, 3 * f) for f in range(ICE)]
         rows = rows_at(j)
         for e in range(SLOTS + 1):
             if e == SLOTS:
@@ -333,12 +370,18 @@
                 )
                 mine = jnp.broadcast_to(e < count, (8, BS))
                 fields = [jnp.where(mine, fields[f], beside[f]) for f in range(ICE)]
+            force = forced
+            if e < SLOTS:
+                force = got[j, e * 32 : (e + 1) * 32, :].astype(F32)
+                force = [jnp.where(mine, force[8 * f : 8 * f + 8], forced[f]) for f in range(4)]
+            for f in range(4):
+                fields_at[UO + f][rows_at(j + 1), lanes] = force[f]
             for f in range(ICE):
                 fields_at[f][rows_at(j + 1), lanes] = fields[f]
             derived(fields[AREA], fields[MASS], j + 1, lanes)
         return carry
 
-    lax.fori_loop(0, groups, own_rows, 0, unroll=UNROLL)
+    lax.fori_loop(0, groups, own_rows, 0, unroll=UNROLL_OWN)
 
     cells = (8, WIDE)
     row = lax.broadcasted_iota(jnp.int32, cells, 0)
@@ -458,7 +501,7 @@
             stress_rows(g, new, last)
             return carry
 
-        lax.fori_loop(0, groups + (1 if last else 2), stress_step, 0, unroll=UNROLL)
+        lax.fori_loop(0, groups + (1 if last else 2), stress_step, 0, unroll=UNROLL_STRESS)
         for f in (SXX, SYY, S12):
             n = S2_OUT + 1 + RENEWED.index(f)
             fields_at[f], fields_at[n] = fields_at[n], fields_at[f]
@@ -477,12 +520,12 @@
         if last:
             for h in range(2):
                 half = groups // 2
-                lax.fori_loop(1 + h * half, 1 + (h + 1) * half, velocity_step, 0, unroll=UNROLL)
+                lax.fori_loop(1 + h * half, 1 + (h + 1) * half, velocity_step, 0, unroll=UNROLL_VELOCITY)
                 made = copies((U_NEW, V_NEW), vel_out, h * BS // 2, BS // 2, 24 + 16 * h)
                 start(made)
                 pending += made
         else:
-            lax.fori_loop(1, groups + 1, velocity_step, 0, unroll=UNROLL)
+            lax.fori_loop(1, groups + 1, velocity_step, 0, unroll=UNROLL_VELOCITY)
             for f in (U, V):
                 n = S2_OUT + 1 + RENEWED.index(f)
                 fields_at[f], fields_at[n] = fields_at[n], fields_at[f]
@@ -501,7 +544,6 @@
         scratch_shapes=[
             *[pltpu.VMEM((ROWS + 8, STRIP), F32) for _ in range(S2_OUT + 6)],
             pltpu.VMEM((BS, BS), F32),
-            pltpu.VMEM((BS, BS), F32),
             pltpu.SemaphoreType.DMA((24 + 32,)),
         ],
         out_shape=[
@@ -581,10 +623,11 @@
     rows = (band_idx * BS + jnp.arange(-TOP, BS + TOP, dtype=jnp.int32)).astype(F32)
     latitude = -78.0 + 168.0 * (rows + 0.5) / (BS * NLAT)
     coriolis = jnp.broadcast_to(jnp.sin(latitude * (jnp.pi / 180.0))[:, None], (ROWS, BS))
-    to_south, to_north, edges = make_edges(lens, *place, *ice, ocean_forcing)
+    to_south, to_north = edge_rows(*ice, ocean_forcing)
     north = lax.ppermute(to_south, "lat", [(b, b - 1) for b in range(1, NLAT)])
     south = lax.ppermute(to_north, "lat", [(b, b + 1) for b in range(NLAT - 1)])
     north, south, coriolis = lax.optimization_barrier((north, south, coriolis))
+    edges = edge_columns(lens, *place, *ice)
     message = spread(ocean_forcing, north, south, edges)
     dealt = to_all(deal(lens, *place, to_all(message)))
     velocity_out, stress_out, handed = dynamics(lens, *place, *ice, dealt, coriolis)

time: 104 us -> 102 us (0.981)
  waiting for transfers between devices: 4.03 us -> 0.01 us
  blocking collectives: 70.2 us -> 73.8 us
    ppermute x1, waiting for transfers between devices: 3.68 us -> 0.01 us  [body(): south = lax.ppermute(to_north, 'lat', [(b, b + 1) for b in range(NLAT - 1)])]
    all_to_all x4, blocking collectives: 70.2 us -> 73.8 us  [to_all(): return lax.all_to_all(block, 'lon', 0, 0, tiled=True)]
    pallas_call x1 -> x2, Pallas kernels: 4 us -> 6.06 us  [the longest x1 3.99 us: edge_columns(): pl.pallas_call(columns_kernel, in_specs=[pl.BlockSpec(memory_space=pltpu....]
    pallas_call x1, Pallas kernels: 11.9 us -> 10.4 us  [dynamics(): pl.pallas_call(dynamics_kernel, in_specs=[smem] * 3 + [vmem] * 6, out_spe...]
    pallas_call x1, Pallas kernels: 4.13 us -> 3.02 us  [deal(): pl.pallas_call(deal_kernel, out_shape=jax.ShapeDtypeStruct((NLON, M2_ROWS...]
  transfers between devices with their start and end apart: 2 -> 2, of which waited for: 2 -> 0; matrix products, arithmetic and copies ran while one was open for 0% -> 0% of each run, Pallas kernels for 0% -> 4%
where the time goes in v4:
time: 102 us; the launch traced here: 101 us
  blocking collectives  73.8 us (72%)
  Pallas kernels  21.6 us (21%)
  starting transfers between devices  4.31 us (4%)
    all_to_all x4, blocking collectives, to_all(): return lax.all_to_all(block, 'lon', 0, 0, tiled=True)  73.8 us
    pallas_call x1, Pallas kernels, dynamics(): pl.pallas_call(dynamics_kernel, in_specs=[smem] * 3 + [vmem] * 6, out_spe...  10.4 us
    pallas_call x1, Pallas kernels, edge_columns(): pl.pallas_call(columns_kernel, in_specs=[pl.BlockSpec(memory_space=pltpu....  3.99 us
    pallas_call x1, Pallas kernels, deal(): pl.pallas_call(deal_kernel, out_shape=jax.ShapeDtypeStruct((NLON, M2_ROWS...  3.02 us
    ppermute x1, starting transfers between devices, body(): south = lax.ppermute(to_north, 'lat', [(b, b + 1) for b in range(NLAT - 1)])  2.41 us
    pallas_call x1, Pallas kernels, edge_rows(): pl.pallas_call(rows_kernel, grid=(1,), in_specs=in_specs, out_specs=[pl.B...  2.08 us
  transfers between devices with their start and end apart: 2, of which 0 were waited for; matrix products, arithmetic and copies ran while one was open for 0% of the time, Pallas kernels for 4%

profile of v4, /device:TPU:8, one launch (start us, length us, event | category | flops | bytes accessed | tf_op | source)
XLA Modules:
  0.0 101.5 jit_solution(8556104964332370810)
XLA Ops:
  0.6 2.1 %edge_rows.1 = (f32[32,1024]{1,0:T(8,128)}, f32[32,1024]{1,0:T(8,128)}) custom-call(f32[2,128,1024]{2,1,0:T(8,128)} %vel.3, f32[2,128,1024]{2,1,0:T(8,128)} %vel.3, f32[3,128,1024]{2,1,0:T(8,128)} %stress.3, f32[3,128,1024]{2,1,0:T(8,128)} %stress.3, f32[5,128,1024]{2,1,0:T(8,128)} %area.3, f32[5,128,1024]{2,1,0:T(8,128)} %area.3, f32[5,128,1024]{2,1,0:T(8,128)} %thick.3, ...), custom_call_target="tpu_custom_call" | custom-call | tf_op jit(solution)/shard_map/edge_rows/pallas_call | solution.py:94
  2.7 1.9 %collective-permute-start = (f32[32,1024]{1,0:T(8,128)}, f32[32,1024]{1,0:T(8,128)S(1)}, u32[]{:S(2)}, u32[]{:S(2)}) collective-permute-start(f32[32,1024]{1,0:T(8,128)} %get-tuple-element.11), channel_id=1, source_target_pairs={{16,0},{32,16},{48,32},{64,48},{80,64},{96,80},{112,96},{17,1},{33... | collective-permute-start | bytes 393224 | tf_op jit(solution)/shard_map/ppermute | solution.py:627
  4.6 2.4 %collective-permute-start.1 = (f32[32,1024]{1,0:T(8,128)}, f32[32,1024]{1,0:T(8,128)S(1)}, u32[]{:S(2)}, u32[]{:S(2)}) collective-permute-start(f32[32,1024]{1,0:T(8,128)} %get-tuple-element.12), channel_id=1, source_target_pairs={{0,16},{16,32},{32,48},{48,64},{64,80},{80,96},{96,112},{1,17},{17... | collective-permute-start | bytes 393224 | tf_op jit(solution)/shard_map/ppermute | solution.py:628
  7.0 0.0 copy-start.4
  7.1 4.0 %edge_columns.1.edges_in = f32[128,128]{1,0:T(8,128)} custom-call(s32[8,16]{1,0:T(8,128)} %lens.7, s32[1]{0:T(128)} %bitcast.band, s32[1]{0:T(128)} %bitcast.1.lon, f32[2,128,1024]{2,1,0:T(8,128)} %vel.3, f32[3,128,1024]{2,1,0:T(8,128)} %stress.3, f32[5,128,1024]{2,1,0:T(8,128)} %area.3, f32[5,128,1024]{2,1,0:T(8,128)} %thick.3), custom_call_target="tpu_custom_call" | custom-call | tf_op jit(solution)/shard_map/edge_columns/pallas_call | solution.py:141
  11.0 0.1 multiply_sine_fusion
  11.1 0.0 collective-permute-done.north
  11.1 0.0 collective-permute-done.1.south
  11.1 0.1 broadcast_in_dim.2.coriolis
  11.2 0.0 copy-done.4
  11.2 0.0 copy-start.5
  11.2 0.8 copy-done.5
  12.1 0.0 copy-start.6
  12.1 0.0 copy-start.2
  12.1 0.4 spread.1
  12.5 0.0 copy-start.1
  12.5 24.0 %all_to_all.20.got = bf16[16,192,128]{2,1,0:T(8,128)(2,1)S(1)} all-to-all(bf16[16,192,128]{2,1,0:T(8,128)(2,1)S(1)} %spread.1), channel_id=1, replica_groups=mesh['lat'=8,'lon'=16] {'lon'}, dimensions={0} | all-to-all | bytes 1572864 | tf_op jit(solution)/shard_map/all_to_all | solution.py:614
  36.5 0.0 copy-done.6
  36.5 0.0 copy-start.3
  36.5 3.0 %deal.1 = bf16[16,336,128]{2,1,0:T(8,128)(2,1)S(1)} custom-call(s32[8,16]{1,0:T(8,128)S(1)} %copy-done.6, s32[1]{0:T(128)} %bitcast.band, s32[1]{0:T(128)} %bitcast.1.lon, bf16[16,192,128]{2,1,0:T(8,128)(2,1)S(1)} %all_to_all.20.got), custom_call_target="tpu_custom_call" | custom-call | tf_op jit(solution)/shard_map/deal/pallas_call | solution.py:279
  39.5 0.0 copy-start
  39.6 24.0 %all_to_all.21.got = bf16[16,336,128]{2,1,0:T(8,128)(2,1)S(1)} all-to-all(bf16[16,336,128]{2,1,0:T(8,128)(2,1)S(1)} %deal.1), channel_id=1, replica_groups=mesh['lat'=8,'lon'=16] {'lon'}, dimensions={0} | all-to-all | bytes 2752512 | tf_op jit(solution)/shard_map/all_to_all | solution.py:614
  63.6 0.0 copy-done.2
  63.6 0.0 copy-done.1
  63.6 0.0 copy-done.3
  63.6 0.0 copy-done
  63.6 10.4 %dynamics.1 = (f32[2,128,1024]{2,1,0:T(8,128)}, f32[3,128,1024]{2,1,0:T(8,128)}, bf16[16,128,128]{2,1,0:T(8,128)(2,1)S(1)}) custom-call(s32[8,16]{1,0:T(8,128)S(1)} %copy-done.6, s32[1]{0:T(128)} %bitcast.band, s32[1]{0:T(128)} %bitcast.1.lon, f32[2,128,1024]{2,1,0:T(8,128)S(1)} %copy-done.3, f32[3,128,1024]{2,1,0:T(8,128)S(1)} %copy-done.2, ...), custom_call_target="tpu_custom_call" | custom-call | tf_op jit(solution)/shard_map/dynamics/pallas_call | solution.py:540
  74.0 14.0 %all_to_all.22 = bf16[16,128,128]{2,1,0:T(8,128)(2,1)S(1)} all-to-all(bf16[16,128,128]{2,1,0:T(8,128)(2,1)S(1)} %get-tuple-element.18), channel_id=1, replica_groups=mesh['lat'=8,'lon'=16] {'lon'}, dimensions={0} | all-to-all | bytes 1048576 | tf_op jit(solution)/shard_map/all_to_all | solution.py:614
  88.0 1.0 %sort_back.1 = bf16[64,16,128]{2,1,0:T(8,128)(2,1)S(1)} custom-call(s32[8,16]{1,0:T(8,128)S(1)} %copy-done.6, s32[1]{0:T(128)} %bitcast.band, bf16[128,16,128]{2,1,0:T(8,128)(2,1)S(1)} %bitcast.4), custom_call_target="tpu_custom_call" | custom-call | tf_op jit(solution)/shard_map/sort_back/pallas_call | solution.py:576
  89.1 11.6 %all_to_all.23.got = bf16[16,64,128]{2,1,0:T(8,128)(2,1)S(1)} all-to-all(bf16[16,64,128]{2,1,0:T(8,128)(2,1)S(1)} %bitcast.5), channel_id=1, replica_groups=mesh['lat'=8,'lon'=16] {'lon'}, dimensions={0} | all-to-all | bytes 524288 | tf_op jit(solution)/shard_map/all_to_all | solution.py:614
  100.7 0.8 settle.1
Async XLA Ops:
  2.7 8.4 %collective-permute-start = (f32[32,1024]{1,0:T(8,128)}, f32[32,1024]{1,0:T(8,128)S(1)}, u32[]{:S(2)}, u32[]{:S(2)}) collective-permute-start(f32[32,1024]{1,0:T(8,128)} %get-tuple-element.11), channel_id=1, source_target_pairs={{16,0},{32,16},{48,32},{64,48},{80,64},{96,80},{112,96},{17,1},{33... | collective-permute-start | bytes 393224 | tf_op jit(solution)/shard_map/ppermute | solution.py:627
  4.6 6.5 %collective-permute-start.1 = (f32[32,1024]{1,0:T(8,128)}, f32[32,1024]{1,0:T(8,128)S(1)}, u32[]{:S(2)}, u32[]{:S(2)}) collective-permute-start(f32[32,1024]{1,0:T(8,128)} %get-tuple-element.12), channel_id=1, source_target_pairs={{0,16},{16,32},{32,48},{48,64},{64,80},{80,96},{96,112},{1,17},{17... | collective-permute-start | bytes 393224 | tf_op jit(solution)/shard_map/ppermute | solution.py:628
  7.0 4.2 %copy-start.4 = (bf16[4,128,512]{2,1,0:T(8,128)(2,1)S(1)}, bf16[4,128,512]{2,1,0:T(8,128)(2,1)}, u32[]{:S(2)}) copy-start(bf16[4,128,512]{2,1,0:T(8,128)(2,1)} %forcing.1) | copy-start | bytes 1572868
  11.2 0.8 copy-start.5
  12.1 24.5 %copy-start.6 = (s32[8,16]{1,0:T(8,128)S(1)}, s32[8,16]{1,0:T(8,128)}, u32[]{:S(2)}) copy-start(s32[8,16]{1,0:T(8,128)} %lens.7) | copy-start | bytes 1540
  12.1 51.5 %copy-start.2 = (f32[3,128,1024]{2,1,0:T(8,128)S(1)}, f32[3,128,1024]{2,1,0:T(8,128)}, u32[]{:S(2)}) copy-start(f32[3,128,1024]{2,1,0:T(8,128)} %stress.3) | copy-start | bytes 4718596
  12.5 51.1 %copy-start.1 = (f32[5,128,1024]{2,1,0:T(8,128)S(1)}, f32[5,128,1024]{2,1,0:T(8,128)}, u32[]{:S(2)}) copy-start(f32[5,128,1024]{2,1,0:T(8,128)} %thick.3) | copy-start | bytes 7864324
  36.5 27.1 %copy-start.3 = (f32[2,128,1024]{2,1,0:T(8,128)S(1)}, f32[2,128,1024]{2,1,0:T(8,128)}, u32[]{:S(2)}) copy-start(f32[2,128,1024]{2,1,0:T(8,128)} %vel.3) | copy-start | bytes 3145732
  39.5 24.1 %copy-start = (f32[5,128,1024]{2,1,0:T(8,128)S(1)}, f32[5,128,1024]{2,1,0:T(8,128)}, u32[]{:S(2)}) copy-start(f32[5,128,1024]{2,1,0:T(8,128)} %area.3) | copy-start | bytes 7864324

commit v5 on v4

--- a/solution.py
+++ b/solution.py
@@ -33,7 +33,8 @@
 WIDE = 3 * BS
 TOP = 8
 ROWS = BS + 2 * TOP
-SEND_ROWS = 32
+SEND_ROWS = 24
+MASS_AT, FORCE_AT = 18, 20
 M1_ROWS = TILE * 32 + SLOTS * 8
 M2_ROWS = SLOTS * 32 + (SLOTS + 1) * 8 + 8
 M3_ROWS = SLOTS * 16
@@ -59,72 +60,44 @@
     return (PSTAR / 6.0) * mass * jnp.exp(-CSTAR * (1.0 - conc))
 
 
-def rows_kernel(*refs):
-    ice = [refs[2 * i : 2 * i + 2] for i in range(4)]
-    f_low, f_high, south, north = refs[8:]
-    for out, which, force, row0, frow0 in (
-        (south, 0, f_low, 0, 0),
-        (north, 1, f_high, 5, 14),
-    ):
+def edges_kernel(lens, band, lon, *refs):
+    ice = [refs[4 * i : 4 * i + 4] for i in range(4)]
+    f_low, f_high, to_mate, to_other, packed_out = refs[16:]
+    odd = lax.rem(band[0], 2) == 1
+
+    def strips(out, which, force, row0, frow0):
         arrays = [ice[i][which] for i in range(4)]
         fields = ice_fields(*[[a[n] for n in range(a.shape[0])] for a in arrays])
-        out[...] = jnp.zeros(out.shape, F32)
-        for f in range(ICE):
+        for f in range(MASS):
             out[3 * f : 3 * f + 3, :] = fields[f][row0 : row0 + 3, :]
+        near = row0 if row0 == 0 else row0 + 1
+        out[MASS_AT : MASS_AT + 2, :] = fields[MASS][near : near + 2, :]
+        if row0:
+            strength = strength_of(fields[AREA], fields[MASS])
+            out[3 * AREA : 3 * AREA + 1, :] = strength[row0 : row0 + 1, :]
         for f in range(4):
             rows = force[f].astype(F32)
-            out[21 + f : 22 + f, 0:512] = rows[frow0 : frow0 + 1, :]
-            out[21 + f : 22 + f, 512:1024] = rows[frow0 + 1 : frow0 + 2, :]
-
-
-def edge_rows(vel, stress, area, thick, forcing):
-    width = SLOTS * BS
-
-    def specs(n):
-        return [
-            pl.BlockSpec((n, 8, width), lambda i: (0, 0, 0)),
-            pl.BlockSpec((n, 8, width), lambda i: (0, BS // 8 - 1, 0)),
-        ]
-
-    in_specs = specs(2) + specs(3) + specs(5) + specs(5)
-    in_specs += [
-        pl.BlockSpec((4, 16, 512), lambda i: (0, 0, 0)),
-        pl.BlockSpec((4, 16, 512), lambda i: (0, BS // 16 - 1, 0)),
-    ]
-    return pl.pallas_call(
-        rows_kernel,
-        grid=(1,),
-        in_specs=in_specs,
-        out_specs=[pl.BlockSpec((SEND_ROWS, width), lambda i: (0, 0))] * 2,
-        out_shape=[jax.ShapeDtypeStruct((SEND_ROWS, width), F32)] * 2,
-        compiler_params=pltpu.CompilerParams(vmem_limit_bytes=60 * 2**20),
-        name="edge_rows",
-    )(*([vel] * 2), *([stress] * 2), *([area] * 2), *([thick] * 2), forcing, forcing)
-
-
-def columns_kernel(lens, band, lon, vel, stress, area, thick, packed_out, blocks, sems):
-    odd = lax.rem(band[0], 2) == 1
-    last = pl.multiple_of((lens[band[0], lon[0]] - 1) * BS, BS)
-    made = []
-    for side, at in ((0, 0), (1, last)):
-        n = 0
-        for ref in (vel, stress, area, thick):
-            for m in range(ref.shape[0]):
-                made.append(
-                    pltpu.make_async_copy(
-                        ref.at[m, :, pl.ds(at, BS)], blocks.at[side, n], sems.at[side, n]
-                    )
-                )
-                n += 1
-    for copy in made:
-        copy.start()
+            at = FORCE_AT + f
+            out[at : at + 1, 0:512] = rows[frow0 : frow0 + 1, :]
+            out[at : at + 1, 512:1024] = rows[frow0 + 1 : frow0 + 2, :]
+
+    low, high = (0, f_low, 0, 0), (1, f_high, 5, 14)
+
+    @pl.when(odd)
+    def _():
+        strips(to_mate, *low)
+        strips(to_other, *high)
+
+    @pl.when(jnp.logical_not(odd))
+    def _():
+        strips(to_mate, *high)
+        strips(to_other, *low)
+
     lane = lanes_of((BS, BS))
     total = jnp.zeros((BS, BS), F32)
     for side in range(2):
-        for copy in made[15 * side : 15 * side + 15]:
-            copy.wait()
-        held = [blocks[side, n] for n in range(15)]
-        fields = ice_fields(held[0:2], held[2:5], held[5:10], held[10:15])
+        arrays = [ice[i][2 + side] for i in range(4)]
+        fields = ice_fields(*[[a[n] for n in range(a.shape[0])] for a in arrays])
         first_columns = jnp.broadcast_to(odd if side else jnp.logical_not(odd), (BS, BS))
         packed = jnp.zeros((BS, BS), F32)
         for f in range(ICE):
@@ -137,23 +110,44 @@
     packed_out[...] = total
 
 
-def edge_columns(lens, band, lon, vel, stress, area, thick):
+def make_edges(lens, band, lon, vel, stress, area, thick, forcing):
+    width = SLOTS * BS
+
+    def at(*index):
+        return lambda i, lens, band, lon: index
+
+    def specs(n):
+        return [
+            pl.BlockSpec((n, 8, width), at(0, 0, 0)),
+            pl.BlockSpec((n, 8, width), at(0, BS // 8 - 1, 0)),
+            pl.BlockSpec((n, BS, BS), at(0, 0, 0)),
+            pl.BlockSpec(
+                (n, BS, BS), lambda i, lens, band, lon: (0, 0, lens[band[0], lon[0]] - 1)
+            ),
+        ]
+
+    in_specs = specs(2) + specs(3) + specs(5) + specs(5)
+    in_specs += [
+        pl.BlockSpec((4, 16, 512), at(0, 0, 0)),
+        pl.BlockSpec((4, 16, 512), at(0, BS // 16 - 1, 0)),
+    ]
     return pl.pallas_call(
-        columns_kernel,
-        in_specs=[pl.BlockSpec(memory_space=pltpu.SMEM)] * 3
-        + [pl.BlockSpec(memory_space=pl.ANY)] * 4,
-        out_specs=pl.BlockSpec(memory_space=pltpu.VMEM),
-        out_shape=jax.ShapeDtypeStruct((BS, BS), F32),
-        scratch_shapes=[pltpu.VMEM((2, 15, BS, BS), F32), pltpu.SemaphoreType.DMA((2, 15))],
+        edges_kernel,
+        grid_spec=pltpu.PrefetchScalarGridSpec(
+            num_scalar_prefetch=3,
+            grid=(1,),
+            in_specs=in_specs,
+            out_specs=[pl.BlockSpec((SEND_ROWS, width), at(0, 0))] * 2
+            + [pl.BlockSpec((BS, BS), at(0, 0))],
+        ),
+        out_shape=[jax.ShapeDtypeStruct((SEND_ROWS, width), F32)] * 2
+        + [jax.ShapeDtypeStruct((BS, BS), F32)],
         compiler_params=pltpu.CompilerParams(vmem_limit_bytes=60 * 2**20),
-        name="edge_columns",
-    )(lens, band, lon, vel, stress, area, thick)
-
-
-def spread_kernel(forcing, north, south, edges_in, out, hold, edges, sem):
-    fetch = pltpu.make_async_copy(edges_in, edges, sem)
-    fetch.start()
-
+        name="edges",
+    )(lens, band, lon, *([vel] * 4), *([stress] * 4), *([area] * 4), *([thick] * 4), forcing, forcing)
+
+
+def spread_kernel(forcing, edges, out):
     def rows16(pair, carry):
         base = pl.multiple_of(pair * 16, 16)
         for cb in range(TILE):
@@ -167,43 +161,69 @@
         return carry
 
     lax.fori_loop(0, BS // 16, rows16, 0, unroll=2)
-    fetch.wait()
+    row = lax.broadcasted_iota(jnp.int32, (SLOTS, 8, BS), 1)
+    for j in range(NLON):
+        rows = edges[8 * j : 8 * j + 8, :].reshape(SLOTS, 1, BS)
+        rows = jnp.where(row == 7, jnp.broadcast_to(rows, (SLOTS, 8, BS)), 0.0)
+        out[j, TILE * 32 :, :] = rows.reshape(SLOTS * 8, BS).astype(BF16)
+
+
+def spread(forcing, edges):
+    return pl.pallas_call(
+        spread_kernel,
+        out_shape=jax.ShapeDtypeStruct((NLON, M1_ROWS, BS), BF16),
+        in_specs=[pl.BlockSpec(memory_space=pltpu.VMEM)] * 2,
+        out_specs=pl.BlockSpec(memory_space=pltpu.VMEM),
+        compiler_params=pltpu.CompilerParams(vmem_limit_bytes=16 * 2**20),
+        name="spread",
+    )(forcing, edges)
+
+
+def spread_strips_kernel(band, message, from_mate, from_other, out, hold):
+    odd = lax.rem(band[0], 2) == 1
+
+    def beside(is_north, row, rows, at, width):
+        from_chip, from_next = (
+            ref[row : row + rows, at : at + width] for ref in (from_mate, from_other)
+        )
+        use_chip = jnp.logical_not(odd) if is_north else odd
+        return jnp.where(jnp.broadcast_to(use_chip, from_chip.shape), from_chip, from_next)
+
     for j in range(NLON):
         hold[...] = jnp.zeros(hold.shape, F32)
-        source = north if j < 8 else south
         f = j % 8
         if f < ICE:
-            rows = source[3 * f : 3 * f + 3, :]
+            if f < MASS:
+                rows = beside(j < 8, 3 * f, 3, 0, SLOTS * BS)
+            else:
+                rows = beside(j < 8, MASS_AT, 2, 0, SLOTS * BS)
+                spare = jnp.zeros((1, SLOTS * BS), F32)
+                rows = jnp.concatenate([rows, spare] if j < 8 else [spare, rows], axis=0)
             high = rows.astype(BF16).astype(F32)
             low = rows - high
             for s in range(SLOTS):
                 hold[8 * s : 8 * s + 3, :] = high[:, s * BS : (s + 1) * BS]
                 hold[8 * s + 3 : 8 * s + 6, :] = low[:, s * BS : (s + 1) * BS]
         field, h = j // 4, j % 4
-        source = south if h < 2 else north
         for cb in range(TILE):
             at = (h % 2) * 512 + cb * BS
-            hold[8 * cb + 6 : 8 * cb + 7, :] = source[21 + field : 22 + field, at : at + BS]
-        for s in range(SLOTS):
-            hold[8 * s + 7 : 8 * s + 8, :] = edges[8 * j + s : 8 * j + s + 1, :]
-        out[j, TILE * 32 :, :] = hold[...].astype(BF16)
-
-
-def spread(forcing, north, south, edges):
+            hold[8 * cb + 6 : 8 * cb + 7, :] = beside(h >= 2, FORCE_AT + field, 1, at, BS)
+        edges = message[j, TILE * 32 :, :].astype(F32)
+        out[j, TILE * 32 :, :] = (hold[...] + edges).astype(BF16)
+
+
+def spread_strips(band, message, from_mate, from_other):
     return pl.pallas_call(
-        spread_kernel,
+        spread_strips_kernel,
         out_shape=jax.ShapeDtypeStruct((NLON, M1_ROWS, BS), BF16),
-        in_specs=[pl.BlockSpec(memory_space=pltpu.VMEM)] * 3
-        + [pl.BlockSpec(memory_space=pl.ANY)],
+        in_specs=[pl.BlockSpec(memory_space=pltpu.SMEM)]
+        + [pl.BlockSpec(memory_space=pltpu.VMEM)] * 3,
         out_specs=pl.BlockSpec(memory_space=pltpu.VMEM),
-        scratch_shapes=[
-            pltpu.VMEM((SLOTS * 8, BS), F32),
-            pltpu.VMEM((BS, BS), F32),
-            pltpu.SemaphoreType.DMA,
-        ],
-        compiler_params=pltpu.CompilerParams(vmem_limit_bytes=32 * 2**20),
-        name="spread",
-    )(forcing, north, south, edges)
+        scratch_shapes=[pltpu.VMEM((SLOTS * 8, BS), F32)],
+        input_output_aliases={1: 0},
+        compiler_params=pltpu.CompilerParams(vmem_limit_bytes=16 * 2**20),
+        name="spread_strips",
+    )(band, message, from_mate, from_other)
 
 
 def note_slots(table, k, count, start, odd):
@@ -337,6 +357,8 @@
 
     for g in (0, groups + 1):
         derived(fields_at[AREA][rows_at(g), :], fields_at[MASS][rows_at(g), :], g, slice(0, STRIP))
+    far = TOP - DEEP
+    fields_at[STR][far : far + 1, :] = fields_at[AREA][far : far + 1, :]
 
     def own_rows(j, carry):
         packed = got[j, M2_ROWS - 16 :, :].astype(F32)[8:16, :]
@@ -623,12 +645,14 @@
     rows = (band_idx * BS + jnp.arange(-TOP, BS + TOP, dtype=jnp.int32)).astype(F32)
     latitude = -78.0 + 168.0 * (rows + 0.5) / (BS * NLAT)
     coriolis = jnp.broadcast_to(jnp.sin(latitude * (jnp.pi / 180.0))[:, None], (ROWS, BS))
-    to_south, to_north = edge_rows(*ice, ocean_forcing)
-    north = lax.ppermute(to_south, "lat", [(b, b - 1) for b in range(1, NLAT)])
-    south = lax.ppermute(to_north, "lat", [(b, b + 1) for b in range(NLAT - 1)])
-    north, south, coriolis = lax.optimization_barrier((north, south, coriolis))
-    edges = edge_columns(lens, *place, *ice)
-    message = spread(ocean_forcing, north, south, edges)
+    to_mate, to_other, edges = make_edges(lens, *place, *ice, ocean_forcing)
+    message = spread(ocean_forcing, edges)
+    pairs = [(b, b ^ 1) for b in range(NLAT)]
+    from_mate = lax.ppermute(to_mate, "lat", pairs)
+    pairs = [(b, b + 1 if b % 2 else b - 1) for b in range(1, NLAT - 1)]
+    from_other = lax.ppermute(to_other, "lat", pairs)
+    from_mate, from_other, coriolis = lax.optimization_barrier((from_mate, from_other, coriolis))
+    message = spread_strips(place[0], message, from_mate, from_other)
     dealt = to_all(deal(lens, *place, to_all(message)))
     velocity_out, stress_out, handed = dynamics(lens, *place, *ice, dealt, coriolis)
     handed = to_all(handed).reshape(NLON * SLOTS, 16, BS)

time: 102 us -> 99 us (0.971)
  waiting for transfers between devices: 0.01 us -> 2.75 us
  blocking collectives: 73.8 us -> 71.6 us
  starting transfers between devices: 4.31 us -> 2.29 us
  Pallas kernels: 21.6 us -> 20.3 us
    ppermute x2, waiting for transfers between devices: 0.01 us -> 2.75 us  [the longest x1 2.75 us: body(): from_other = lax.ppermute(to_other, 'lat', pairs)]
    all_to_all x4, blocking collectives: 73.8 us -> 71.6 us  [to_all(): return lax.all_to_all(block, 'lon', 0, 0, tiled=True)]
    ppermute x2, starting transfers between devices: 4.31 us -> 2.29 us  [the longest x1 2.29 us: body(): from_other = lax.ppermute(to_other, 'lat', pairs)]
    pallas_call x2, Pallas kernels: 6.06 us -> 4.95 us  [the longest x1 4.73 us: make_edges(): pl.pallas_call(edges_kernel, grid_spec=pltpu.PrefetchScalarGridSpec(num_s...]
  transfers between devices with their start and end apart: 2 -> 2, of which waited for: 0 -> 1; matrix products, arithmetic and copies ran while one was open for 0% -> 0% of each run, Pallas kernels for 4% -> 0%
where the time goes in v5:
time: 99 us; the launch traced here: 98.7 us
  blocking collectives  71.6 us (72%)
  Pallas kernels  20.3 us (21%)
  waiting for transfers between devices  2.75 us (3%)
  starting transfers between devices  2.29 us (2%)
    all_to_all x4, blocking collectives, to_all(): return lax.all_to_all(block, 'lon', 0, 0, tiled=True)  71.6 us
    pallas_call x1, Pallas kernels, dynamics(): pl.pallas_call(dynamics_kernel, in_specs=[smem] * 3 + [vmem] * 6, out_spe...  10.4 us
    pallas_call x1, Pallas kernels, make_edges(): pl.pallas_call(edges_kernel, grid_spec=pltpu.PrefetchScalarGridSpec(num_s...  4.73 us
    pallas_call x1, Pallas kernels, deal(): pl.pallas_call(deal_kernel, out_shape=jax.ShapeDtypeStruct((NLON, M2_ROWS...  3.02 us
    ppermute x1, waiting for transfers between devices, body(): from_other = lax.ppermute(to_other, 'lat', pairs)  2.75 us
    ppermute x1, starting transfers between devices, body(): from_other = lax.ppermute(to_other, 'lat', pairs)  2.29 us
  transfers between devices with their start and end apart: 2, of which 1 were waited for; matrix products, arithmetic and copies ran while one was open for 0% of the time, Pallas kernels for 0%

profile of v5, /device:TPU:8, one launch (start us, length us, event | category | flops | bytes accessed | tf_op | source)
XLA Modules:
  0.0 98.7 jit_solution(3336820755112584836)
XLA Ops:
  0.6 0.0 copy-start.4
  0.6 4.7 %edges.1 = (f32[24,1024]{1,0:T(8,128)}, f32[24,1024]{1,0:T(8,128)}, f32[128,128]{1,0:T(8,128)}) custom-call(s32[8,16]{1,0:T(8,128)} %lens.7, s32[1]{0:T(128)} %bitcast.band, s32[1]{0:T(128)} %bitcast.1.lon, f32[2,128,1024]{2,1,0:T(8,128)} %vel.1, f32[2,128,1024]{2,1,0:T(8,128)} %vel.1, f32[2,128,1024]{2,1,0:T(8,128)} %vel.1, f32[2,128,1024]{2,1,0:T(8,128)} %vel.1, ...), custom_call_target="tpu_custom_call" | custom-call | tf_op jit(solution)/shard_map/edges/pallas_call | solution.py:134
  5.4 0.0 collective-permute-start
  5.4 2.3 %collective-permute-start.1 = (f32[24,1024]{1,0:T(8,128)}, f32[24,1024]{1,0:T(8,128)S(1)}, u32[]{:S(2)}, u32[]{:S(2)}) collective-permute-start(f32[24,1024]{1,0:T(8,128)} %get-tuple-element.14), channel_id=1, source_target_pairs={{16,32},{32,16},{48,64},{64,48},{80,96},{96,80},{17,33},{33,17},{4... | collective-permute-start | bytes 294920 | tf_op jit(solution)/shard_map/ppermute | solution.py:653
  7.7 0.0 copy-done.4
  7.7 0.0 copy-start.6
  7.7 0.8 copy-done.6
  8.5 0.2 spread.1.message
  8.7 0.1 multiply_sine_fusion
  8.8 0.0 collective-permute-done.from_mate
  8.8 2.7 %collective-permute-done.1.from_other = f32[24,1024]{1,0:T(8,128)S(1)} collective-permute-done((f32[24,1024]{1,0:T(8,128)}, f32[24,1024]{1,0:T(8,128)S(1)}, u32[]{:S(2)}, u32[]{:S(2)}) %collective-permute-start.1) | collective-permute-done | bytes 98336 | tf_op jit(solution)/shard_map/ppermute | solution.py:653
  11.5 0.1 broadcast_in_dim.2.coriolis
  11.6 0.0 copy-start.5
  11.6 0.0 copy-start.2
  11.6 0.2 spread_strips.1
  11.8 0.0 copy-start.1
  11.9 22.9 %all_to_all.20.got = bf16[16,192,128]{2,1,0:T(8,128)(2,1)S(1)} all-to-all(bf16[16,192,128]{2,1,0:T(8,128)(2,1)S(1)} %spread_strips.1), channel_id=1, replica_groups=mesh['lat'=8,'lon'=16] {'lon'}, dimensions={0} | all-to-all | bytes 1572864 | tf_op jit(solution)/shard_map/all_to_all | solution.py:636
  34.7 0.0 copy-done.5
  34.7 0.0 copy-start.3
  34.7 3.0 %deal.1 = bf16[16,336,128]{2,1,0:T(8,128)(2,1)S(1)} custom-call(s32[8,16]{1,0:T(8,128)S(1)} %copy-done.5, s32[1]{0:T(128)} %bitcast.band, s32[1]{0:T(128)} %bitcast.1.lon, bf16[16,192,128]{2,1,0:T(8,128)(2,1)S(1)} %all_to_all.20.got), custom_call_target="tpu_custom_call" | custom-call | tf_op jit(solution)/shard_map/deal/pallas_call | solution.py:299
  37.7 0.0 copy-start
  37.8 23.6 %all_to_all.21.got = bf16[16,336,128]{2,1,0:T(8,128)(2,1)S(1)} all-to-all(bf16[16,336,128]{2,1,0:T(8,128)(2,1)S(1)} %deal.1), channel_id=1, replica_groups=mesh['lat'=8,'lon'=16] {'lon'}, dimensions={0} | all-to-all | bytes 2752512 | tf_op jit(solution)/shard_map/all_to_all | solution.py:636
  61.4 0.0 copy-done.2
  61.4 0.0 copy-done.1
  61.4 0.0 copy-done.3
  61.4 0.0 copy-done
  61.4 10.4 %dynamics.1 = (f32[2,128,1024]{2,1,0:T(8,128)}, f32[3,128,1024]{2,1,0:T(8,128)}, bf16[16,128,128]{2,1,0:T(8,128)(2,1)S(1)}) custom-call(s32[8,16]{1,0:T(8,128)S(1)} %copy-done.5, s32[1]{0:T(128)} %bitcast.band, s32[1]{0:T(128)} %bitcast.1.lon, f32[2,128,1024]{2,1,0:T(8,128)S(1)} %copy-done.3, f32[3,128,1024]{2,1,0:T(8,128)S(1)} %copy-done.2, ...), custom_call_target="tpu_custom_call" | custom-call | tf_op jit(solution)/shard_map/dynamics/pallas_call | solution.py:562
  71.8 13.5 %all_to_all.22 = bf16[16,128,128]{2,1,0:T(8,128)(2,1)S(1)} all-to-all(bf16[16,128,128]{2,1,0:T(8,128)(2,1)S(1)} %get-tuple-element.20), channel_id=1, replica_groups=mesh['lat'=8,'lon'=16] {'lon'}, dimensions={0} | all-to-all | bytes 1048576 | tf_op jit(solution)/shard_map/all_to_all | solution.py:636
  85.3 1.0 %sort_back.1 = bf16[64,16,128]{2,1,0:T(8,128)(2,1)S(1)} custom-call(s32[8,16]{1,0:T(8,128)S(1)} %copy-done.5, s32[1]{0:T(128)} %bitcast.band, bf16[128,16,128]{2,1,0:T(8,128)(2,1)S(1)} %bitcast.4), custom_call_target="tpu_custom_call" | custom-call | tf_op jit(solution)/shard_map/sort_back/pallas_call | solution.py:598
  86.3 11.6 %all_to_all.23.got = bf16[16,64,128]{2,1,0:T(8,128)(2,1)S(1)} all-to-all(bf16[16,64,128]{2,1,0:T(8,128)(2,1)S(1)} %bitcast.5), channel_id=1, replica_groups=mesh['lat'=8,'lon'=16] {'lon'}, dimensions={0} | all-to-all | bytes 524288 | tf_op jit(solution)/shard_map/all_to_all | solution.py:636
  97.9 0.8 settle.1
Async XLA Ops:
  0.6 7.0 %copy-start.4 = (bf16[4,128,512]{2,1,0:T(8,128)(2,1)S(1)}, bf16[4,128,512]{2,1,0:T(8,128)(2,1)}, u32[]{:S(2)}) copy-start(bf16[4,128,512]{2,1,0:T(8,128)(2,1)} %forcing.1) | copy-start | bytes 1572868
  5.4 3.4 %collective-permute-start = (f32[24,1024]{1,0:T(8,128)}, f32[24,1024]{1,0:T(8,128)S(1)}, u32[]{:S(2)}, u32[]{:S(2)}) collective-permute-start(f32[24,1024]{1,0:T(8,128)} %get-tuple-element.13), channel_id=1, source_target_pairs={{0,16},{16,0},{32,48},{48,32},{64,80},{80,64},{96,112},{112,96},{1... | collective-permute-start | bytes 294920 | tf_op jit(solution)/shard_map/ppermute | solution.py:651
  5.4 6.1 %collective-permute-start.1 = (f32[24,1024]{1,0:T(8,128)}, f32[24,1024]{1,0:T(8,128)S(1)}, u32[]{:S(2)}, u32[]{:S(2)}) collective-permute-start(f32[24,1024]{1,0:T(8,128)} %get-tuple-element.14), channel_id=1, source_target_pairs={{16,32},{32,16},{48,64},{64,48},{80,96},{96,80},{17,33},{33,17},{4... | collective-permute-start | bytes 294920 | tf_op jit(solution)/shard_map/ppermute | solution.py:653
  7.7 0.8 copy-start.6
  11.6 23.1 %copy-start.5 = (s32[8,16]{1,0:T(8,128)S(1)}, s32[8,16]{1,0:T(8,128)}, u32[]{:S(2)}) copy-start(s32[8,16]{1,0:T(8,128)} %lens.7) | copy-start | bytes 1540
  11.6 49.7 %copy-start.2 = (f32[3,128,1024]{2,1,0:T(8,128)S(1)}, f32[3,128,1024]{2,1,0:T(8,128)}, u32[]{:S(2)}) copy-start(f32[3,128,1024]{2,1,0:T(8,128)} %stress.1) | copy-start | bytes 4718596
  11.8 49.5 %copy-start.1 = (f32[5,128,1024]{2,1,0:T(8,128)S(1)}, f32[5,128,1024]{2,1,0:T(8,128)}, u32[]{:S(2)}) copy-start(f32[5,128,1024]{2,1,0:T(8,128)} %thick.1) | copy-start | bytes 7864324
  34.7 26.6 %copy-start.3 = (f32[2,128,1024]{2,1,0:T(8,128)S(1)}, f32[2,128,1024]{2,1,0:T(8,128)}, u32[]{:S(2)}) copy-start(f32[2,128,1024]{2,1,0:T(8,128)} %vel.1) | copy-start | bytes 3145732
  37.7 23.6 %copy-start = (f32[5,128,1024]{2,1,0:T(8,128)S(1)}, f32[5,128,1024]{2,1,0:T(8,128)}, u32[]{:S(2)}) copy-start(f32[5,128,1024]{2,1,0:T(8,128)} %area.1) | copy-start | bytes 7864324

commit v6 on v5

--- a/solution.py
+++ b/solution.py
@@ -28,11 +28,10 @@
 STRIP = (SLOTS + 1) * BS
 UNROLL = 4
 UNROLL_OWN = 8
-UNROLL_STRESS = 9
+UNROLL_STRESS = 8
 UNROLL_VELOCITY = 8
 WIDE = 3 * BS
-TOP = 8
-ROWS = BS + 2 * TOP
+ROWS = BS + 8
 SEND_ROWS = 24
 MASS_AT, FORCE_AT = 18, 20
 M1_ROWS = TILE * 32 + SLOTS * 8
@@ -292,7 +291,7 @@
         out[k, SLOTS * 32 :, :] = jnp.concatenate(parts, axis=0).astype(BF16)
         return start + count
 
-    lax.fori_loop(0, NLON, owner, 0, unroll=4)
+    lax.fori_loop(0, NLON, owner, 0, unroll=NLON)
 
 
 def deal(lens, band, lon, got):
@@ -329,24 +328,33 @@
         return pl.ds(pl.multiple_of(jnp.where(odd, SLOTS - 1 - slot, slot) * BS, BS), BS)
 
     edge_lanes = pl.ds(SLOTS * BS, BS)
+
+    def strips_of(j):
+        group = got[j, SLOTS * 32 : SLOTS * 32 + 8 * (SLOTS + 1), :].astype(F32)
+        return group.reshape(SLOTS + 1, 8, BS)
+
     empty[...] = jnp.zeros(empty.shape, F32)
 
+    below4 = lax.broadcasted_iota(jnp.int32, (SLOTS + 1, 8, BS), 1) < 4
+    groups_of = []
     for j in range(NLON):
-        group = got[j, SLOTS * 32 : SLOTS * 32 + 8 * (SLOTS + 1), :].astype(F32)
-        group = group.reshape(SLOTS + 1, 8, BS)
-        whole = group + pltpu.roll(group, 5, 1)
-        if j >= 8:
-            whole = pltpu.roll(whole, 5, 1)
-        f = j % 8
-        g = groups + 1 if j < 8 else 0
-        force_row = (TOP - 2, TOP - 1, TOP + BS, TOP + BS + 1)[j % 4]
+        group = strips_of(j)
+        groups_of.append(group)
+        force_row = (BS + 6, BS + 7, BS, BS + 1)[j % 4]
         for e in range(SLOTS + 1):
             lanes = slot_lanes(e) if e < SLOTS else edge_lanes
             mine = jnp.broadcast_to(e < count, (8, BS))
-            if f < ICE:
-                fields_at[f][rows_at(g), lanes] = jnp.where(mine, whole[e], whole[SLOTS])
             rows = jnp.where(mine, group[e], group[SLOTS])
             fields_at[UO + j // 4][force_row : force_row + 1, lanes] = rows[6:7, :]
+    for f in range(ICE):
+        north, south = groups_of[f], groups_of[f + 8]
+        north = north + pltpu.roll(north, 5, 1)
+        south = pltpu.roll(south + pltpu.roll(south, 5, 1), 5, 1)
+        both = jnp.where(below4, north, south)
+        for e in range(SLOTS + 1):
+            lanes = slot_lanes(e) if e < SLOTS else edge_lanes
+            mine = jnp.broadcast_to(e < count, (8, BS))
+            fields_at[f][rows_at(groups), lanes] = jnp.where(mine, both[e], both[SLOTS])
 
     def derived(conc, mass, g, lanes):
         turn = coriolis[rows_at(g), :]
@@ -355,9 +363,8 @@
         fields_at[STR][rows_at(g), lanes] = strength_of(conc, mass)
         fields_at[TURN][rows_at(g), lanes] = turn * mass
 
-    for g in (0, groups + 1):
-        derived(fields_at[AREA][rows_at(g), :], fields_at[MASS][rows_at(g), :], g, slice(0, STRIP))
-    far = TOP - DEEP
+    derived(fields_at[AREA][rows_at(groups), :], fields_at[MASS][rows_at(groups), :], groups, slice(0, STRIP))
+    far = ROWS - DEEP
     fields_at[STR][far : far + 1, :] = fields_at[AREA][far : far + 1, :]
 
     def own_rows(j, carry):
@@ -397,10 +404,10 @@
                 force = got[j, e * 32 : (e + 1) * 32, :].astype(F32)
                 force = [jnp.where(mine, force[8 * f : 8 * f + 8], forced[f]) for f in range(4)]
             for f in range(4):
-                fields_at[UO + f][rows_at(j + 1), lanes] = force[f]
+                fields_at[UO + f][rows_at(j), lanes] = force[f]
             for f in range(ICE):
-                fields_at[f][rows_at(j + 1), lanes] = fields[f]
-            derived(fields[AREA], fields[MASS], j + 1, lanes)
+                fields_at[f][rows_at(j), lanes] = fields[f]
+            derived(fields[AREA], fields[MASS], j, lanes)
         return carry
 
     lax.fori_loop(0, groups, own_rows, 0, unroll=UNROLL_OWN)
@@ -412,10 +419,12 @@
         return fields_at[f][rows_at(g), c : c + width]
 
     def north_of(f, x, g, c):
-        return pltpu.roll(jnp.where(row == 0, load(f, g + 1, c), x), 7, 0)
+        above = 0 if isinstance(g, int) and g == groups else g + 1
+        return pltpu.roll(jnp.where(row == 0, load(f, above, c), x), 7, 0)
 
     def south_of(f, x, g, c):
-        return pltpu.roll(jnp.where(row == 7, load(f, max(g - 1, 0) if isinstance(g, int) else g - 1, c), x), 1, 0)
+        below = lax.rem(g + groups, groups + 1)
+        return pltpu.roll(jnp.where(row == 7, load(f, below, c), x), 1, 0)
 
     def east_of(f, x, g, c):
         if WIDE == STRIP:
@@ -471,9 +480,8 @@
             u = (d * ru + q * rv) * inv
             v = (d * rv - q * ru) * inv
             if beyond is not None:
-                mask = jnp.broadcast_to(beyond, cells)
-                u = jnp.where(mask, 0.0, u)
-                v = jnp.where(mask, 0.0, v)
+                u = jnp.where(beyond, 0.0, u)
+                v = jnp.where(beyond, 0.0, v)
             at = slice(c, c + WIDE)
             new[U][rows_at(g), at] = u
             new[V][rows_at(g), at] = v
@@ -488,7 +496,7 @@
                     if p < SLOTS:
                         slot = jnp.where(odd, SLOTS - 1 - p, p)
                         pair = [x[:, i * BS : (i + 1) * BS], y[:, i * BS : (i + 1) * BS]]
-                        handed[g - 1, pl.ds(pl.multiple_of(slot * 16, 16), 16), :] = (
+                        handed[g, pl.ds(pl.multiple_of(slot * 16, 16), 16), :] = (
                             jnp.concatenate(pair, axis=0).astype(BF16)
                         )
 
@@ -498,7 +506,7 @@
             for e in range(SLOTS):
                 to = out.at[n, pl.ds(row0, rows), pl.ds(e * BS, BS)]
                 sem = sems.at[sem0 + n * SLOTS + e]
-                block = fields_at[f].at[pl.ds(TOP + row0, rows), slot_lanes(e)]
+                block = fields_at[f].at[pl.ds(row0, rows), slot_lanes(e)]
                 made.append((e, pltpu.make_async_copy(block, to, sem),
                              pltpu.make_async_copy(empty.at[pl.ds(0, rows), :], to, sem)))
         return made
@@ -523,7 +531,8 @@
             stress_rows(g, new, last)
             return carry
 
-        lax.fori_loop(0, groups + (1 if last else 2), stress_step, 0, unroll=UNROLL_STRESS)
+        lax.fori_loop(0, groups, stress_step, 0, unroll=UNROLL_STRESS)
+        stress_rows(groups, new, last)
         for f in (SXX, SYY, S12):
             n = S2_OUT + 1 + RENEWED.index(f)
             fields_at[f], fields_at[n] = fields_at[n], fields_at[f]
@@ -532,8 +541,8 @@
             start(made)
             pending += made
         else:
-            velocity_rows(0, new, band == 0)
-            velocity_rows(groups + 1, new, band == NLAT - 1)
+            beyond = (row < 4) & (band == NLAT - 1) | (row >= 4) & (band == 0)
+            velocity_rows(groups, new, beyond)
 
         def velocity_step(g, carry):
             velocity_rows(g, new, None, last)
@@ -542,12 +551,12 @@
         if last:
             for h in range(2):
                 half = groups // 2
-                lax.fori_loop(1 + h * half, 1 + (h + 1) * half, velocity_step, 0, unroll=UNROLL_VELOCITY)
+                lax.fori_loop(h * half, (h + 1) * half, velocity_step, 0, unroll=UNROLL_VELOCITY)
                 made = copies((U_NEW, V_NEW), vel_out, h * BS // 2, BS // 2, 24 + 16 * h)
                 start(made)
                 pending += made
         else:
-            lax.fori_loop(1, groups + 1, velocity_step, 0, unroll=UNROLL_VELOCITY)
+            lax.fori_loop(0, groups, velocity_step, 0, unroll=UNROLL_VELOCITY)
             for f in (U, V):
                 n = S2_OUT + 1 + RENEWED.index(f)
                 fields_at[f], fields_at[n] = fields_at[n], fields_at[f]
@@ -564,7 +573,7 @@
         in_specs=[smem] * 3 + [vmem] * 6,
         out_specs=[pl.BlockSpec(memory_space=pl.ANY)] * 2 + [vmem],
         scratch_shapes=[
-            *[pltpu.VMEM((ROWS + 8, STRIP), F32) for _ in range(S2_OUT + 6)],
+            *[pltpu.VMEM((ROWS, STRIP), F32) for _ in range(S2_OUT + 6)],
             pltpu.VMEM((BS, BS), F32),
             pltpu.SemaphoreType.DMA((24 + 32,)),
         ],
@@ -585,13 +594,13 @@
         note_slots(table, k, lens[band[0], k], start, odd)
         return start + lens[band[0], k]
 
-    lax.fori_loop(0, NLON, owner, 0, unroll=UNROLL)
+    lax.fori_loop(0, NLON, owner, 0, unroll=NLON)
 
     def block(c, carry):
         out[c] = got[table[c]]
         return carry
 
-    lax.fori_loop(0, NBB, block, 0, unroll=8)
+    lax.fori_loop(0, NBB, block, 0, unroll=16)
 
 
 def sort_back(lens, band, got):
@@ -618,7 +627,7 @@
             out[1, rows, lanes] = jnp.concatenate([a[8:16], b[8:16]], axis=0).astype(BF16)
         return carry
 
-    lax.fori_loop(0, BS // 16, rows16, 0, unroll=UNROLL)
+    lax.fori_loop(0, BS // 16, rows16, 0, unroll=8)
 
 
 def settle(got):
@@ -642,7 +651,9 @@
     lens = run_lengths
     place = (jnp.reshape(band_idx, (1,)), jnp.reshape(lon_idx, (1,)))
     ice = (ice_velocity, ice_stress, cat_area, cat_thick)
-    rows = (band_idx * BS + jnp.arange(-TOP, BS + TOP, dtype=jnp.int32)).astype(F32)
+    place_of = jnp.arange(ROWS, dtype=jnp.int32)
+    place_of = jnp.where(place_of < BS + 4, place_of, place_of - ROWS)
+    rows = (band_idx * BS + place_of).astype(F32)
     latitude = -78.0 + 168.0 * (rows + 0.5) / (BS * NLAT)
     coriolis = jnp.broadcast_to(jnp.sin(latitude * (jnp.pi / 180.0))[:, None], (ROWS, BS))
     to_mate, to_other, edges = make_edges(lens, *place, *ice, ocean_forcing)

time: 99 us -> 98.2 us (level)
  no operation moved by 1% of the time
where the time goes in v6:
time: 98.2 us; the launch traced here: 97.8 us
  blocking collectives  71.6 us (73%)
  Pallas kernels  19.4 us (20%)
  waiting for transfers between devices  2.58 us (3%)
  starting transfers between devices  2.46 us (3%)
    all_to_all x4, blocking collectives, to_all(): return lax.all_to_all(block, 'lon', 0, 0, tiled=True)  71.6 us
    pallas_call x1, Pallas kernels, dynamics(): pl.pallas_call(dynamics_kernel, in_specs=[smem] * 3 + [vmem] * 6, out_spe...  9.89 us
    pallas_call x1, Pallas kernels, make_edges(): pl.pallas_call(edges_kernel, grid_spec=pltpu.PrefetchScalarGridSpec(num_s...  4.64 us
    pallas_call x1, Pallas kernels, deal(): pl.pallas_call(deal_kernel, out_shape=jax.ShapeDtypeStruct((NLON, M2_ROWS...  2.7 us
    ppermute x1, waiting for transfers between devices, body(): from_other = lax.ppermute(to_other, 'lat', pairs)  2.58 us
    ppermute x1, starting transfers between devices, body(): from_other = lax.ppermute(to_other, 'lat', pairs)  2.45 us
  transfers between devices with their start and end apart: 2, of which 1 were waited for; matrix products, arithmetic and copies ran while one was open for 0% of the time, Pallas kernels for 0%

profile of v6, /device:TPU:8, one launch (start us, length us, event | category | flops | bytes accessed | tf_op | source)
XLA Modules:
  0.0 97.8 jit_solution(14969275112169583317)
XLA Ops:
  0.6 0.0 copy-start.4
  0.6 4.6 %edges.1 = (f32[24,1024]{1,0:T(8,128)}, f32[24,1024]{1,0:T(8,128)}, f32[128,128]{1,0:T(8,128)}) custom-call(s32[8,16]{1,0:T(8,128)} %lens.7, s32[1]{0:T(128)} %bitcast.band, s32[1]{0:T(128)} %bitcast.1.lon, f32[2,128,1024]{2,1,0:T(8,128)} %vel.1, f32[2,128,1024]{2,1,0:T(8,128)} %vel.1, f32[2,128,1024]{2,1,0:T(8,128)} %vel.1, f32[2,128,1024]{2,1,0:T(8,128)} %vel.1, ...), custom_call_target="tpu_custom_call" | custom-call | tf_op jit(solution)/shard_map/edges/pallas_call | solution.py:133
  5.3 0.0 collective-permute-start
  5.3 2.5 %collective-permute-start.1 = (f32[24,1024]{1,0:T(8,128)}, f32[24,1024]{1,0:T(8,128)S(1)}, u32[]{:S(2)}, u32[]{:S(2)}) collective-permute-start(f32[24,1024]{1,0:T(8,128)} %get-tuple-element.14), channel_id=1, source_target_pairs={{16,32},{32,16},{48,64},{64,48},{80,96},{96,80},{17,33},{33,17},{4... | collective-permute-start | bytes 294920 | tf_op jit(solution)/shard_map/ppermute | solution.py:664
  7.8 0.0 copy-done.4
  7.8 0.0 copy-start.6
  7.8 0.8 copy-done.6
  8.6 0.2 spread.1.message
  8.8 0.1 fusion.6
  8.8 0.0 collective-permute-done.from_mate
  8.9 2.6 %collective-permute-done.1.from_other = f32[24,1024]{1,0:T(8,128)S(1)} collective-permute-done((f32[24,1024]{1,0:T(8,128)}, f32[24,1024]{1,0:T(8,128)S(1)}, u32[]{:S(2)}, u32[]{:S(2)}) %collective-permute-start.1) | collective-permute-done | bytes 98336 | tf_op jit(solution)/shard_map/ppermute | solution.py:664
  11.4 0.1 broadcast_in_dim.2.coriolis
  11.5 0.0 copy-start.5
  11.5 0.0 copy-start.2
  11.5 0.2 spread_strips.1
  11.8 0.0 copy-start.1
  11.8 22.9 %all_to_all.20.got = bf16[16,192,128]{2,1,0:T(8,128)(2,1)S(1)} all-to-all(bf16[16,192,128]{2,1,0:T(8,128)(2,1)S(1)} %spread_strips.1), channel_id=1, replica_groups=mesh['lat'=8,'lon'=16] {'lon'}, dimensions={0} | all-to-all | bytes 1572864 | tf_op jit(solution)/shard_map/all_to_all | solution.py:645
  34.7 0.0 copy-done.5
  34.7 0.0 copy-start.3
  34.7 2.7 %deal.1 = bf16[16,336,128]{2,1,0:T(8,128)(2,1)S(1)} custom-call(s32[8,16]{1,0:T(8,128)S(1)} %copy-done.5, s32[1]{0:T(128)} %bitcast.band, s32[1]{0:T(128)} %bitcast.1.lon, bf16[16,192,128]{2,1,0:T(8,128)(2,1)S(1)} %all_to_all.20.got), custom_call_target="tpu_custom_call" | custom-call | tf_op jit(solution)/shard_map/deal/pallas_call | solution.py:298
  37.4 0.0 copy-start
  37.4 23.6 %all_to_all.21.got = bf16[16,336,128]{2,1,0:T(8,128)(2,1)S(1)} all-to-all(bf16[16,336,128]{2,1,0:T(8,128)(2,1)S(1)} %deal.1), channel_id=1, replica_groups=mesh['lat'=8,'lon'=16] {'lon'}, dimensions={0} | all-to-all | bytes 2752512 | tf_op jit(solution)/shard_map/all_to_all | solution.py:645
  61.0 0.0 copy-done.2
  61.0 0.0 copy-done.1
  61.0 0.0 copy-done.3
  61.0 0.0 copy-done
  61.1 9.9 %dynamics.1 = (f32[2,128,1024]{2,1,0:T(8,128)}, f32[3,128,1024]{2,1,0:T(8,128)}, bf16[16,128,128]{2,1,0:T(8,128)(2,1)S(1)}) custom-call(s32[8,16]{1,0:T(8,128)S(1)} %copy-done.5, s32[1]{0:T(128)} %bitcast.band, s32[1]{0:T(128)} %bitcast.1.lon, f32[2,128,1024]{2,1,0:T(8,128)S(1)} %copy-done.3, f32[3,128,1024]{2,1,0:T(8,128)S(1)} %copy-done.2, ...), custom_call_target="tpu_custom_call" | custom-call | tf_op jit(solution)/shard_map/dynamics/pallas_call | solution.py:571
  71.0 13.5 %all_to_all.22 = bf16[16,128,128]{2,1,0:T(8,128)(2,1)S(1)} all-to-all(bf16[16,128,128]{2,1,0:T(8,128)(2,1)S(1)} %get-tuple-element.20), channel_id=1, replica_groups=mesh['lat'=8,'lon'=16] {'lon'}, dimensions={0} | all-to-all | bytes 1048576 | tf_op jit(solution)/shard_map/all_to_all | solution.py:645
  84.5 1.0 sort_back.1
  85.4 11.6 %all_to_all.23.got = bf16[16,64,128]{2,1,0:T(8,128)(2,1)S(1)} all-to-all(bf16[16,64,128]{2,1,0:T(8,128)(2,1)S(1)} %bitcast.5), channel_id=1, replica_groups=mesh['lat'=8,'lon'=16] {'lon'}, dimensions={0} | all-to-all | bytes 524288 | tf_op jit(solution)/shard_map/all_to_all | solution.py:645
  97.0 0.7 settle.1
Async XLA Ops:
  0.6 7.1 %copy-start.4 = (bf16[4,128,512]{2,1,0:T(8,128)(2,1)S(1)}, bf16[4,128,512]{2,1,0:T(8,128)(2,1)}, u32[]{:S(2)}) copy-start(bf16[4,128,512]{2,1,0:T(8,128)(2,1)} %forcing.1) | copy-start | bytes 1572868
  5.3 3.6 %collective-permute-start = (f32[24,1024]{1,0:T(8,128)}, f32[24,1024]{1,0:T(8,128)S(1)}, u32[]{:S(2)}, u32[]{:S(2)}) collective-permute-start(f32[24,1024]{1,0:T(8,128)} %get-tuple-element.13), channel_id=1, source_target_pairs={{0,16},{16,0},{32,48},{48,32},{64,80},{80,64},{96,112},{112,96},{1... | collective-permute-start | bytes 294920 | tf_op jit(solution)/shard_map/ppermute | solution.py:662
  5.3 6.1 %collective-permute-start.1 = (f32[24,1024]{1,0:T(8,128)}, f32[24,1024]{1,0:T(8,128)S(1)}, u32[]{:S(2)}, u32[]{:S(2)}) collective-permute-start(f32[24,1024]{1,0:T(8,128)} %get-tuple-element.14), channel_id=1, source_target_pairs={{16,32},{32,16},{48,64},{64,48},{80,96},{96,80},{17,33},{33,17},{4... | collective-permute-start | bytes 294920 | tf_op jit(solution)/shard_map/ppermute | solution.py:664
  7.8 0.8 copy-start.6
  11.5 23.2 %copy-start.5 = (s32[8,16]{1,0:T(8,128)S(1)}, s32[8,16]{1,0:T(8,128)}, u32[]{:S(2)}) copy-start(s32[8,16]{1,0:T(8,128)} %lens.7) | copy-start | bytes 1540
  11.5 49.5 %copy-start.2 = (f32[3,128,1024]{2,1,0:T(8,128)S(1)}, f32[3,128,1024]{2,1,0:T(8,128)}, u32[]{:S(2)}) copy-start(f32[3,128,1024]{2,1,0:T(8,128)} %stress.1) | copy-start | bytes 4718596
  11.8 49.3 %copy-start.1 = (f32[5,128,1024]{2,1,0:T(8,128)S(1)}, f32[5,128,1024]{2,1,0:T(8,128)}, u32[]{:S(2)}) copy-start(f32[5,128,1024]{2,1,0:T(8,128)} %thick.1) | copy-start | bytes 7864324
  34.7 26.3 %copy-start.3 = (f32[2,128,1024]{2,1,0:T(8,128)S(1)}, f32[2,128,1024]{2,1,0:T(8,128)}, u32[]{:S(2)}) copy-start(f32[2,128,1024]{2,1,0:T(8,128)} %vel.1) | copy-start | bytes 3145732
  37.4 23.6 %copy-start = (f32[5,128,1024]{2,1,0:T(8,128)S(1)}, f32[5,128,1024]{2,1,0:T(8,128)}, u32[]{:S(2)}) copy-start(f32[5,128,1024]{2,1,0:T(8,128)} %area.1) | copy-start | bytes 7864324

commit v7 on v6

--- a/solution.py
+++ b/solution.py
@@ -28,7 +28,7 @@
 STRIP = (SLOTS + 1) * BS
 UNROLL = 4
 UNROLL_OWN = 8
-UNROLL_STRESS = 8
+UNROLL_STRESS = 16
 UNROLL_VELOCITY = 8
 WIDE = 3 * BS
 ROWS = BS + 8

time: 98.2 us -> 97.4 us (level)
  no operation moved by 1% of the time
where the time goes in v7:
time: 97.4 us; the launch traced here: 97 us
  blocking collectives  71.6 us (74%)
  Pallas kernels  18.6 us (19%)
  waiting for transfers between devices  2.67 us (3%)
  starting transfers between devices  2.37 us (2%)
    all_to_all x4, blocking collectives, to_all(): return lax.all_to_all(block, 'lon', 0, 0, tiled=True)  71.6 us
    pallas_call x1, Pallas kernels, dynamics(): pl.pallas_call(dynamics_kernel, in_specs=[smem] * 3 + [vmem] * 6, out_spe...  9.12 us
    pallas_call x1, Pallas kernels, make_edges(): pl.pallas_call(edges_kernel, grid_spec=pltpu.PrefetchScalarGridSpec(num_s...  4.64 us
    pallas_call x1, Pallas kernels, deal(): pl.pallas_call(deal_kernel, out_shape=jax.ShapeDtypeStruct((NLON, M2_ROWS...  2.7 us
    ppermute x1, waiting for transfers between devices, body(): from_other = lax.ppermute(to_other, 'lat', pairs)  2.66 us
    ppermute x1, starting transfers between devices, body(): from_other = lax.ppermute(to_other, 'lat', pairs)  2.37 us
  transfers between devices with their start and end apart: 2, of which 1 were waited for; matrix products, arithmetic and copies ran while one was open for 0% of the time, Pallas kernels for 0%

profile of v7, /device:TPU:8, one launch (start us, length us, event | category | flops | bytes accessed | tf_op | source)
XLA Modules:
  0.0 97.0 jit_solution(7097845178369685270)
XLA Ops:
  0.6 0.0 copy-start.4
  0.6 4.6 %edges.1 = (f32[24,1024]{1,0:T(8,128)}, f32[24,1024]{1,0:T(8,128)}, f32[128,128]{1,0:T(8,128)}) custom-call(s32[8,16]{1,0:T(8,128)} %lens.7, s32[1]{0:T(128)} %bitcast.band, s32[1]{0:T(128)} %bitcast.1.lon, f32[2,128,1024]{2,1,0:T(8,128)} %vel.1, f32[2,128,1024]{2,1,0:T(8,128)} %vel.1, f32[2,128,1024]{2,1,0:T(8,128)} %vel.1, f32[2,128,1024]{2,1,0:T(8,128)} %vel.1, ...), custom_call_target="tpu_custom_call" | custom-call | tf_op jit(solution)/shard_map/edges/pallas_call | solution.py:133
  5.3 0.0 collective-permute-start
  5.3 2.4 %collective-permute-start.1 = (f32[24,1024]{1,0:T(8,128)}, f32[24,1024]{1,0:T(8,128)S(1)}, u32[]{:S(2)}, u32[]{:S(2)}) collective-permute-start(f32[24,1024]{1,0:T(8,128)} %get-tuple-element.14), channel_id=1, source_target_pairs={{16,32},{32,16},{48,64},{64,48},{80,96},{96,80},{17,33},{33,17},{4... | collective-permute-start | bytes 294920 | tf_op jit(solution)/shard_map/ppermute | solution.py:664
  7.7 0.0 copy-done.4
  7.7 0.0 copy-start.6
  7.7 0.8 copy-done.6
  8.5 0.2 spread.1.message
  8.7 0.1 fusion.6
  8.8 0.0 collective-permute-done.from_mate
  8.8 2.7 %collective-permute-done.1.from_other = f32[24,1024]{1,0:T(8,128)S(1)} collective-permute-done((f32[24,1024]{1,0:T(8,128)}, f32[24,1024]{1,0:T(8,128)S(1)}, u32[]{:S(2)}, u32[]{:S(2)}) %collective-permute-start.1) | collective-permute-done | bytes 98336 | tf_op jit(solution)/shard_map/ppermute | solution.py:664
  11.4 0.1 broadcast_in_dim.2.coriolis
  11.5 0.0 copy-start.5
  11.5 0.0 copy-start.2
  11.5 0.2 spread_strips.1
  11.8 0.0 copy-start.1
  11.8 22.9 %all_to_all.20.got = bf16[16,192,128]{2,1,0:T(8,128)(2,1)S(1)} all-to-all(bf16[16,192,128]{2,1,0:T(8,128)(2,1)S(1)} %spread_strips.1), channel_id=1, replica_groups=mesh['lat'=8,'lon'=16] {'lon'}, dimensions={0} | all-to-all | bytes 1572864 | tf_op jit(solution)/shard_map/all_to_all | solution.py:645
  34.7 0.0 copy-done.5
  34.7 0.0 copy-start.3
  34.7 2.7 %deal.1 = bf16[16,336,128]{2,1,0:T(8,128)(2,1)S(1)} custom-call(s32[8,16]{1,0:T(8,128)S(1)} %copy-done.5, s32[1]{0:T(128)} %bitcast.band, s32[1]{0:T(128)} %bitcast.1.lon, bf16[16,192,128]{2,1,0:T(8,128)(2,1)S(1)} %all_to_all.20.got), custom_call_target="tpu_custom_call" | custom-call | tf_op jit(solution)/shard_map/deal/pallas_call | solution.py:298
  37.4 0.0 copy-start
  37.4 23.6 %all_to_all.21.got = bf16[16,336,128]{2,1,0:T(8,128)(2,1)S(1)} all-to-all(bf16[16,336,128]{2,1,0:T(8,128)(2,1)S(1)} %deal.1), channel_id=1, replica_groups=mesh['lat'=8,'lon'=16] {'lon'}, dimensions={0} | all-to-all | bytes 2752512 | tf_op jit(solution)/shard_map/all_to_all | solution.py:645
  61.0 0.0 copy-done.2
  61.0 0.0 copy-done.1
  61.0 0.0 copy-done.3
  61.0 0.0 copy-done
  61.1 9.1 %dynamics.1 = (f32[2,128,1024]{2,1,0:T(8,128)}, f32[3,128,1024]{2,1,0:T(8,128)}, bf16[16,128,128]{2,1,0:T(8,128)(2,1)S(1)}) custom-call(s32[8,16]{1,0:T(8,128)S(1)} %copy-done.5, s32[1]{0:T(128)} %bitcast.band, s32[1]{0:T(128)} %bitcast.1.lon, f32[2,128,1024]{2,1,0:T(8,128)S(1)} %copy-done.3, f32[3,128,1024]{2,1,0:T(8,128)S(1)} %copy-done.2, ...), custom_call_target="tpu_custom_call" | custom-call | tf_op jit(solution)/shard_map/dynamics/pallas_call | solution.py:571
  70.2 13.5 %all_to_all.22 = bf16[16,128,128]{2,1,0:T(8,128)(2,1)S(1)} all-to-all(bf16[16,128,128]{2,1,0:T(8,128)(2,1)S(1)} %get-tuple-element.20), channel_id=1, replica_groups=mesh['lat'=8,'lon'=16] {'lon'}, dimensions={0} | all-to-all | bytes 1048576 | tf_op jit(solution)/shard_map/all_to_all | solution.py:645
  83.7 1.0 sort_back.1
  84.7 11.6 %all_to_all.23.got = bf16[16,64,128]{2,1,0:T(8,128)(2,1)S(1)} all-to-all(bf16[16,64,128]{2,1,0:T(8,128)(2,1)S(1)} %bitcast.5), channel_id=1, replica_groups=mesh['lat'=8,'lon'=16] {'lon'}, dimensions={0} | all-to-all | bytes 524288 | tf_op jit(solution)/shard_map/all_to_all | solution.py:645
  96.3 0.7 settle.1
Async XLA Ops:
  0.6 7.0 %copy-start.4 = (bf16[4,128,512]{2,1,0:T(8,128)(2,1)S(1)}, bf16[4,128,512]{2,1,0:T(8,128)(2,1)}, u32[]{:S(2)}) copy-start(bf16[4,128,512]{2,1,0:T(8,128)(2,1)} %forcing.1) | copy-start | bytes 1572868
  5.3 3.5 %collective-permute-start = (f32[24,1024]{1,0:T(8,128)}, f32[24,1024]{1,0:T(8,128)S(1)}, u32[]{:S(2)}, u32[]{:S(2)}) collective-permute-start(f32[24,1024]{1,0:T(8,128)} %get-tuple-element.13), channel_id=1, source_target_pairs={{0,16},{16,0},{32,48},{48,32},{64,80},{80,64},{96,112},{112,96},{1... | collective-permute-start | bytes 294920 | tf_op jit(solution)/shard_map/ppermute | solution.py:662
  5.3 6.1 %collective-permute-start.1 = (f32[24,1024]{1,0:T(8,128)}, f32[24,1024]{1,0:T(8,128)S(1)}, u32[]{:S(2)}, u32[]{:S(2)}) collective-permute-start(f32[24,1024]{1,0:T(8,128)} %get-tuple-element.14), channel_id=1, source_target_pairs={{16,32},{32,16},{48,64},{64,48},{80,96},{96,80},{17,33},{33,17},{4... | collective-permute-start | bytes 294920 | tf_op jit(solution)/shard_map/ppermute | solution.py:664
  7.7 0.8 copy-start.6
  11.5 23.2 %copy-start.5 = (s32[8,16]{1,0:T(8,128)S(1)}, s32[8,16]{1,0:T(8,128)}, u32[]{:S(2)}) copy-start(s32[8,16]{1,0:T(8,128)} %lens.7) | copy-start | bytes 1540
  11.5 49.5 %copy-start.2 = (f32[3,128,1024]{2,1,0:T(8,128)S(1)}, f32[3,128,1024]{2,1,0:T(8,128)}, u32[]{:S(2)}) copy-start(f32[3,128,1024]{2,1,0:T(8,128)} %stress.1) | copy-start | bytes 4718596
  11.8 49.3 %copy-start.1 = (f32[5,128,1024]{2,1,0:T(8,128)S(1)}, f32[5,128,1024]{2,1,0:T(8,128)}, u32[]{:S(2)}) copy-start(f32[5,128,1024]{2,1,0:T(8,128)} %thick.1) | copy-start | bytes 7864324
  34.7 26.3 %copy-start.3 = (f32[2,128,1024]{2,1,0:T(8,128)S(1)}, f32[2,128,1024]{2,1,0:T(8,128)}, u32[]{:S(2)}) copy-start(f32[2,128,1024]{2,1,0:T(8,128)} %vel.1) | copy-start | bytes 3145732
  37.4 23.6 %copy-start = (f32[5,128,1024]{2,1,0:T(8,128)S(1)}, f32[5,128,1024]{2,1,0:T(8,128)}, u32[]{:S(2)}) copy-start(f32[5,128,1024]{2,1,0:T(8,128)} %area.1) | copy-start | bytes 7864324

commit v8 on v7

--- a/solution.py
+++ b/solution.py
@@ -245,7 +245,7 @@
         note_slots(table, l, lens[other, l], start, other_odd)
         return start + lens[other, l]
 
-    lax.fori_loop(0, NLON, fill, 0, unroll=UNROLL)
+    lax.fori_loop(0, NLON, fill, 0, unroll=NLON)
     row6 = lax.broadcasted_iota(jnp.int32, (8, BS), 0) == 6
 
     def halo(c, carry):
@@ -253,7 +253,7 @@
         halos[c] = jnp.where(row6, groups[own], groups[table[c]])
         return carry
 
-    lax.fori_loop(0, NBB, halo, 0, unroll=8)
+    lax.fori_loop(0, NBB, halo, 0, unroll=32)
     lane = lanes_of((8, BS))
 
     def column_at(p):
@@ -600,7 +600,7 @@
         out[c] = got[table[c]]
         return carry
 
-    lax.fori_loop(0, NBB, block, 0, unroll=16)
+    lax.fori_loop(0, NBB, block, 0, unroll=NBB)
 
 
 def sort_back(lens, band, got):

time: 97.4 us -> 97.3 us (level)
  no operation moved by 1% of the time
where the time goes in v8:
time: 97.3 us; the launch traced here: 96.9 us
  blocking collectives  71.6 us (74%)
  Pallas kernels  18.6 us (19%)
  waiting for transfers between devices  2.75 us (3%)
  starting transfers between devices  2.29 us (2%)
    all_to_all x4, blocking collectives, to_all(): return lax.all_to_all(block, 'lon', 0, 0, tiled=True)  71.6 us
    pallas_call x1, Pallas kernels, dynamics(): pl.pallas_call(dynamics_kernel, in_specs=[smem] * 3 + [vmem] * 6, out_spe...  9.13 us
    pallas_call x1, Pallas kernels, make_edges(): pl.pallas_call(edges_kernel, grid_spec=pltpu.PrefetchScalarGridSpec(num_s...  4.73 us
    ppermute x1, waiting for transfers between devices, body(): from_other = lax.ppermute(to_other, 'lat', pairs)  2.75 us
    pallas_call x1, Pallas kernels, deal(): pl.pallas_call(deal_kernel, out_shape=jax.ShapeDtypeStruct((NLON, M2_ROWS...  2.62 us
    ppermute x1, starting transfers between devices, body(): from_other = lax.ppermute(to_other, 'lat', pairs)  2.29 us
  transfers between devices with their start and end apart: 2, of which 1 were waited for; matrix products, arithmetic and copies ran while one was open for 0% of the time, Pallas kernels for 0%

profile of v8, /device:TPU:8, one launch (start us, length us, event | category | flops | bytes accessed | tf_op | source)
XLA Modules:
  0.0 96.9 jit_solution(13109478970310279913)
XLA Ops:
  0.6 0.0 copy-start.4
  0.6 4.7 %edges.1 = (f32[24,1024]{1,0:T(8,128)}, f32[24,1024]{1,0:T(8,128)}, f32[128,128]{1,0:T(8,128)}) custom-call(s32[8,16]{1,0:T(8,128)} %lens.7, s32[1]{0:T(128)} %bitcast.band, s32[1]{0:T(128)} %bitcast.1.lon, f32[2,128,1024]{2,1,0:T(8,128)} %vel.1, f32[2,128,1024]{2,1,0:T(8,128)} %vel.1, f32[2,128,1024]{2,1,0:T(8,128)} %vel.1, f32[2,128,1024]{2,1,0:T(8,128)} %vel.1, ...), custom_call_target="tpu_custom_call" | custom-call | tf_op jit(solution)/shard_map/edges/pallas_call | solution.py:133
  5.4 0.0 collective-permute-start
  5.4 2.3 %collective-permute-start.1 = (f32[24,1024]{1,0:T(8,128)}, f32[24,1024]{1,0:T(8,128)S(1)}, u32[]{:S(2)}, u32[]{:S(2)}) collective-permute-start(f32[24,1024]{1,0:T(8,128)} %get-tuple-element.14), channel_id=1, source_target_pairs={{16,32},{32,16},{48,64},{64,48},{80,96},{96,80},{17,33},{33,17},{4... | collective-permute-start | bytes 294920 | tf_op jit(solution)/shard_map/ppermute | solution.py:664
  7.7 0.0 copy-done.4
  7.7 0.0 copy-start.6
  7.7 0.8 copy-done.6
  8.5 0.2 spread.1.message
  8.7 0.1 fusion.6
  8.8 0.0 collective-permute-done.from_mate
  8.8 2.7 %collective-permute-done.1.from_other = f32[24,1024]{1,0:T(8,128)S(1)} collective-permute-done((f32[24,1024]{1,0:T(8,128)}, f32[24,1024]{1,0:T(8,128)S(1)}, u32[]{:S(2)}, u32[]{:S(2)}) %collective-permute-start.1) | collective-permute-done | bytes 98336 | tf_op jit(solution)/shard_map/ppermute | solution.py:664
  11.5 0.1 broadcast_in_dim.2.coriolis
  11.6 0.0 copy-start.5
  11.6 0.0 copy-start.2
  11.6 0.2 spread_strips.1
  11.8 0.0 copy-start.1
  11.9 22.9 %all_to_all.20.got = bf16[16,192,128]{2,1,0:T(8,128)(2,1)S(1)} all-to-all(bf16[16,192,128]{2,1,0:T(8,128)(2,1)S(1)} %spread_strips.1), channel_id=1, replica_groups=mesh['lat'=8,'lon'=16] {'lon'}, dimensions={0} | all-to-all | bytes 1572864 | tf_op jit(solution)/shard_map/all_to_all | solution.py:645
  34.7 0.0 copy-done.5
  34.7 0.0 copy-start.3
  34.7 2.6 %deal.1 = bf16[16,336,128]{2,1,0:T(8,128)(2,1)S(1)} custom-call(s32[8,16]{1,0:T(8,128)S(1)} %copy-done.5, s32[1]{0:T(128)} %bitcast.band, s32[1]{0:T(128)} %bitcast.1.lon, bf16[16,192,128]{2,1,0:T(8,128)(2,1)S(1)} %all_to_all.20.got), custom_call_target="tpu_custom_call" | custom-call | tf_op jit(solution)/shard_map/deal/pallas_call | solution.py:298
  37.3 0.0 copy-start
  37.4 23.6 %all_to_all.21.got = bf16[16,336,128]{2,1,0:T(8,128)(2,1)S(1)} all-to-all(bf16[16,336,128]{2,1,0:T(8,128)(2,1)S(1)} %deal.1), channel_id=1, replica_groups=mesh['lat'=8,'lon'=16] {'lon'}, dimensions={0} | all-to-all | bytes 2752512 | tf_op jit(solution)/shard_map/all_to_all | solution.py:645
  61.0 0.0 copy-done.2
  61.0 0.0 copy-done.1
  61.0 0.0 copy-done.3
  61.0 0.0 copy-done
  61.0 9.1 %dynamics.1 = (f32[2,128,1024]{2,1,0:T(8,128)}, f32[3,128,1024]{2,1,0:T(8,128)}, bf16[16,128,128]{2,1,0:T(8,128)(2,1)S(1)}) custom-call(s32[8,16]{1,0:T(8,128)S(1)} %copy-done.5, s32[1]{0:T(128)} %bitcast.band, s32[1]{0:T(128)} %bitcast.1.lon, f32[2,128,1024]{2,1,0:T(8,128)S(1)} %copy-done.3, f32[3,128,1024]{2,1,0:T(8,128)S(1)} %copy-done.2, ...), custom_call_target="tpu_custom_call" | custom-call | tf_op jit(solution)/shard_map/dynamics/pallas_call | solution.py:571
  70.1 13.5 %all_to_all.22 = bf16[16,128,128]{2,1,0:T(8,128)(2,1)S(1)} all-to-all(bf16[16,128,128]{2,1,0:T(8,128)(2,1)S(1)} %get-tuple-element.20), channel_id=1, replica_groups=mesh['lat'=8,'lon'=16] {'lon'}, dimensions={0} | all-to-all | bytes 1048576 | tf_op jit(solution)/shard_map/all_to_all | solution.py:645
  83.6 0.9 sort_back.1
  84.6 11.6 %all_to_all.23.got = bf16[16,64,128]{2,1,0:T(8,128)(2,1)S(1)} all-to-all(bf16[16,64,128]{2,1,0:T(8,128)(2,1)S(1)} %bitcast.5), channel_id=1, replica_groups=mesh['lat'=8,'lon'=16] {'lon'}, dimensions={0} | all-to-all | bytes 524288 | tf_op jit(solution)/shard_map/all_to_all | solution.py:645
  96.2 0.7 settle.1
Async XLA Ops:
  0.6 7.0 %copy-start.4 = (bf16[4,128,512]{2,1,0:T(8,128)(2,1)S(1)}, bf16[4,128,512]{2,1,0:T(8,128)(2,1)}, u32[]{:S(2)}) copy-start(bf16[4,128,512]{2,1,0:T(8,128)(2,1)} %forcing.1) | copy-start | bytes 1572868
  5.4 3.4 %collective-permute-start = (f32[24,1024]{1,0:T(8,128)}, f32[24,1024]{1,0:T(8,128)S(1)}, u32[]{:S(2)}, u32[]{:S(2)}) collective-permute-start(f32[24,1024]{1,0:T(8,128)} %get-tuple-element.13), channel_id=1, source_target_pairs={{0,16},{16,0},{32,48},{48,32},{64,80},{80,64},{96,112},{112,96},{1... | collective-permute-start | bytes 294920 | tf_op jit(solution)/shard_map/ppermute | solution.py:662
  5.4 6.1 %collective-permute-start.1 = (f32[24,1024]{1,0:T(8,128)}, f32[24,1024]{1,0:T(8,128)S(1)}, u32[]{:S(2)}, u32[]{:S(2)}) collective-permute-start(f32[24,1024]{1,0:T(8,128)} %get-tuple-element.14), channel_id=1, source_target_pairs={{16,32},{32,16},{48,64},{64,48},{80,96},{96,80},{17,33},{33,17},{4... | collective-permute-start | bytes 294920 | tf_op jit(solution)/shard_map/ppermute | solution.py:664
  7.7 0.8 copy-start.6
  11.6 23.1 %copy-start.5 = (s32[8,16]{1,0:T(8,128)S(1)}, s32[8,16]{1,0:T(8,128)}, u32[]{:S(2)}) copy-start(s32[8,16]{1,0:T(8,128)} %lens.7) | copy-start | bytes 1540
  11.6 49.4 %copy-start.2 = (f32[3,128,1024]{2,1,0:T(8,128)S(1)}, f32[3,128,1024]{2,1,0:T(8,128)}, u32[]{:S(2)}) copy-start(f32[3,128,1024]{2,1,0:T(8,128)} %stress.1) | copy-start | bytes 4718596
  11.8 49.1 %copy-start.1 = (f32[5,128,1024]{2,1,0:T(8,128)S(1)}, f32[5,128,1024]{2,1,0:T(8,128)}, u32[]{:S(2)}) copy-start(f32[5,128,1024]{2,1,0:T(8,128)} %thick.1) | copy-start | bytes 7864324
  34.7 26.2 %copy-start.3 = (f32[2,128,1024]{2,1,0:T(8,128)S(1)}, f32[2,128,1024]{2,1,0:T(8,128)}, u32[]{:S(2)}) copy-start(f32[2,128,1024]{2,1,0:T(8,128)} %vel.1) | copy-start | bytes 3145732
  37.3 23.6 %copy-start = (f32[5,128,1024]{2,1,0:T(8,128)S(1)}, f32[5,128,1024]{2,1,0:T(8,128)}, u32[]{:S(2)}) copy-start(f32[5,128,1024]{2,1,0:T(8,128)} %area.1) | copy-start | bytes 7864324
